TPU v7x, 32 devices: a whole 2x2x4 slice. The times are simulated.
32 devices in a mesh: batch: 8 (over z, x), seq: 4 (over y, core).
Axes of the slice: x: 2, y: 2, z: 4, core: 2. Of those that a mesh axis runs over, the one named last changes fastest.
Arguments:
- tokens: bfloat16 [32, 1024, 768], P('batch', 'seq'), may hold values from -6 to 6
- cotangent: bfloat16 [32, 1024, 768], P('batch', 'seq'), may hold values from -6 to 6
- lengths: int32 [32], replicated, may hold values from 256 to 1024, as said below
- order: int32 [32], P('batch'), may hold values from 0 to 31, as said below
- expert_route: int32 [32, 1024], P('batch', 'seq'), may hold values from 0 to 7, as said below
- slot_index: int32 [32, 1024], P('batch', 'seq'), may hold values from -1 to 39, as said below
- norm_gain: bfloat16 [768], P(('batch', 'seq')), may hold values from 0.5 to 1.5
- in_proj: bfloat16 [768, 3072], P(('batch', 'seq')), may hold values from -0.21875 to 0.21875
- conv_weight: bfloat16 [1536, 4], P(('batch', 'seq')), may hold values from -3 to 3
- conv_bias: bfloat16 [1536], P(('batch', 'seq')), may hold values from -1.5 to 1.5
- x_proj: bfloat16 [1536, 80], P(('batch', 'seq')), may hold values from -0.15625 to 0.15625
- dt_proj: bfloat16 [1536, 48], P(('batch', 'seq')), may hold values from -0.875 to 0.875
- dt_bias: bfloat16 [1536], P(('batch', 'seq')), may hold values from -7 to -3
- a_log: bfloat16 [1536, 16], P(('batch', 'seq')), may hold values from -1 to 2.796875
- skip_gain: bfloat16 [1536], P(('batch', 'seq')), may hold values from 0.5 to 1.5
- out_proj: bfloat16 [1536, 768], P(('batch', 'seq')), may hold values from -0.15625 to 0.15625
- moe_gain: bfloat16 [768], P(('batch', 'seq')), may hold values from 0.5 to 1.5
- router: bfloat16 [768, 8], P(('batch', 'seq')), may hold values from -0.15625 to 0.15625
- expert_in: bfloat16 [8, 768, 3072], P('batch', None, 'seq'), may hold values from -0.21875 to 0.21875
- expert_out: bfloat16 [8, 3072, 768], P('batch', 'seq'), may hold values from -0.875 to 0.875
Outputs:
- activations: bfloat16 [32, 1024, 768], P('batch', 'seq')
- input_grad: float32 [32, 1024, 768], P('batch', 'seq')
- norm_gain_grad: float32 [768], P(('batch', 'seq'))
- in_proj_grad: float32 [768, 3072], P(('batch', 'seq'))
- conv_weight_grad: float32 [1536, 4], P(('batch', 'seq'))
- conv_bias_grad: float32 [1536], P(('batch', 'seq'))
- x_proj_grad: float32 [1536, 80], P(('batch', 'seq'))
- dt_proj_grad: float32 [1536, 48], P(('batch', 'seq'))
- dt_bias_grad: float32 [1536], P(('batch', 'seq'))
- a_log_grad: float32 [1536, 16], P(('batch', 'seq'))
- skip_gain_grad: float32 [1536], P(('batch', 'seq'))
- out_proj_grad: float32 [1536, 768], P(('batch', 'seq'))
- moe_gain_grad: float32 [768], P(('batch', 'seq'))
- router_grad: float32 [768, 8], P(('batch', 'seq'))
- expert_in_grad: float32 [8, 768, 3072], P('batch', None, 'seq')
- expert_out_grad: float32 [8, 3072, 768], P('batch', 'seq')
Inputs may be any that keep to these rules, and one draw needn't show every extreme that they name: `lengths`: positions from a sequence's length on are padding. Some sequence has exactly 1024 tokens and some exactly 256. `order`: A permutation of the sequences: taken by decreasing length (ties by number), they are dealt to the batch indices in turns, forward in even turns and backward in odd ones, the j-th turn filling the j-th row of each batch index. `expert_route`: A block is the 1 sequence of one micro-batch (the m-th run of 1 among the 4 rows of a batch index) at the 256 positions of one index of seq. In every block one expert, the same in all blocks of a draw, is chosen by more than 40 tokens. `slot_index`: A token's slot is its rank, counting tokens of its block in order of row then position, among the block's tokens with the same expert; -1 where that rank is 40 or more.
All inputs are finite; a program needn't handle non-finite values.
Results may differ from a plain program's by a relative error of at most 0.015.
Values may be sent and summed in bfloat16 or wider, within the bound.
No kernel may reach another device: no remote copies, remote signals or barrier semaphores. Data moves between devices by JAX's collectives and lax.ppermute only.
A program may use at most 896 MiB of HBM per device.

v0:
```python
import math

import jax
import jax.numpy as jnp
from jax import lax
from jax.sharding import PartitionSpec as P

DI = 1536
STATE = 16
DT_RANK = 48
CONV = 4
SEQ_MB = 1


EPSILON = 1e-05


def shifted(block, axis, distance):
    devices = range(lax.axis_size(axis))
    route = [(i - distance, i) for i in devices if i - distance in devices]
    return lax.ppermute(block, axis, route)


def entering(x, axis, join, neutral, backward):
    count = lax.axis_size(axis)
    place = lax.axis_index(axis)
    ahead = count - 1 - place if backward else place
    gathered = jax.tree.map(
        lambda a, kind: lax.all_gather(a.astype(kind), axis), x, (jnp.bfloat16, jnp.bfloat16)
    )
    state = jax.tree.map(lambda a, e: jnp.zeros_like(a) + jnp.asarray(e, a.dtype), x, neutral)

    def one(lap, state):
        source = count - 1 - lap if backward else lap
        return join(
            state,
            jax.tree.map(
                lambda a, own: lax.dynamic_index_in_dim(a, source, 0, False).astype(own.dtype),
                gathered,
                x,
            ),
        )

    return lax.fori_loop(0, ahead, one, state)


def rows_product(left, right):
    return lax.dot_general(
        left, right, (((0,), (0,)), ((), ())), preferred_element_type=jnp.float32
    )


def cols_product(left, right):
    return lax.dot_general(
        left, right, (((1,), (1,)), ((), ())), preferred_element_type=jnp.float32
    )


def chain(before, behind):
    return (before[0] * behind[0], behind[1] + behind[0] * before[1])


def silu_slope(array_in):
    sigmoid_val = jax.nn.sigmoid(array_in)
    return sigmoid_val * (1.0 + array_in * (1.0 - sigmoid_val))


def norm_back(grad_norm, array_in, scale_val):
    return scale_val * grad_norm - array_in * scale_val**3 * jnp.mean(
        grad_norm * array_in, axis=-1, keepdims=True
    )


def gelu_tanh(array_in):
    return jax.nn.gelu(array_in, approximate=True)


def time_major(array_in, per_batch, span_len):
    return jnp.swapaxes(array_in.reshape(per_batch, span_len, -1), 0, 1)


def row_major(array_in, block_rows):
    return jnp.swapaxes(array_in, 0, 1).reshape(block_rows, -1)


def by_source(array_in, local_experts, capacity, model_width):
    return jnp.swapaxes(array_in.reshape(local_experts, -1, capacity, model_width), 0, 1)


def by_expert(array_in, local_experts, model_width):
    return jnp.swapaxes(array_in, 0, 1).reshape(local_experts, -1, model_width)


def fetch_dense(
    norm_gain,
    in_proj,
    conv_weight,
    conv_bias,
    x_proj,
    dt_proj,
    dt_bias,
    a_log,
    skip_gain,
    out_proj,
    moe_gain,
    router,
):
    return (
        lax.all_gather(norm_gain, ("batch", "seq"), axis=0, tiled=True),
        lax.all_gather(in_proj, ("batch", "seq"), axis=0, tiled=True),
        lax.all_gather(conv_weight, ("batch", "seq"), axis=0, tiled=True),
        lax.all_gather(conv_bias, ("batch", "seq"), axis=0, tiled=True),
        lax.all_gather(x_proj, ("batch", "seq"), axis=0, tiled=True),
        lax.all_gather(dt_proj, ("batch", "seq"), axis=0, tiled=True),
        lax.all_gather(dt_bias, ("batch", "seq"), axis=0, tiled=True),
        lax.all_gather(a_log, ("batch", "seq"), axis=0, tiled=True),
        lax.all_gather(skip_gain, ("batch", "seq"), axis=0, tiled=True),
        lax.all_gather(out_proj, ("batch", "seq"), axis=0, tiled=True),
        lax.all_gather(moe_gain, ("batch", "seq"), axis=0, tiled=True),
        lax.all_gather(router, ("batch", "seq"), axis=0, tiled=True),
    )


def shards(
    tokens,
    cotangent,
    lengths,
    order,
    expert_route,
    slot_index,
    norm_gain,
    in_proj,
    conv_weight,
    conv_bias,
    x_proj,
    dt_proj,
    dt_bias,
    a_log,
    skip_gain,
    out_proj,
    moe_gain,
    router,
    expert_in,
    expert_out,
):
    seq_count, span_len, model_width = tokens.shape
    per_batch = SEQ_MB
    batch_size = lax.axis_size("batch")
    local_experts = expert_in.shape[0]
    expert_count = local_experts * batch_size
    block_rows = per_batch * span_len
    capacity = max(2, (5 * block_rows + 4 * expert_count - 1) // (4 * expert_count))
    inner_width = DI
    dt_width = DT_RANK
    state_dimension = STATE
    conv_taps = CONV
    sub_len = math.gcd(span_len, 8)
    sub_count = span_len // sub_len
    sub_ids = jnp.arange(sub_len, dtype=jnp.int32)
    lower_mask = (sub_ids[:, None] >= sub_ids[None, :]).astype(jnp.float32)
    upper_mask = jnp.transpose(lower_mask)
    positions = lax.axis_index("seq") * span_len + jnp.arange(span_len, dtype=jnp.int32)
    row_length = jnp.sum(
        jnp.where(
            order[:, None] == jnp.arange(lengths.shape[0], dtype=jnp.int32)[None, :],
            lengths[None, :],
            0,
        ),
        axis=1,
    )
    slot_ids = jnp.arange(expert_count * capacity, dtype=jnp.int32)
    expert_ids = jnp.arange(expert_count, dtype=jnp.int32)
    first_weight, second_weight = (expert_in, expert_out)
    grad_shapes = [
        (model_width,),
        (model_width, 2 * inner_width),
        (inner_width, conv_taps),
        (inner_width,),
        (inner_width, dt_width + 2 * state_dimension),
        (inner_width, dt_width),
        (inner_width,),
        (inner_width, state_dimension),
        (inner_width,),
        (inner_width, model_width),
        (model_width,),
        (model_width, expert_count),
    ]
    dense_grads = [jnp.zeros(grad_shape, jnp.float32) for grad_shape in grad_shapes]
    grad_first = jnp.zeros(first_weight.shape, jnp.float32)
    grad_second = jnp.zeros(second_weight.shape, jnp.float32)
    zero_state = jnp.zeros((per_batch, inner_width, state_dimension), jnp.float32)
    unit_state = jnp.ones_like(zero_state)

    def sub_blocks(array_in):
        return array_in.reshape((sub_count, sub_len) + array_in.shape[1:])

    def whole_span(array_in):
        return array_in.reshape((span_len,) + array_in.shape[2:])

    out_parts = []
    grad_parts = []
    for micro_batch in range(seq_count // per_batch):
        weights = fetch_dense(
            norm_gain,
            in_proj,
            conv_weight,
            conv_bias,
            x_proj,
            dt_proj,
            dt_bias,
            a_log,
            skip_gain,
            out_proj,
            moe_gain,
            router,
        )
        (
            gain_one,
            w_joint,
            w_conv,
            bias_conv,
            w_proj,
            w_step,
            bias_step,
            log_rate,
            w_skip,
            w_back,
            gain_two,
            router_weight,
        ) = weights
        lower = micro_batch * per_batch
        upper = lower + per_batch
        block_in = tokens[lower:upper].reshape(block_rows, model_width).astype(jnp.float32)
        keep_mask = (positions[None, :] < row_length[lower:upper][:, None]).astype(jnp.float32)
        grad_out = (cotangent[lower:upper].astype(jnp.float32) * keep_mask[..., None]).reshape(
            block_rows, model_width
        )
        expert_pick = expert_route[lower:upper].reshape(block_rows)
        slot_row = slot_index[lower:upper].reshape(block_rows)
        gain_first = gain_one.astype(jnp.float32)
        gain_second = gain_two.astype(jnp.float32)
        skip_scale = w_skip.astype(jnp.float32)
        conv_scale = w_conv.astype(jnp.float32)
        decay_rate = -jnp.exp(log_rate.astype(jnp.float32))

        def advance_block(hidden_state, block_items):
            step_block, drive_block = block_items
            running = jnp.cumsum(step_block, axis=0)
            spread = running[:, None] - running[None, :]
            spread = jnp.where(lower_mask[:, :, None, None] > 0, spread, 0.0)
            weight = jnp.exp(spread[..., None] * decay_rate) * lower_mask[:, :, None, None, None]
            block_states = (
                jnp.sum(weight * drive_block[None], axis=1)
                + jnp.exp(running[..., None] * decay_rate) * hidden_state[None]
            )
            return (block_states[-1], block_states)

        def retreat_block(loop_carry, block_items):
            step_block, source_block = block_items
            running = jnp.cumsum(step_block, axis=0)
            spread = running[None, :] - running[:, None]
            spread = jnp.where(upper_mask[:, :, None, None] > 0, spread, 0.0)
            weight = jnp.exp(spread[..., None] * decay_rate) * upper_mask[:, :, None, None, None]
            block_adjoint = (
                jnp.sum(weight * source_block[None], axis=1)
                + jnp.exp((running[-1][None] - running)[..., None] * decay_rate) * loop_carry[None]
            )
            next_carry = jnp.exp(step_block[0][..., None] * decay_rate) * block_adjoint[0]
            return (next_carry, block_adjoint)

        scale_one = lax.rsqrt(jnp.mean(block_in * block_in, axis=-1, keepdims=True) + EPSILON)
        normed = (block_in * scale_one * gain_first).astype(jnp.bfloat16)
        joint_proj = jnp.dot(normed, w_joint, preferred_element_type=jnp.float32)
        conv_in = joint_proj[:, :inner_width].reshape(per_batch, span_len, inner_width)
        gate_in = joint_proj[:, inner_width:]
        rim_cells = shifted(conv_in[:, span_len - (conv_taps - 1) :, :], "seq", 1)
        padded = jnp.concatenate([rim_cells, conv_in], axis=1)
        conv_out = bias_conv.astype(jnp.float32) + sum(
            (
                padded[:, tap_index : tap_index + span_len, :] * conv_scale[:, tap_index]
                for tap_index in range(conv_taps)
            )
        )
        conv_out = conv_out.reshape(block_rows, inner_width)
        act_low = jax.nn.silu(conv_out).astype(jnp.bfloat16)
        activated = act_low.astype(jnp.float32)
        projected = jnp.dot(act_low, w_proj, preferred_element_type=jnp.float32)
        delta_low = projected[:, :dt_width].astype(jnp.bfloat16)
        input_map = projected[:, dt_width : dt_width + state_dimension]
        output_map = projected[:, dt_width + state_dimension :]
        step_arg = cols_product(delta_low, w_step) + bias_step.astype(jnp.float32)
        step_size = jax.nn.softplus(step_arg)
        step_time = time_major(step_size, per_batch, span_len)
        act_time = time_major(activated, per_batch, span_len)
        in_time = time_major(input_map, per_batch, span_len)
        out_time = time_major(output_map, per_batch, span_len)
        decay = jnp.exp(step_time[..., None] * decay_rate)
        drive = (step_time * act_time)[..., None] * in_time[:, :, None, :]
        _, local_blocks = lax.scan(
            advance_block, zero_state, (sub_blocks(step_time), sub_blocks(drive))
        )
        local_states = whole_span(local_blocks)
        elapsed = jnp.cumsum(step_time, axis=0)
        reach = jnp.exp(elapsed[..., None] * decay_rate)
        carried = entering(
            (reach[-1], local_states[-1]), "seq", chain, (unit_state, zero_state), False
        )
        state_init = carried[1]
        states = local_states + reach * state_init[None]
        mixed_time = jnp.sum(states * out_time[:, :, None, :], axis=-1)
        mixed_out = row_major(mixed_time, block_rows) + skip_scale * activated
        gate_act = jax.nn.silu(gate_in)
        gated_out = (mixed_out * gate_act).astype(jnp.bfloat16)
        mixed_rows = block_in + jnp.dot(gated_out, w_back, preferred_element_type=jnp.float32)
        scale_two = lax.rsqrt(jnp.mean(mixed_rows * mixed_rows, axis=-1, keepdims=True) + EPSILON)
        routed_tokens = (mixed_rows * scale_two * gain_second).astype(jnp.bfloat16)
        router_logits = jnp.dot(routed_tokens, router_weight, preferred_element_type=jnp.float32)
        softmax_out = jax.nn.softmax(router_logits, axis=-1)
        kept_slot = slot_row >= 0
        target = jnp.where(kept_slot, expert_pick * capacity + slot_row, -1)
        selector = (target[:, None] == slot_ids[None, :]).astype(jnp.bfloat16)
        chosen = jnp.logical_and(expert_pick[:, None] == expert_ids[None, :], kept_slot[:, None])
        gate_value = jnp.sum(jnp.where(chosen, softmax_out, 0.0), axis=-1)
        send_rows = (
            rows_product(selector, routed_tokens)
            .astype(jnp.bfloat16)
            .reshape(batch_size, local_experts, capacity, model_width)
        )
        arrived = lax.all_to_all(send_rows, "batch", split_axis=0, concat_axis=0, tiled=True)
        all_rows = lax.all_gather(arrived, "seq", axis=0, tiled=True)
        expert_rows_in = by_expert(all_rows, local_experts, model_width)
        hidden = jnp.einsum(
            "jrd,jdf->jrf", expert_rows_in, first_weight, preferred_element_type=jnp.float32
        )
        activation, gelu_back = jax.vjp(gelu_tanh, hidden)
        act_rows = activation.astype(jnp.bfloat16)
        partial_out = jnp.einsum(
            "jrf,jfd->jrd", act_rows, second_weight, preferred_element_type=jnp.float32
        )
        summed = lax.psum_scatter(
            by_source(partial_out, local_experts, capacity, model_width).astype(jnp.bfloat16),
            "seq",
            scatter_dimension=0,
            tiled=True,
        )
        returned = lax.all_to_all(summed, "batch", split_axis=0, concat_axis=0, tiled=True).reshape(
            expert_count * capacity, model_width
        )
        expert_tok = jnp.dot(selector, returned, preferred_element_type=jnp.float32)
        result_rows = mixed_rows + gate_value[:, None] * expert_tok
        out_parts.append(result_rows.astype(jnp.bfloat16).reshape(per_batch, span_len, model_width))
        grad_expert = (gate_value[:, None] * grad_out).astype(jnp.bfloat16)
        grad_gate = jnp.sum(expert_tok * grad_out, axis=-1)
        send_grads = (
            rows_product(selector, grad_expert)
            .astype(jnp.bfloat16)
            .reshape(batch_size, local_experts, capacity, model_width)
        )
        grads_arrived = lax.all_to_all(send_grads, "batch", split_axis=0, concat_axis=0, tiled=True)
        grads_all = lax.all_gather(grads_arrived, "seq", axis=0, tiled=True)
        grad_rows_in = by_expert(grads_all, local_experts, model_width)
        grad_act = jnp.einsum(
            "jrd,jfd->jrf", grad_rows_in, second_weight, preferred_element_type=jnp.float32
        )
        grad_hidden = gelu_back(grad_act)[0].astype(jnp.bfloat16)
        grad_second = grad_second + jnp.einsum(
            "jrf,jrd->jfd", act_rows, grad_rows_in, preferred_element_type=jnp.float32
        )
        grad_first = grad_first + jnp.einsum(
            "jrd,jrf->jdf", expert_rows_in, grad_hidden, preferred_element_type=jnp.float32
        )
        grad_partial = jnp.einsum(
            "jrf,jdf->jrd", grad_hidden, first_weight, preferred_element_type=jnp.float32
        )
        grad_summed = lax.psum_scatter(
            by_source(grad_partial, local_experts, capacity, model_width).astype(jnp.bfloat16),
            "seq",
            scatter_dimension=0,
            tiled=True,
        )
        grad_back = lax.all_to_all(
            grad_summed, "batch", split_axis=0, concat_axis=0, tiled=True
        ).reshape(expert_count * capacity, model_width)
        grad_routed = jnp.dot(selector, grad_back, preferred_element_type=jnp.float32)
        grad_prob = jnp.where(chosen, grad_gate[:, None], 0.0)
        grad_logit = (
            softmax_out * (grad_prob - jnp.sum(softmax_out * grad_prob, axis=-1, keepdims=True))
        ).astype(jnp.bfloat16)
        dense_grads[11] = dense_grads[11] + rows_product(routed_tokens, grad_logit)
        grad_routed = grad_routed + cols_product(grad_logit, router_weight)
        dense_grads[10] = dense_grads[10] + jnp.sum(grad_routed * mixed_rows * scale_two, axis=0)
        grad_mixed = grad_out + norm_back(grad_routed * gain_second, mixed_rows, scale_two)
        grad_branch = grad_mixed.astype(jnp.bfloat16)
        dense_grads[9] = dense_grads[9] + rows_product(gated_out, grad_branch)
        grad_gated = cols_product(grad_branch, w_back)
        grad_mixed_out = grad_gated * gate_act
        grad_gate_in = grad_gated * mixed_out * silu_slope(gate_in)
        dense_grads[8] = dense_grads[8] + jnp.sum(grad_mixed_out * activated, axis=0)
        grad_time = time_major(grad_mixed_out, per_batch, span_len)
        source_term = grad_time[..., None] * out_time[:, :, None, :]
        first_term, adjoint_blocks = lax.scan(
            retreat_block,
            zero_state,
            (sub_blocks(step_time), sub_blocks(source_term)),
            reverse=True,
        )
        local_adjoint = whole_span(adjoint_blocks)
        behind = entering((reach[-1], first_term), "seq", chain, (unit_state, zero_state), True)
        adjoint = (
            local_adjoint
            + jnp.exp((elapsed[-1][None] - elapsed)[..., None] * decay_rate) * behind[1][None]
        )
        prior = jnp.concatenate([state_init[None], states[:-1]], axis=0)
        flow = adjoint * prior * decay
        input_pull = jnp.sum(adjoint * in_time[:, :, None, :], axis=-1)
        grad_step_time = jnp.sum(flow * decay_rate, axis=-1) + act_time * input_pull
        dense_grads[7] = (
            dense_grads[7] + jnp.sum(flow * step_time[..., None], axis=(0, 1)) * decay_rate
        )
        grad_in_time = jnp.sum(adjoint * (step_time * act_time)[..., None], axis=2)
        grad_out_time = jnp.sum(grad_time[..., None] * states, axis=2)
        grad_act_val = skip_scale * grad_mixed_out + row_major(step_time * input_pull, block_rows)
        grad_arg = row_major(grad_step_time, block_rows) * jax.nn.sigmoid(step_arg)
        dense_grads[6] = dense_grads[6] + jnp.sum(grad_arg, axis=0)
        grad_pre = grad_arg.astype(jnp.bfloat16)
        dense_grads[5] = dense_grads[5] + rows_product(grad_pre, delta_low)
        grad_delta = jnp.dot(grad_pre, w_step, preferred_element_type=jnp.float32)
        grad_proj = jnp.concatenate(
            [grad_delta, row_major(grad_in_time, block_rows), row_major(grad_out_time, block_rows)],
            axis=-1,
        ).astype(jnp.bfloat16)
        dense_grads[4] = dense_grads[4] + rows_product(act_low, grad_proj)
        grad_act_val = grad_act_val + cols_product(grad_proj, w_proj)
        grad_conv = (grad_act_val * silu_slope(conv_out)).reshape(per_batch, span_len, inner_width)
        dense_grads[3] = dense_grads[3] + jnp.sum(grad_conv, axis=(0, 1))
        dense_grads[2] = dense_grads[2] + jnp.stack(
            [
                jnp.sum(grad_conv * padded[:, tap_index : tap_index + span_len, :], axis=(0, 1))
                for tap_index in range(conv_taps)
            ],
            axis=-1,
        )
        grad_padded = sum(
            (
                jnp.pad(
                    grad_conv * conv_scale[:, tap_index],
                    ((0, 0), (tap_index, conv_taps - 1 - tap_index), (0, 0)),
                )
                for tap_index in range(conv_taps)
            )
        )
        rim_back = shifted(grad_padded[:, : conv_taps - 1, :], "seq", -1)
        grad_conv_in = grad_padded[:, conv_taps - 1 :, :] + jnp.pad(
            rim_back, ((0, 0), (span_len - (conv_taps - 1), 0), (0, 0))
        )
        grad_joint = jnp.concatenate(
            [grad_conv_in.reshape(block_rows, inner_width), grad_gate_in], axis=-1
        ).astype(jnp.bfloat16)
        dense_grads[1] = dense_grads[1] + rows_product(normed, grad_joint)
        grad_normed = cols_product(grad_joint, w_joint)
        dense_grads[0] = dense_grads[0] + jnp.sum(grad_normed * block_in * scale_one, axis=0)
        grad_input = grad_mixed + norm_back(grad_normed * gain_first, block_in, scale_one)
        grad_parts.append(grad_input.reshape(per_batch, span_len, model_width))
    dense_sums = (
        lax.psum_scatter(dense_grads[0], ("batch", "seq"), scatter_dimension=0, tiled=True),
        lax.psum_scatter(dense_grads[1], ("batch", "seq"), scatter_dimension=0, tiled=True),
        lax.psum_scatter(dense_grads[2], ("batch", "seq"), scatter_dimension=0, tiled=True),
        lax.psum_scatter(dense_grads[3], ("batch", "seq"), scatter_dimension=0, tiled=True),
        lax.psum_scatter(dense_grads[4], ("batch", "seq"), scatter_dimension=0, tiled=True),
        lax.psum_scatter(dense_grads[5], ("batch", "seq"), scatter_dimension=0, tiled=True),
        lax.psum_scatter(dense_grads[6], ("batch", "seq"), scatter_dimension=0, tiled=True),
        lax.psum_scatter(dense_grads[7], ("batch", "seq"), scatter_dimension=0, tiled=True),
        lax.psum_scatter(dense_grads[8], ("batch", "seq"), scatter_dimension=0, tiled=True),
        lax.psum_scatter(dense_grads[9], ("batch", "seq"), scatter_dimension=0, tiled=True),
        lax.psum_scatter(dense_grads[10], ("batch", "seq"), scatter_dimension=0, tiled=True),
        lax.psum_scatter(dense_grads[11], ("batch", "seq"), scatter_dimension=0, tiled=True),
    )
    return (
        jnp.concatenate(out_parts, axis=0),
        jnp.concatenate(grad_parts, axis=0),
        dense_sums[0],
        dense_sums[1],
        dense_sums[2],
        dense_sums[3],
        dense_sums[4],
        dense_sums[5],
        dense_sums[6],
        dense_sums[7],
        dense_sums[8],
        dense_sums[9],
        dense_sums[10],
        dense_sums[11],
        grad_first,
        grad_second,
    )


def solution(mesh):
    return jax.shard_map(
        shards,
        mesh=mesh,
        in_specs=(
            P("batch", "seq", None),
            P("batch", "seq", None),
            P(),
            P("batch"),
            P("batch", "seq"),
            P("batch", "seq"),
            P(("batch", "seq")),
            P(("batch", "seq"), None),
            P(("batch", "seq"), None),
            P(("batch", "seq")),
            P(("batch", "seq"), None),
            P(("batch", "seq"), None),
            P(("batch", "seq")),
            P(("batch", "seq"), None),
            P(("batch", "seq")),
            P(("batch", "seq"), None),
            P(("batch", "seq")),
            P(("batch", "seq"), None),
            P("batch", None, "seq"),
            P("batch", "seq", None),
        ),
        out_specs=(
            P("batch", "seq", None),
            P("batch", "seq", None),
            P(("batch", "seq")),
            P(("batch", "seq"), None),
            P(("batch", "seq"), None),
            P(("batch", "seq")),
            P(("batch", "seq"), None),
            P(("batch", "seq"), None),
            P(("batch", "seq")),
            P(("batch", "seq"), None),
            P(("batch", "seq")),
            P(("batch", "seq"), None),
            P(("batch", "seq")),
            P(("batch", "seq"), None),
            P("batch", None, "seq"),
            P("batch", "seq", None),
        ),
        check_vma=False,
    )
```

profile of v0, /device:TPU:0, one launch (start us, length us, event | category | flops | bytes accessed | tf_op | source)
XLA Modules:
  0.0 3714.8 jit_solution(8535298011308958539)
XLA Ops:
  13.0 42.4 %all-reduce.32 = (bf16[768]{0:T(1024)(128)(2,1)S(1)}, bf16[1536]{0:T(1024)(128)(2,1)S(1)}, bf16[1536]{0:T(1024)(128)(2,1)S(1)}, bf16[1536]{0:T(1024)(128)(2,1)}, bf16[768]{0:T(1024)(128)(2,1)}) all-reduce(bf16[768]{0:T(1024)(128)(2,1)S(1)} %dynamic-update-slice.1, ...), channel_id=1, replica_groups=mesh['batch'=8,'seq'=4] {'batch','seq'}, use_global_device_ids=true, to_apply=%add.21 | all-reduce | flops 6144 | bytes 24576
  58.9 40.8 %all-gather.4 = bf16[32,48,4]{1,2,0:T(4,128)(2,1)S(1)} all-gather(bf16[1,48,4]{1,2,0:T(4,128)(2,1)S(1)} %bitcast.1374), channel_id=1, replica_groups=mesh['batch'=8,'seq'=4] {'batch','seq'}, dimensions={0}, use_global_device_ids=true | all-gather | bytes 12672 | tf_op jit(solution)/shard_map/all_gather | solution.py:111
  99.9 40.7 %all_gather.76 = bf16[1536,80]{1,0:T(8,128)(2,1)} all-gather(bf16[48,80]{1,0:T(8,128)(2,1)S(1)} %copy-done.372), channel_id=1, replica_groups=mesh['batch'=8,'seq'=4] {'batch','seq'}, dimensions={0}, use_global_device_ids=true | all-gather | bytes 253440 | tf_op jit(solution)/shard_map/all_gather | solution.py:113
  140.6 39.1 %all_gather.77 = bf16[1536,48]{1,0:T(8,128)(2,1)S(1)} all-gather(bf16[48,48]{1,0:T(8,128)(2,1)S(1)} %copy-done.373), channel_id=1, replica_groups=mesh['batch'=8,'seq'=4] {'batch','seq'}, dimensions={0}, use_global_device_ids=true | all-gather | bytes 152064 | tf_op jit(solution)/shard_map/all_gather | solution.py:114
  180.9 37.0 all-gather.5
  347.8 153.0 %while.243 = (s32[]{:T(128)}, f32[1,1536,16]{1,2,0:T(8,128)S(1)}, f32[32,8,1,1536,16]{3,4,1,2,0:T(8,128)}, f32[32,8,1,1536]{3,1,2,0:T(8,128)}, f32[1536,16]{0,1:...) while((s32[]{:T(128)}, f32[1,1536,16]{1,2,0:T(8,128)S(1)}, ...), condition=%wide.region_49.50_spmd.clone.clone, body=%wide.region_46.49_spmd.clone.clone.sunk | while | flops 7041346 | bytes 6704353 | solution.py:299
  534.9 153.1 %while.242 = (s32[]{:T(128)}, f32[1,1536,16]{1,2,0:T(8,128)S(1)}, f32[32,8,1,1536,16]{3,4,1,2,0:T(8,128)}, f32[32,8,1,1536]{3,1,2,0:T(8,128)}, f32[1536,16]{0,1:...) while((s32[]{:T(128)}, f32[1,1536,16]{1,2,0:T(8,128)S(1)}, ...), condition=%wide.region_34.35_spmd.clone.clone, body=%wide.region_31.34_spmd.clone.clone.sunk | while | flops 7041346 | bytes 6704353 | solution.py:299
  723.3 153.0 %while.241 = (s32[]{:T(128)}, f32[1,1536,16]{1,2,0:T(8,128)S(1)}, f32[32,8,1,1536,16]{3,4,1,2,0:T(8,128)}, f32[32,8,1,1536]{3,1,2,0:T(8,128)}, f32[1536,16]{0,1:...) while((s32[]{:T(128)}, f32[1,1536,16]{1,2,0:T(8,128)S(1)}, ...), condition=%wide.region_19.20_spmd.clone.clone, body=%wide.region_16.19_spmd.clone.clone.sunk | while | flops 7041346 | bytes 6704353 | solution.py:299
  912.2 152.8 %while.240 = (s32[]{:T(128)}, f32[1,1536,16]{1,2,0:T(8,128)S(1)}, f32[32,8,1,1536,16]{3,4,1,2,0:T(8,128)}, f32[32,8,1,1536]{3,1,2,0:T(8,128)}, f32[1536,16]{0,1:...) while((s32[]{:T(128)}, f32[1,1536,16]{1,2,0:T(8,128)S(1)}, ...), condition=%wide.region_4.5_spmd.clone.clone, body=%wide.region_1.4_spmd.clone.clone.sunk | while | flops 7041346 | bytes 6704353 | solution.py:299
  1073.3 53.2 %multiply_reduce_fusion.31 = (f32[32,8,1536]{2,1,0:T(8,128)}, f32[32,8,1536]{2,1,0:T(8,128)}, f32[32,8,1536]{2,1,0:T(8,128)}, f32[32,8,1536]{2,1,0:T(8,128)}) fusion(f32[32,8,1,1536,16]{3,4,1,2,0:T(8,128)} %get-tuple-element.1268, f32[32,8,16]{2,1,0:T(8,128)} %bitcast.1324, f32[1536,16]{0,1:T(8,128)S(1)} %bitcast.1261, ...), kind=kLoop, calls=%fused_computation.188 | loop fusion | flops 124256256 | bytes 113803264 | tf_op jit(solution)/shard_map/reduce_sum | solution.py:310
  1328.5 43.1 %all-gather.6 = bf16[32,24,8]{1,2,0:T(8,128)(2,1)S(1)} all-gather(bf16[1,24,8]{1,2,0:T(8,128)(2,1)S(1)} %bitcast.1373), channel_id=1, replica_groups=mesh['batch'=8,'seq'=4] {'batch','seq'}, dimensions={0}, use_global_device_ids=true | all-gather | bytes 12672 | tf_op jit(solution)/shard_map/all_gather | solution.py:120
  1789.2 179.8 %while.244 = (s32[]{:T(128)}, f32[1,1536,16]{1,2,0:T(8,128)S(1)}, f32[32,8,1,1536,16]{3,4,1,2,0:T(8,128)}, f32[32,8,1,1536]{3,1,2,0:T(8,128)}, f32[1536,16]{0,1:...) while((s32[]{:T(128)}, f32[1,1536,16]{1,2,0:T(8,128)S(1)}, ...), condition=%wide.region_68.69_spmd.clone.clone, body=%wide.region_65.68_spmd.clone.clone.sunk | while | flops 7127364 | bytes 6939407 | solution.py:401
  2009.5 226.9 %while.245 = (s32[]{:T(128)}, f32[1,1536,16]{1,2,0:T(8,128)}, f32[32,8,1,1536,16]{3,4,1,2,0:T(8,128)}, f32[32,8,1,1536]{3,1,2,0:T(8,128)}, f32[1536,16]{0,1:T(8,...) while((s32[]{:T(128)}, f32[1,1536,16]{1,2,0:T(8,128)}, ...), condition=%wide.region_83.84_spmd.clone.clone, body=%wide.region_80.83_spmd.clone.clone.sunk | while | flops 7127364 | bytes 6939407 | solution.py:401
  2245.6 60.7 %multiply_reduce_fusion.10 = (f32[1536,16]{0,1:T(8,128)}, f32[32,8,1536]{2,1,0:T(8,128)}, bf16[32,8,16]{2,1,0:T(8,128)(2,1)}, f32[32,8,1536]{2,1,0:T(8,128)}, f3...) fusion(f32[32,8,1536]{2,1,0:T(8,128)} %get-tuple-element.2324, ...), kind=kLoop, calls=%fused_computation.146 | loop fusion | flops 205983744 | bytes 145350656 | tf_op jit(solution)/shard_map/reduce_sum | solution.py:418
  2321.4 37.9 %multiply_reduce_fusion.16 = (bf16[32,8,16]{2,1,0:T(8,128)(2,1)}, bf16[32,8,16]{2,1,0:T(8,128)(2,1)}, f32[32,8,1,1536,16]{3,4,2,1,0:T(8,128)}, f32[32,8,1,1536,16]{3,4,2,1,0:T(8,128)}) fusion(f32[32,8,1,1536,16]{3,4,1,2,0:T(8,128)} %get-tuple-element.1272, f32[32,8,1536]{2,1,0:T(8,128)S(1)} %bitcast.1308, f32[1536,16]{0,1:T(8,128)S(1)} %bitcast.1256, ...), kind=kLoop, calls=%fused_computation.155 | loop fusion | flops 75489280 | bytes 107298816 | tf_op jit(solution)/shard_map/reduce_sum | solution.py:421
  2370.9 274.0 %while.247 = (s32[]{:T(128)}, f32[1,1536,16]{1,2,0:T(8,128)S(1)}, f32[32,8,1,1536,16]{3,4,1,2,0:T(8,128)}, f32[32,8,1,1536]{3,1,2,0:T(8,128)}, f32[1536,16]{0,1:...) while((s32[]{:T(128)}, f32[1,1536,16]{1,2,0:T(8,128)S(1)}, ...), condition=%wide.region_113.114_spmd.clone.clone, body=%wide.region_110.113_spmd.clone.clone.sunk | while | flops 7127364 | bytes 6939407 | solution.py:401
  2664.6 274.0 %while.246 = (s32[]{:T(128)}, f32[1,1536,16]{1,2,0:T(8,128)S(1)}, f32[32,8,1,1536,16]{3,4,1,2,0:T(8,128)}, f32[32,8,1,1536]{3,1,2,0:T(8,128)}, f32[1536,16]{0,1:...) while((s32[]{:T(128)}, f32[1,1536,16]{1,2,0:T(8,128)S(1)}, ...), condition=%wide.region_98.99_spmd.clone.clone, body=%wide.region_95.98_spmd.clone.clone.sunk | while | flops 7127364 | bytes 6939407 | solution.py:401
  2954.4 62.2 %multiply_reduce_fusion.9 = (f32[1536,16]{0,1:T(8,128)}, f32[32,8,1536]{2,1,0:T(8,128)}, bf16[32,8,16]{2,1,0:T(8,128)(2,1)}, f32[32,8,1536]{2,1,0:T(8,128)S(1)},...) fusion(f32[32,8,1536]{2,1,0:T(8,128)} %get-tuple-element.2334, ...), kind=kLoop, calls=%fused_computation.145 | loop fusion | flops 205983744 | bytes 145350656 | tf_op jit(solution)/shard_map/reduce_sum | solution.py:418
  3159.2 42.4 %all-reduce.31 = (f32[768]{0:T(1024)S(1)}, f32[1536]{0:T(1024)S(1)}, f32[1536]{0:T(1024)S(1)}, f32[1536]{0:T(1024)S(1)}, f32[768]{0:T(1024)S(1)}, /*index=5*/f32[768,8]{0,1:T(8,128)S(1)}) all-reduce(f32[768]{0:T(1024)S(1)} %add_add_fusion.6, ...), channel_id=14, replica_groups=mesh['batch'=8,'seq'=4] {'batch','seq'}, use_global_device_ids=true, to_apply=%region_125.126.clone | all-reduce | flops 12288 | bytes 98304
  3212.3 40.9 %reduce-scatter.46.cloned.1.call-done = f32[48,16]{1,0:T(8,128)} async-done(((f32[1536,16]{1,0:T(8,128)}), f32[48,16]{1,0:T(8,128)}) %reduce-scatter.46.cloned.1.call-update) | async-done | bytes 3088
  3254.5 98.9 %reduce-scatter.40.cloned.1.call-done = f32[48,48]{1,0:T(8,128)} async-done(((f32[1536,48]{1,0:T(8,128)}), f32[48,48]{1,0:T(8,128)}) %reduce-scatter.40.cloned.1.call-update) | async-done | bytes 9232 | tf_op jit(solution)/shard_map/reduce_scatter | solution.py:470
  3353.4 100.3 %reduce-scatter.38.cloned.1.call-done = f32[48,80]{1,0:T(8,128)} async-done(((f32[1536,80]{1,0:T(8,128)}), f32[48,80]{1,0:T(8,128)}) %reduce-scatter.38.cloned.1.call-update) | async-done | bytes 15376 | tf_op jit(solution)/shard_map/reduce_scatter | solution.py:469
  3453.7 112.1 %reduce-scatter.42.cloned.1.call-done = f32[48,768]{1,0:T(8,128)} async-done(((f32[1536,768]{1,0:T(8,128)}), f32[48,768]{1,0:T(8,128)}) %reduce-scatter.42.cloned.1.call-update) | async-done | bytes 147472 | tf_op jit(solution)/shard_map/reduce_scatter | solution.py:474
  3565.8 141.9 %reduce-scatter.36.cloned.1.call-done = f32[24,3072]{1,0:T(8,128)} async-done(((f32[768,3072]{1,0:T(8,128)}), f32[24,3072]{1,0:T(8,128)}) %reduce-scatter.36.cloned.1.call-update) | async-done | bytes 294928 | tf_op jit(solution)/shard_map/reduce_scatter | solution.py:466
  (4580 shorter events, 2694.9 us)
Async XLA Ops:
  7.2 217.0 %all-gather.18.cloned.1.call-start = ((), (), s32[]{:S(2)}) async-start(), calls=%async_computation.30 | async-start | bytes 4866048 | tf_op jit(solution)/shard_map/all_gather | solution.py:110
  8.0 1125.5 %all-gather.20.cloned.1.call-start = ((), (), s32[]{:S(2)}) async-start(), calls=%async_computation.31 | async-start | bytes 2433024 | tf_op jit(solution)/shard_map/all_gather | solution.py:118
  8.7 1207.9 %all-gather.28.cloned.1.call-start = ((), (), s32[]{:S(2)}) async-start(), calls=%async_computation.38 | async-start | bytes 2457600 | tf_op jit(solution)/shard_map/all_gather | solution.py:330
  1163.2 63.9 %all-gather.26.cloned.1.call-start = ((), (), s32[]{:S(2)}) async-start(), calls=%async_computation.36 | async-start | bytes 2457600 | tf_op jit(solution)/shard_map/all_gather | solution.py:330
  1181.6 55.8 %all-gather.24.cloned.1.call-start = ((), (), s32[]{:S(2)}) async-start(), calls=%async_computation.34 | async-start | bytes 2457600 | tf_op jit(solution)/shard_map/all_gather | solution.py:330
  1199.2 56.6 %all-gather.22.cloned.1.call-start = ((), (), s32[]{:S(2)}) async-start(), calls=%async_computation.32 | async-start | bytes 2457600 | tf_op jit(solution)/shard_map/all_gather | solution.py:330
  1216.6 72.4 %reduce-scatter.26.cloned.1.call-start = ((), (), s32[]{:S(2)}) async-start(), calls=%async_computation.39 | async-start | bytes 2457600 | tf_op jit(solution)/shard_map/reduce_scatter | solution.py:340
  1227.0 95.9 %reduce-scatter.24.cloned.1.call-start = ((), (), s32[]{:S(2)}) async-start(), calls=%async_computation.37 | async-start | bytes 2457600 | tf_op jit(solution)/shard_map/reduce_scatter | solution.py:340
  1237.3 135.2 %reduce-scatter.22.cloned.1.call-start = ((), (), s32[]{:S(2)}) async-start(), calls=%async_computation.35 | async-start | bytes 2457600 | tf_op jit(solution)/shard_map/reduce_scatter | solution.py:340
  1247.6 142.6 %reduce-scatter.20.cloned.1.call-start = ((), (), s32[]{:S(2)}) async-start(), calls=%async_computation.33 | async-start | bytes 2457600 | tf_op jit(solution)/shard_map/reduce_scatter | solution.py:340
  1395.8 111.7 %all-gather.30.cloned.1.call-start = ((), (), s32[]{:S(2)}) async-start(), calls=%async_computation.40 | async-start | bytes 2457600 | tf_op jit(solution)/shard_map/all_gather | solution.py:360
  1432.6 139.7 %all-gather.32.cloned.1.call-start = ((), (), s32[]{:S(2)}) async-start(), calls=%async_computation.42 | async-start | bytes 2457600 | tf_op jit(solution)/shard_map/all_gather | solution.py:360
  1459.1 169.2 %all-gather.36.cloned.1.call-start = ((), (), s32[]{:S(2)}) async-start(), calls=%async_computation.46 | async-start | bytes 2457600 | tf_op jit(solution)/shard_map/all_gather | solution.py:360
  1507.0 167.3 %reduce-scatter.28.cloned.1.call-start = ((), (), s32[]{:S(2)}) async-start(), calls=%async_computation.41 | async-start | bytes 2457600 | tf_op jit(solution)/shard_map/reduce_scatter | solution.py:375
  1518.4 162.1 %all-gather.34.cloned.1.call-start = ((), (), s32[]{:S(2)}) async-start(), calls=%async_computation.44 | async-start | bytes 2457600 | tf_op jit(solution)/shard_map/all_gather | solution.py:360
  1545.5 145.9 %reduce-scatter.30.cloned.1.call-start = ((), (), s32[]{:S(2)}) async-start(), calls=%async_computation.43 | async-start | bytes 2457600 | tf_op jit(solution)/shard_map/reduce_scatter | solution.py:375
  1583.2 135.4 %reduce-scatter.34.cloned.1.call-start = ((), (), s32[]{:S(2)}) async-start(), calls=%async_computation.47 | async-start | bytes 2457600 | tf_op jit(solution)/shard_map/reduce_scatter | solution.py:375
  1680.4 50.8 %reduce-scatter.32.cloned.1.call-start = ((), (), s32[]{:S(2)}) async-start(), calls=%async_computation.45 | async-start | bytes 2457600 | tf_op jit(solution)/shard_map/reduce_scatter | solution.py:375
  1738.8 1472.1 %reduce-scatter.44.cloned.1.call-start = ((), (), s32[]{:S(2)}) async-start(), calls=%async_computation.52 | async-start | bytes 811008
  3059.7 193.4 %reduce-scatter.46.cloned.1.call-start = ((), (), s32[]{:S(2)}) async-start(), calls=%async_computation.53 | async-start | bytes 811008
  3061.5 292.0 %reduce-scatter.40.cloned.1.call-start = ((), (), s32[]{:S(2)}) async-start(), calls=%async_computation.50 | async-start | bytes 811008 | tf_op jit(solution)/shard_map/reduce_scatter | solution.py:470
  3062.8 390.8 %reduce-scatter.38.cloned.1.call-start = ((), (), s32[]{:S(2)}) async-start(), calls=%async_computation.49 | async-start | bytes 811008 | tf_op jit(solution)/shard_map/reduce_scatter | solution.py:469
  3068.4 497.5 %reduce-scatter.42.cloned.1.call-start = ((), (), s32[]{:S(2)}) async-start(), calls=%async_computation.51 | async-start | bytes 4866048 | tf_op jit(solution)/shard_map/reduce_scatter | solution.py:474
  3076.7 631.1 %reduce-scatter.36.cloned.1.call-start = ((), (), s32[]{:S(2)}) async-start(), calls=%async_computation.48 | async-start | bytes 9732096 | tf_op jit(solution)/shard_map/reduce_scatter | solution.py:466
  (465 other events, 12321.5 us)
Sparse Core Ops, SparseCore 0:
  11.0 66.3 all-gather.17
  80.3 56.1 all-gather.19
  1163.3 22.4 all-gather.27
  1187.2 21.8 all-gather.25
  1210.5 21.8 all-gather.23
  1233.8 21.8 all-gather.21
  1258.3 30.6 reduce-scatter.25
  1292.3 30.6 reduce-scatter.23
  1326.1 30.8 reduce-scatter.21
  1359.6 30.6 reduce-scatter.19
  1432.7 19.9 all-gather.29
  1454.2 21.8 all-gather.31
  1477.6 21.8 all-gather.35
  1518.5 30.9 reduce-scatter.27
  1551.1 21.8 all-gather.33
  1583.3 31.0 reduce-scatter.29
  1639.3 31.1 reduce-scatter.33
  1691.5 31.0 reduce-scatter.31
  3059.8 93.6 reduce-scatter.43
  3158.5 94.5 reduce-scatter.45
  3258.8 94.5 reduce-scatter.39
  3359.1 94.5 reduce-scatter.37
  3459.7 106.0 reduce-scatter.41
  3573.2 134.5 reduce-scatter.35
where the time goes:
time: 3760 us; the launch traced here: 3710 us
  other arithmetic  1510 us (40%)
  local copies, waits for them, and re-layouts  805 us (21%)
  waiting for transfers between devices  596 us (16%)
  blocking collectives  464 us (12%)
  matrix products  232 us (6%)
  starting transfers between devices  66.6 us (2%)
    dynamic_update_slice x256, other arithmetic, shards(): lax.scan(advance_block, zero_state, (sub_blocks(step_time), sub_blocks(dr...  345 us
    reduce_sum x128, other arithmetic, retreat_block(): jnp.sum(weight * source_block[None], axis=1)  242 us
    reduce_sum x128, other arithmetic, advance_block(): jnp.sum(weight * drive_block[None], axis=1)  183 us
    mul x128, local copies, waits for them, and re-layouts, advance_block(): weight * drive_block[None]  153 us
    mul x128, local copies, waits for them, and re-layouts, retreat_block(): weight * source_block[None]  153 us
    reduce_scatter x1, waiting for transfers between devices, shards(): lax.psum_scatter(dense_grads[1], ('batch', 'seq'), scatter_dimension=0, t...  142 us
    reduce_sum x2, other arithmetic, shards(): jnp.sum(flow * step_time[..., None], axis=(0, 1)) * decay_rate  123 us
    reduce_scatter x1, waiting for transfers between devices, shards(): lax.psum_scatter(dense_grads[9], ('batch', 'seq'), scatter_dimension=0, t...  112 us

commit v1 on v0

v1 whole, which is shorter than its diff:
```python
import functools
import math

import jax
import jax.numpy as jnp
from jax import lax
from jax.experimental import pallas as pl
from jax.experimental.pallas import tpu as pltpu
from jax.sharding import PartitionSpec as P

DI = 1536
STATE = 16
DT_RANK = 48
CONV = 4
SEQ_MB = 1
EPSILON = 1e-05
F32 = jnp.float32
BF = jnp.bfloat16
U = 16
CB = 512
LOG2E = 1.0 / math.log(2.0)
LN2 = math.log(2.0)
HALO = 8


def end_kernel(backward, chunks, s_ref, x_ref, bt_ref, r_ref, h_ref):
    r = r_ref[...]
    width = r.shape[1]
    def chunk(c, h):
        if backward: c = chunks-1-c
        rows = pl.ds(pl.multiple_of(c*U,U),U)
        s8 = s_ref[0, rows, :]
        d8 = x_ref[0, rows, :].astype(F32)
        if not backward: d8 = d8*s8
        bt = bt_ref[0, c]
        for k in (range(U-1,-1,-1) if backward else range(U)):
            s = jnp.broadcast_to(s8[k:k+1], (STATE,width))
            d = jnp.broadcast_to(d8[k:k+1], (STATE,width))
            b = jnp.broadcast_to(bt[(STATE if backward else 0):(2*STATE if backward else STATE), k:k+1], (STATE,width))
            if backward:
                h = jnp.exp2(s*r)*(h + d*b)
            else:
                h = jnp.exp2(s*r)*h + d*b
        return h
    h_ref[0] = lax.fori_loop(0, chunks, chunk, jnp.zeros((STATE,width),F32))

def scan_end(s, x, bt, r, backward):
    S,T,C = s.shape
    cb=min(CB,C)
    row=pl.BlockSpec((1,T,cb), lambda i,j:(i,0,j))
    return pl.pallas_call(functools.partial(end_kernel, backward, T//U),
        grid=(S,C//cb),
        in_specs=[row,row,pl.BlockSpec((1,T//U,2*STATE,U),lambda i,j:(i,0,0,0)),pl.BlockSpec((STATE,cb),lambda i,j:(0,j))],
        out_specs=pl.BlockSpec((1,STATE,cb),lambda i,j:(i,0,j)),
        out_shape=jax.ShapeDtypeStruct((S,STATE,C),F32),
        compiler_params=pltpu.CompilerParams(vmem_limit_bytes=48<<20),
        cost_estimate=pl.CostEstimate(flops=6*S*T*C*STATE,bytes_accessed=8*S*T*C,transcendentals=S*T*C*STATE),
        name="scan_end_b" if backward else "scan_end_f",
    )(s,x,bt,r)

def fwd_kernel(chunks, s_ref, x_ref, bt_ref, l_ref, r_ref, h0_ref, y_ref, h_ref):
    r = r_ref[...]
    width = r.shape[1]
    def chunk(c, h):
        rows = pl.ds(pl.multiple_of(c*U,U),U)
        s8 = s_ref[0, rows, :]
        d8 = x_ref[0, rows, :].astype(F32)*s8
        bt = bt_ref[0, c]
        for k in range(U):
            s = jnp.broadcast_to(s8[k:k+1], (STATE,width))
            d = jnp.broadcast_to(d8[k:k+1], (STATE,width))
            b = jnp.broadcast_to(bt[0:STATE, k:k+1], (STATE,width))
            h = jnp.exp2(s*r)*h + d*b
            h_ref[0, pl.ds(pl.multiple_of(c*U*STATE+k*STATE,STATE),STATE), :] = h.astype(BF)
        y_ref[0, rows, :] = jnp.dot(l_ref[0, rows, :], h_ref[0, pl.ds(pl.multiple_of(c*U*STATE,U*STATE),U*STATE), :], preferred_element_type=F32)
        return h
    lax.fori_loop(0, chunks, chunk, h0_ref[0])

def scan_fwd(s, x, bt, l, r, h0):
    S,T,C = s.shape
    cb=min(CB,C)
    row=pl.BlockSpec((1,T,cb), lambda i,j:(i,0,j))
    st=pl.BlockSpec((1,STATE,cb),lambda i,j:(i,0,j))
    return pl.pallas_call(functools.partial(fwd_kernel, T//U),
        grid=(S,C//cb),
        in_specs=[row,row,pl.BlockSpec((1,T//U,2*STATE,U),lambda i,j:(i,0,0,0)),pl.BlockSpec((1,T,U*STATE),lambda i,j:(i,0,0)),pl.BlockSpec((STATE,cb),lambda i,j:(0,j)),st],
        out_specs=[row,pl.BlockSpec((1,T*STATE,cb),lambda i,j:(i,0,j))],
        out_shape=[jax.ShapeDtypeStruct((S,T,C),F32),jax.ShapeDtypeStruct((S,T*STATE,C),BF)],
        compiler_params=pltpu.CompilerParams(vmem_limit_bytes=48<<20),
        cost_estimate=pl.CostEstimate(flops=8*S*T*C*STATE,bytes_accessed=42*S*T*C,transcendentals=S*T*C*STATE),
        name="scan_fwd",
    )(s,x,bt,l,r,h0)

def bwd_kernel(chunks, s_ref, x_ref, g_ref, bt_ref, l_ref, one_ref, r_ref, h0_ref, m0_ref, h_ref,
               pull_ref, gs_ref, alog_ref, gi_ref, go_ref, lam_s, fr_s):
    r = r_ref[...]
    width = r.shape[1]
    j = pl.program_id(1)
    @pl.when(j==0)
    def _():
        gi_ref[...]=jnp.zeros_like(gi_ref)
        go_ref[...]=jnp.zeros_like(go_ref)
    def chunk(c, carry):
        c = chunks-1-c
        lam_c, alog = carry
        rows = pl.ds(pl.multiple_of(c*U,U),U)
        big = pl.ds(pl.multiple_of(c*U*STATE,U*STATE),U*STATE)
        s8 = s_ref[0, rows, :]
        g8 = g_ref[0, rows, :]
        bt = bt_ref[0, c]
        for k in range(U-1,-1,-1):
            s = jnp.broadcast_to(s8[k:k+1], (STATE,width))
            g = jnp.broadcast_to(g8[k:k+1], (STATE,width))
            cc = jnp.broadcast_to(bt[STATE:2*STATE, k:k+1], (STATE,width))
            if k:
                hp = h_ref[0, pl.ds(pl.multiple_of(c*U*STATE+(k-1)*STATE,STATE),STATE), :].astype(F32)
            else:
                hp = h_ref[0, pl.ds(pl.multiple_of(jnp.maximum(c*U*STATE-STATE,0),STATE),STATE), :].astype(F32)
                hp = jnp.where(c==0, h0_ref[0], hp)
            lam = lam_c + g*cc
            lam_c = jnp.exp2(s*r)*lam
            fr = lam_c*hp*r
            alog = alog + fr*s
            lam_s[k*STATE:(k+1)*STATE,:] = lam.astype(BF)
            fr_s[k*STATE:(k+1)*STATE,:] = fr.astype(BF)
        lam_all = lam_s[...]
        d8 = (x_ref[0, rows, :].astype(F32)*s8).astype(BF)
        pull_ref[0, rows, :] = jnp.dot(l_ref[0, rows, :], lam_all, preferred_element_type=F32)
        gs_ref[0, rows, :] = jnp.dot(one_ref[...], fr_s[...], preferred_element_type=F32)
        nt=(((1,),(1,)),((),()))
        gi_ref[0, rows, :] += lax.dot_general(d8, lam_all, nt, preferred_element_type=F32)
        go_ref[0, rows, :] += lax.dot_general(g8.astype(BF), h_ref[0, big, :], nt, preferred_element_type=F32)
        return lam_c, alog
    _, alog = lax.fori_loop(0, chunks, chunk, (m0_ref[0], jnp.zeros((STATE,width),F32)))
    alog_ref[0] = alog

def scan_bwd(s, x, g, bt, l, one, r, h0, m0, h):
    S,T,C = s.shape
    cb=min(CB,C)
    row=pl.BlockSpec((1,T,cb), lambda i,j:(i,0,j))
    st=pl.BlockSpec((1,STATE,cb),lambda i,j:(i,0,j))
    lo=pl.BlockSpec((1,T,U*STATE),lambda i,j:(i,0,0))
    return pl.pallas_call(functools.partial(bwd_kernel, T//U),
        grid=(S,C//cb),
        in_specs=[row,row,row,pl.BlockSpec((1,T//U,2*STATE,U),lambda i,j:(i,0,0,0)),lo,pl.BlockSpec((U,U*STATE),lambda i,j:(0,0)),pl.BlockSpec((STATE,cb),lambda i,j:(0,j)),st,st,pl.BlockSpec((1,T*STATE,cb),lambda i,j:(i,0,j))],
        out_specs=[row,row,st,lo,lo],
        out_shape=[jax.ShapeDtypeStruct((S,T,C),F32),jax.ShapeDtypeStruct((S,T,C),F32),jax.ShapeDtypeStruct((S,STATE,C),F32),jax.ShapeDtypeStruct((S,T,U*STATE),F32),jax.ShapeDtypeStruct((S,T,U*STATE),F32)],
        scratch_shapes=[pltpu.VMEM((U*STATE,cb),BF),pltpu.VMEM((U*STATE,cb),BF)],
        compiler_params=pltpu.CompilerParams(vmem_limit_bytes=48<<20),
        cost_estimate=pl.CostEstimate(flops=16*S*T*C*STATE,bytes_accessed=50*S*T*C,transcendentals=S*T*C*STATE),
        name="scan_bwd",
    )(s,x,g,bt,l,one,r,h0,m0,h)


def fold(z):
    seqs, span, _ = z.shape
    same = jnp.arange(span)[:, None] % U == jnp.arange(U * STATE)[None] // STATE
    return jnp.sum(jnp.where(same, z, 0).reshape(seqs, span, U, STATE), 2)


def spread_rows(m):
    same = jnp.arange(m.shape[1])[:, None] % U == jnp.arange(U * STATE)[None] // STATE
    return jnp.where(same, jnp.tile(m, (1, 1, U)), 0).astype(BF)


def bits_of(axis):
    return lax.axis_size(axis).bit_length() - 1


def my_bit(axis, k):
    return (lax.axis_index(axis) >> k) & 1


def swap(x, axis, k):
    count = lax.axis_size(axis)
    return lax.ppermute(x, axis, [(i, i ^ (1 << k)) for i in range(count)])


def shift(x, axis, distance):
    count = lax.axis_size(axis)
    return lax.ppermute(
        x, axis, [(i, i + distance) for i in range(count) if 0 <= i + distance < count]
    )


def mesh_bits():
    return [("batch", k) for k in reversed(range(bits_of("batch")))] + [
        ("seq", k) for k in reversed(range(bits_of("seq")))
    ]


def ordered(which):
    bits = mesh_bits()
    core = ("seq", 0)
    y_bits = [b for b in bits if b[0] == "seq" and b != core]
    x_bits = [("batch", 0)]
    z_bits = [b for b in bits if b[0] == "batch" and b[1] > 0]
    parts = {
        0: z_bits + x_bits + y_bits,
        1: y_bits + z_bits + x_bits,
        2: x_bits + y_bits + z_bits,
    }[which]
    return parts + [core]


def gather_all(x, which):
    bits = mesh_bits()
    out = x.reshape((1,) * len(bits) + x.shape)
    for axis, k in ordered(which):
        place = bits.index((axis, k))
        other = swap(out, axis, k)
        high = my_bit(axis, k) == 1
        out = jnp.concatenate(
            [jnp.where(high, other, out), jnp.where(high, out, other)], axis=place
        )
    return out.reshape((-1,) + x.shape[1:])


def scatter_sum(x, which, kind):
    bits = mesh_bits()
    rows = x.shape[0] >> len(bits)
    out = x.reshape((2,) * len(bits) + (rows,) + x.shape[1:])
    for axis, k in reversed(ordered(which)):
        place = bits.index((axis, k))
        bit = my_bit(axis, k)
        mine = lax.dynamic_index_in_dim(out, bit, place, True)
        theirs = lax.dynamic_index_in_dim(out, 1 - bit, place, True).astype(kind)
        out = mine + swap(theirs, axis, k).astype(F32)
    return out.reshape((rows,) + x.shape[1:])


def gather_seq(x):
    parts = [x]
    for k in reversed(range(bits_of("seq"))):
        parts = parts + [swap(p, "seq", k) for p in parts]
    count = len(parts)
    order = []
    for k in reversed(range(bits_of("seq"))):
        order = (order or [0]) + [o ^ (1 << k) for o in (order or [0])]
    return [parts[order.index(j)] for j in range(count)]


def scatter_seq(parts):
    parts = dict(enumerate(parts))
    for k in range(bits_of("seq")):
        bit = 1 << k
        moved = {j ^ bit: swap(p.astype(BF), "seq", k) for j, p in parts.items() if j & bit}
        parts = {j: p + moved[j].astype(F32) for j, p in parts.items() if not j & bit}
    return parts[0]


def prefix(total, state, rate, backward):
    before = jnp.zeros_like(state)
    before_total = jnp.zeros_like(total)
    stages = bits_of("seq")
    for k in range(stages):
        other_total = swap(total, "seq", k)
        other = swap(state.astype(BF), "seq", k).astype(F32)
        first = my_bit("seq", k) == (0 if backward else 1)
        before = jnp.where(
            first, before + jnp.exp2(before_total[:, None, :] * rate) * other, before
        )
        before_total = jnp.where(first, before_total + other_total, before_total)
        if k + 1 < stages:
            near = jnp.where(first, state, other)
            far = jnp.where(first, other, state)
            near_total = jnp.where(first, total, other_total)
            state = near + jnp.exp2(near_total[:, None, :] * rate) * far
            total = total + other_total
    return before


def mm(left, right, dims):
    return lax.dot_general(left, right, (dims, ((), ())), preferred_element_type=F32)


def nn(left, right):
    return mm(left, right, ((left.ndim - 1,), (0,)))


def nt(left, right):
    return mm(left, right, ((left.ndim - 1,), (1,)))


def tn(left, right):
    lead = tuple(range(left.ndim - 1))
    return mm(left, right, (lead, lead))


def silu_slope(v):
    s = jax.nn.sigmoid(v)
    return s * (1.0 + v * (1.0 - s))


def norm_back(grad_norm, x, scale):
    return scale * grad_norm - x * scale**3 * jnp.mean(grad_norm * x, axis=-1, keepdims=True)


def gelu_tanh(v):
    return jax.nn.gelu(v, approximate=True)


def rms(x):
    return lax.rsqrt(jnp.mean(x * x, axis=-1, keepdims=True) + EPSILON)


def pad_cols(x, width):
    return jnp.pad(x, ((0, 0), (0, width - x.shape[1])))


def shards(
    tokens,
    cotangent,
    lengths,
    order,
    expert_route,
    slot_index,
    norm_gain,
    in_proj,
    conv_weight,
    conv_bias,
    x_proj,
    dt_proj,
    dt_bias,
    a_log,
    skip_gain,
    out_proj,
    moe_gain,
    router,
    expert_in,
    expert_out,
):
    seqs, span, width = tokens.shape
    batch = lax.axis_size("batch")
    experts = expert_in.shape[0] * batch
    capacity = max(2, (5 * SEQ_MB * span + 4 * experts - 1) // (4 * experts))
    maps = DT_RANK + 2 * STATE

    chan = jnp.concatenate(
        [
            x_proj,
            dt_proj,
            a_log,
            conv_weight,
            conv_bias[:, None],
            dt_bias[:, None],
            skip_gain[:, None],
        ],
        axis=1,
    )
    feat = jnp.concatenate([norm_gain[:, None], moe_gain[:, None], router], axis=1)
    feat = gather_all(pad_cols(feat, 128), 1)
    w_conv_in = gather_all(in_proj[:, :DI], 0)
    chan = gather_all(pad_cols(chan, 256), 2)
    w_gate_in = gather_all(in_proj[:, DI:], 1)
    w_back = gather_all(out_proj, 2)
    gain_one = feat[:, 0].astype(F32)
    gain_two = feat[:, 1].astype(F32)
    router_weight = feat[:, 2 : 2 + experts]
    w_proj = chan[:, :maps]
    at = maps + DT_RANK
    w_step = chan[:, maps:at]
    rate = -jnp.exp(chan[:, at : at + STATE].astype(F32)).T * LOG2E
    at = at + STATE
    taps = chan[:, at : at + CONV].astype(F32).T
    bias_conv = chan[:, at + CONV].astype(F32)
    bias_step = chan[:, at + CONV + 1].astype(F32)
    skip = chan[:, at + CONV + 2].astype(F32)

    halo = shift(tokens[:, span - HALO :, :], "seq", 1)
    tail = jnp.arange(HALO)[:, None] >= HALO - (CONV - 1)
    halo = jnp.where(tail, halo, 0)

    first_weight = jnp.concatenate(gather_seq(expert_in[0]), axis=1)
    second_weight = jnp.concatenate(gather_seq(expert_out[0]), axis=0)

    positions = lax.axis_index("seq") * span + jnp.arange(span, dtype=jnp.int32)
    row_length = jnp.sum(
        jnp.where(
            order[:, None] == jnp.arange(lengths.shape[0], dtype=jnp.int32)[None, :],
            lengths[None, :],
            0,
        ),
        axis=1,
    )
    keep = (positions[None, :] < row_length[:, None]).astype(F32)
    grad_out = cotangent.astype(F32) * keep[..., None]

    block = tokens.astype(F32)
    scale_one = rms(block)
    ext = jnp.concatenate([halo, tokens], axis=1).astype(F32)
    normed_ext = (ext * rms(ext) * gain_one).astype(BF)
    normed = normed_ext[:, HALO:]
    conv_ext = nn(normed_ext, w_conv_in)
    gate_in = nn(normed, w_gate_in)
    lo = HALO - (CONV - 1)
    conv_out = bias_conv + sum(conv_ext[:, lo + k : lo + k + span, :] * taps[k] for k in range(CONV))
    act = jax.nn.silu(conv_out).astype(BF)
    projected = nn(act, w_proj)
    delta = projected[..., :DT_RANK].astype(BF)
    input_map = projected[..., DT_RANK : DT_RANK + STATE]
    output_map = projected[..., DT_RANK + STATE :]
    step_arg = nt(delta, w_step) + bias_step
    step = jax.nn.softplus(step_arg)
    total = jnp.sum(step, axis=1)
    both = jnp.swapaxes(projected[..., DT_RANK:].reshape(seqs, span // U, U, 2 * STATE), 2, 3)
    in_rows = spread_rows(input_map)
    out_rows = spread_rows(output_map)
    ones = (jnp.arange(U)[:, None] == jnp.arange(U * STATE)[None] // STATE).astype(BF)
    end = scan_end(step, act, both, rate, False)
    init = prefix(total, end, rate, False)
    y, states = scan_fwd(step, act, both, out_rows, rate, init)
    actf = act.astype(F32)
    mix = y + skip * actf
    gate_act = jax.nn.silu(gate_in)
    gated = (mix * gate_act).astype(BF)
    mixed = block + nn(gated, w_back)

    scale_two = rms(mixed)
    routed = (mixed * scale_two * gain_two).astype(BF)
    probs = jax.nn.softmax(nn(routed, router_weight), axis=-1)
    kept = slot_index >= 0
    target = jnp.where(kept, expert_route * capacity + slot_index, -1)
    slots = jnp.arange(experts * capacity, dtype=jnp.int32)
    selector = (target[..., None] == slots).astype(BF)
    chosen = jnp.logical_and(
        expert_route[..., None] == jnp.arange(experts, dtype=jnp.int32), kept[..., None]
    )
    gate = jnp.sum(jnp.where(chosen, probs, 0.0), axis=-1)[..., None]
    grad_value = (gate * grad_out).astype(BF)
    packed = jnp.concatenate([routed, grad_value], axis=-1)
    send = jnp.einsum("stc,std->scd", selector, packed, preferred_element_type=F32).astype(BF)
    send = jnp.swapaxes(send.reshape(seqs, batch, capacity, 2 * width), 0, 1)
    arrived = lax.all_to_all(send, "batch", split_axis=0, concat_axis=0, tiled=True)
    arrived = arrived.reshape(batch * seqs * capacity, 2 * width)

    rows_in = arrived[:, :width]
    grad_rows = arrived[:, width:]
    hidden = nn(rows_in, first_weight)
    value, gelu_back = jax.vjp(gelu_tanh, hidden)
    value = value.astype(BF)
    rows_out = nn(value, second_weight).astype(BF)
    grad_hidden = gelu_back(nt(grad_rows, second_weight))[0].astype(BF)
    grad_in = nt(grad_hidden, first_weight).astype(BF)
    back = jnp.concatenate([rows_out, grad_in], axis=-1)
    back = back.reshape(batch, seqs, capacity, 2 * width)
    back = lax.all_to_all(back, "batch", split_axis=0, concat_axis=0, tiled=True)
    back = jnp.swapaxes(back, 0, 1).reshape(seqs, experts * capacity, 2 * width)
    quarter = expert_in.shape[2]
    pieces = first_weight.shape[1] // quarter
    grad_first = tn(rows_in, grad_hidden)
    grad_second = tn(value, grad_rows)
    grad_first = scatter_seq([grad_first[:, j * quarter : (j + 1) * quarter] for j in range(pieces)])
    grad_second = scatter_seq([grad_second[j * quarter : (j + 1) * quarter] for j in range(pieces)])

    picked = jnp.einsum("stc,scd->std", selector, back, preferred_element_type=F32)
    expert_tok = picked[..., :width]
    activations = (mixed + gate * expert_tok).astype(BF)

    grad_gate = jnp.sum(expert_tok * grad_out, axis=-1, keepdims=True)
    grad_prob = jnp.where(chosen, grad_gate, 0.0)
    grad_logits = (
        probs * (grad_prob - jnp.sum(probs * grad_prob, axis=-1, keepdims=True))
    ).astype(BF)
    g_router = tn(routed, grad_logits)
    grad_routed = picked[..., width:] + nt(grad_logits, router_weight)
    g_gain_two = jnp.sum(grad_routed * mixed * scale_two, axis=(0, 1))
    grad_mixed = grad_out + norm_back(grad_routed * gain_two, mixed, scale_two)
    grad_branch = grad_mixed.astype(BF)

    grad_gated = nt(grad_branch, w_back)
    grad_mix = grad_gated * gate_act
    grad_gate_in = (grad_gated * mix * silu_slope(gate_in)).astype(BF)
    behind = scan_end(step, grad_mix, both, rate, True)
    after = prefix(total, behind, rate, True)
    g_back = scatter_sum(tn(gated, grad_branch), 2, BF)
    g_gate_half = scatter_sum(tn(normed, grad_gate_in), 1, BF)
    g_skip = jnp.sum(grad_mix * actf, axis=(0, 1))
    pull, grad_rate, g_log, grad_in_map, grad_out_map = scan_bwd(
        step, act, grad_mix, both, in_rows, ones, rate, init, after, states
    )
    g_log = jnp.sum(g_log, axis=0).T * LN2
    grad_arg = (grad_rate * LN2 + actf * pull) * jax.nn.sigmoid(step_arg)
    g_step_bias = jnp.sum(grad_arg, axis=(0, 1))
    grad_pre = grad_arg.astype(BF)
    g_step = tn(grad_pre, delta)
    grad_proj = jnp.concatenate(
        [nn(grad_pre, w_step), fold(grad_in_map), fold(grad_out_map)], axis=-1
    ).astype(BF)
    g_proj = tn(act, grad_proj)
    grad_act = skip * grad_mix + step * pull + nt(grad_proj, w_proj)
    grad_conv = grad_act * silu_slope(conv_out)
    g_conv_bias = jnp.sum(grad_conv, axis=(0, 1))
    g_taps = jnp.stack(
        [
            jnp.sum(grad_conv * conv_ext[:, lo + k : lo + k + span, :], axis=(0, 1))
            for k in range(CONV)
        ],
        axis=-1,
    )
    rim = shift(grad_conv[:, :HALO, :], "seq", -1)
    longer = jnp.concatenate([grad_conv, rim], axis=1)
    grad_conv_in = sum(
        longer[:, CONV - 1 - k : CONV - 1 - k + span, :] * taps[k] for k in range(CONV)
    ).astype(BF)
    g_conv_half = scatter_sum(tn(normed, grad_conv_in), 0, BF)
    grad_normed = nt(grad_conv_in, w_conv_in) + nt(grad_gate_in, w_gate_in)
    g_gain_one = jnp.sum(grad_normed * block * scale_one, axis=(0, 1))
    input_grad = grad_mixed + norm_back(grad_normed * gain_one, block, scale_one)

    g_chan = jnp.concatenate(
        [
            g_proj,
            g_step,
            g_log,
            g_taps,
            g_conv_bias[:, None],
            g_step_bias[:, None],
            g_skip[:, None],
        ],
        axis=1,
    )
    g_chan = scatter_sum(pad_cols(g_chan, 256), 2, F32)
    g_feat = jnp.concatenate([g_gain_one[:, None], g_gain_two[:, None], g_router], axis=1)
    g_feat = scatter_sum(pad_cols(g_feat, 128), 1, F32)
    at = maps + DT_RANK
    return (
        activations,
        input_grad,
        g_feat[:, 0],
        jnp.concatenate([g_conv_half, g_gate_half], axis=1),
        g_chan[:, at + STATE : at + STATE + CONV],
        g_chan[:, at + STATE + CONV],
        g_chan[:, :maps],
        g_chan[:, maps:at],
        g_chan[:, at + STATE + CONV + 1],
        g_chan[:, at : at + STATE],
        g_chan[:, at + STATE + CONV + 2],
        g_back,
        g_feat[:, 1],
        g_feat[:, 2 : 2 + experts],
        grad_first[None],
        grad_second[None],
    )


def solution(mesh):
    return jax.shard_map(
        shards,
        mesh=mesh,
        in_specs=(
            P("batch", "seq", None),
            P("batch", "seq", None),
            P(),
            P("batch"),
            P("batch", "seq"),
            P("batch", "seq"),
            P(("batch", "seq")),
            P(("batch", "seq"), None),
            P(("batch", "seq"), None),
            P(("batch", "seq")),
            P(("batch", "seq"), None),
            P(("batch", "seq"), None),
            P(("batch", "seq")),
            P(("batch", "seq"), None),
            P(("batch", "seq")),
            P(("batch", "seq"), None),
            P(("batch", "seq")),
            P(("batch", "seq"), None),
            P("batch", None, "seq"),
            P("batch", "seq", None),
        ),
        out_specs=(
            P("batch", "seq", None),
            P("batch", "seq", None),
            P(("batch", "seq")),
            P(("batch", "seq"), None),
            P(("batch", "seq"), None),
            P(("batch", "seq")),
            P(("batch", "seq"), None),
            P(("batch", "seq"), None),
            P(("batch", "seq")),
            P(("batch", "seq"), None),
            P(("batch", "seq")),
            P(("batch", "seq"), None),
            P(("batch", "seq")),
            P(("batch", "seq"), None),
            P("batch", None, "seq"),
            P("batch", "seq", None),
        ),
        check_vma=False,
    )
```

time: 3760 us -> 886 us (0.24)
  other arithmetic: 1510 us -> 111 us
  local copies, waits for them, and re-layouts: 805 us -> 87.8 us
  blocking collectives: 464 us -> 0 us
  waiting for transfers between devices: 596 us -> 214 us
  Pallas kernels: 0 us -> 219 us
  matrix products: 232 us -> 172 us
    reduce_sum x275 -> x10, other arithmetic: 665 us -> 39 us  [the longest x1 20.4 us: shards(): jnp.sum(grad_conv * conv_ext[:, lo + k:lo + k + span, :], axis=(0, 1))]
    reduce_scatter x12 -> x0, waiting for transfers between devices: 515 us -> none  [the longest x1 142 us: shards(): lax.psum_scatter(dense_grads[1], ('batch', 'seq'), scatter_dimension=0, t...]
    dynamic_update_slice x256 -> x0, other arithmetic: 345 us -> none  [shards(): lax.scan(advance_block, zero_state, (sub_blocks(step_time), sub_blocks(dr...]
    mul x256 -> x0, local copies, waits for them, and re-layouts: 305 us -> none  [the longest x128 153 us: advance_block(): weight * drive_block[None]]
    all_gather x17 -> x0, blocking collectives: 275 us -> none  [the longest x12 74.6 us: entering(): lax.all_gather(a.astype(kind), axis)]
    pallas_call x0 -> x4, Pallas kernels: none -> 219 us  [the longest x1 102 us: scan_bwd(): pl.pallas_call(functools.partial(bwd_kernel, T // U), grid=(S, C // cb),...]
    another operation x176 -> x8, local copies, waits for them, and re-layouts: 202 us -> 9.65 us  [the longest x4 7.25 us: spread_rows(): return jnp.where(same, jnp.tile(m, (1, 1, U)), 0).astype(BF)]
    ppermute x8 -> x69, waiting for transfers between devices: 0.02 us -> 179 us  [the longest x67 179 us: swap(): return lax.ppermute(x, axis, [(i, i ^ 1 << k) for i in range(count)])]
where the time goes in v1:
time: 886 us; the launch traced here: 876 us
  Pallas kernels  219 us (25%)
  waiting for transfers between devices  214 us (24%)
  matrix products  172 us (19%)
  other arithmetic  111 us (13%)
  local copies, waits for them, and re-layouts  87.8 us (10%)
  starting transfers between devices  69.2 us (8%)
    ppermute x67, waiting for transfers between devices, swap(): return lax.ppermute(x, axis, [(i, i ^ 1 << k) for i in range(count)])  179 us
    dot_general x24, matrix products, mm(): lax.dot_general(left, right, (dims, ((), ())), preferred_element_type=F32)  169 us
    pallas_call x1, Pallas kernels, scan_bwd(): pl.pallas_call(functools.partial(bwd_kernel, T // U), grid=(S, C // cb),...  102 us
    pallas_call x1, Pallas kernels, scan_fwd(): pl.pallas_call(functools.partial(fwd_kernel, T // U), grid=(S, C // cb),...  61.6 us
    ppermute x67, starting transfers between devices, swap(): return lax.ppermute(x, axis, [(i, i ^ 1 << k) for i in range(count)])  57.3 us
    pallas_call x2, Pallas kernels, scan_end(): pl.pallas_call(functools.partial(end_kernel, backward, T // U), grid=(S,...  55.1 us
    all_to_all x1, waiting for transfers between devices, shards(): lax.all_to_all(send, 'batch', split_axis=0, concat_axis=0, tiled=True)  34.5 us
    unnamed x227, local copies, waits for them, and re-layouts  22.9 us
  transfers between devices with their start and end apart: 71, of which 24 were waited for; matrix products, arithmetic and copies ran while one was open for 28% of the time, Pallas kernels for 15%

profile of v1, /device:TPU:0, one launch (start us, length us, event | category | flops | bytes accessed | tf_op | source)
XLA Modules:
  0.0 875.9 jit_solution(9951018506523390455)
XLA Ops:
  94.2 9.1 %fusion.107 = (f32[4,1536]{1,0:T(4,128)}, f32[4,256,1536]{2,1,0:T(8,128)}, f32[4,256,1536]{2,1,0:T(8,128)}) fusion(f32[1536]{0:T(1024)S(1)} %get-tuple-element.104, bf16[1536,256]{1,0:T(8,128)(2,1)S(1)} %bitcast.152, f32[4,256,80]{1,2,0:T(8,128)S(1)} %fusion.78), kind=kOutput, calls=%fused_computation.354 | convolution fusion | flops 163571712 | bytes 13107200 | tf_op jit(solution)/shard_map/dot_general | solution.py:274
  121.1 28.6 %scan_end_f.1 = f32[4,16,1536]{2,1,0:T(8,128)S(1)} custom-call(f32[4,256,1536]{2,1,0:T(8,128)} %get-tuple-element.122.s_ref, bf16[4,256,1536]{2,1,0:T(8,128)(2,1)S(1)} %get-tuple-element.123.x_ref, f32[4,16,32,16]{3,2,1,0:T(8,128)S(1)} %bitcast.143, f32[16,1536]{1,0:T(8,128)S(1)} %get-tuple-element.188.r_ref), custom_call_target="tpu_custom_call" | custom-call | flops 150994944 | bytes 12582912 | tf_op jit(solution)/shard_map/scan_end_f/pallas_call | solution.py:51
  159.0 61.6 %scan_fwd.1 = (f32[4,256,1536]{2,1,0:T(8,128)}, bf16[4,4096,1536]{2,1,0:T(8,128)(2,1)}) custom-call(f32[4,256,1536]{2,1,0:T(8,128)} %get-tuple-element.122.s_ref, bf16[4,256,1536]{2,1,0:T(8,128)(2,1)S(1)} %get-tuple-element.123.x_ref, f32[4,16,32,16]{3,2,1,0:T(8,128)S(1)} %bitcast.144, bf16[4,256,256]{2,1,0:T(8,128)(2,1)S(1)} %get-tuple-element.184.l_ref, ...), custom_call_target="tpu_custom_call" | custom-call | flops 201326592 | bytes 66060288 | tf_op jit(solution)/shard_map/scan_fwd/pallas_call | solution.py:84
  220.7 7.9 multiply_convert_fusion.2
  244.8 27.1 %collective-permute-done.30 = bf16[768,768]{1,0:T(8,128)(2,1)S(1)} collective-permute-done((bf16[768,768]{1,0:T(8,128)(2,1)}, bf16[768,768]{1,0:T(8,128)(2,1)S(1)}, u32[]{:S(2)}, u32[]{:S(2)}) %collective-permute-start.30) | collective-permute-done | bytes 1179680 | tf_op jit(solution)/shard_map/ppermute | solution.py:176
  273.4 22.0 %collective-permute-done.33 = bf16[768,768]{1,0:T(8,128)(2,1)} collective-permute-done((bf16[768,768]{1,0:T(8,128)(2,1)}, bf16[768,768]{1,0:T(8,128)(2,1)}, u32[]{:S(2)}, u32[]{:S(2)}) %collective-permute-start.33) | collective-permute-done | bytes 1179680 | tf_op jit(solution)/shard_map/ppermute | solution.py:176
  295.4 34.5 %all-to-all-done = bf16[8,4,40,1536]{3,2,1,0:T(8,128)(2,1)} async-done(((bf16[8,4,40,1536]{3,2,1,0:T(8,128)(2,1)}), bf16[8,4,40,1536]{3,2,1,0:T(8,128)(2,1)}, u32[]{:S(2)}, u32[]{:S(2)}) %all-to-all-start) | async-done | bytes 3932192 | tf_op jit(solution)/shard_map/all_to_all | solution.py:434
  329.9 14.6 %fusion.46 = f32[1280,3072]{1,0:T(8,128)} fusion(bf16[1280,1536]{1,0:T(8,128)(2,1)} %bitcast.29, bf16[768,768]{1,0:T(8,128)(2,1)} %collective-permute-done.31, bf16[768,768]{1,0:T(8,128)(2,1)} %copy-done.103, bf16[768,768]{1,0:T(8,128)(2,1)} %collective-permute-done.29, bf16[768,768]{1,0:T(8,128)(2,1)} %bitcast.196), kind=kOutput, calls=%fused_computation.106 | convolution fusion | flops 6058672128 | bytes 22413312 | tf_op jit(solution)/shard_map/dot_general | solution.py:274
  344.5 23.3 %fusion.7 = bf16[1280,3072]{1,0:T(8,128)(2,1)} fusion(f32[1280,3072]{1,0:T(8,128)} %fusion.46, bf16[1280,1536]{1,0:T(8,128)(2,1)} %bitcast.29, bf16[768,768]{1,0:T(8,128)(2,1)} %collective-permute-done.34, bf16[768,768]{1,0:T(8,128)(2,1)} %collective-permute-done.33, bf16[768,768]{1,0:T(8,128)(2,1)} %collective-permute-done.32, bf16[768,768]{1,0:T(8,128)(2,1)} %bitcast.192), kind=kOutput, calls=%fused_computation.10 | convolution fusion | flops 6137315328 | bytes 30277632 | tf_op jit(solution)/shard_map/dot_general | solution.py:274
  367.8 15.4 %convolution_convert_fusion.2 = bf16[1280,768]{0,1:T(8,128)(2,1)} fusion(bf16[768,768]{1,0:T(8,128)(2,1)} %collective-permute-done.34, bf16[768,768]{1,0:T(8,128)(2,1)} %collective-permute-done.33, bf16[768,768]{1,0:T(8,128)(2,1)} %collective-permute-done.32, bf16[768,768]{1,0:T(8,128)(2,1)} %bitcast.193, f32[1280,3072]{1,0:T(8,128)} %fusion.46), kind=kOutput, calls=%fused_computation.56 | convolution fusion | flops 6095044608 | bytes 22413312 | tf_op jit(solution)/shard_map/dot_general | solution.py:274
  383.3 10.6 %convolution_convert_fusion.1 = bf16[1280,768]{0,1:T(8,128)(2,1)S(1)} fusion(bf16[1280,3072]{1,0:T(8,128)(2,1)} %fusion.7, bf16[768,768]{1,0:T(8,128)(2,1)} %collective-permute-done.31, bf16[768,768]{1,0:T(8,128)(2,1)} %copy-done.103, bf16[768,768]{1,0:T(8,128)(2,1)} %collective-permute-done.29, bf16[768,768]{1,0:T(8,128)(2,1)} %bitcast.197), kind=kOutput, calls=%fused_computation.55 | convolution fusion | flops 6059655168 | bytes 14548992 | tf_op jit(solution)/shard_map/dot_general | solution.py:274
  407.2 9.4 %fusion.112 = (bf16[768,3072]{1,0:T(8,128)(2,1)S(1)}, f32[768,3072]{1,0:T(8,128)S(1)}) fusion(bf16[1280,3072]{1,0:T(8,128)(2,1)} %fusion.7, bf16[1280,1536]{1,0:T(8,128)(2,1)} %bitcast.29), kind=kOutput, calls=%fused_computation.359 | convolution fusion | flops 6042157056 | bytes 23986176 | tf_op jit(solution)/shard_map/dot_general | solution.py:274
  418.3 17.3 %fusion.113 = (bf16[3072,768]{1,0:T(8,128)(2,1)S(1)}, f32[3072,768]{1,0:T(8,128)}) fusion(bf16[1280,1536]{1,0:T(8,128)(2,1)} %bitcast.29, f32[1280,3072]{1,0:T(8,128)} %fusion.46), kind=kOutput, calls=%fused_computation.360 | convolution fusion | flops 6077546496 | bytes 31850496 | tf_op jit(solution)/shard_map/dot_general | solution.py:274
  448.6 20.5 %collective-permute-done.65 = bf16[768,768]{1,0:T(8,128)(2,1)} collective-permute-done((bf16[768,768]{1,0:T(8,128)(2,1)}, bf16[768,768]{1,0:T(8,128)(2,1)}, u32[]{:S(2)}, u32[]{:S(2)}) %collective-permute-start.65) | collective-permute-done | bytes 1179680 | tf_op jit(solution)/shard_map/ppermute | solution.py:176
  473.2 20.3 %collective-permute-done.68 = bf16[768,768]{1,0:T(8,128)(2,1)} collective-permute-done((bf16[768,768]{1,0:T(8,128)(2,1)}, bf16[768,768]{1,0:T(8,128)(2,1)}, u32[]{:S(2)}, u32[]{:S(2)}) %collective-permute-start.68) | collective-permute-done | bytes 1179680 | tf_op jit(solution)/shard_map/ppermute | solution.py:176
  516.3 10.1 %fusion.19 = (f32[1536]{0:T(1024)S(1)}, f32[4,256,1536]{2,1,0:T(8,128)}, bf16[4,256,1536]{2,1,0:T(8,128)(2,1)S(1)}) fusion(bf16[4,256,1536]{2,1,0:T(8,128)(2,1)S(1)} %copy-done.1, f32[4,256,1536]{2,1,0:T(8,128)} %get-tuple-element.205, f32[4,256,1536]{2,1,0:T(8,128)} %get-tuple-element.23, f32[1536]{0:T(1024)S(1)} %copy-done.100, ...), kind=kOutput, calls=%fused_computation.28 | convolution fusion | flops 2443442688 | bytes 30683136 | tf_op jit(solution)/shard_map/dot_general | solution.py:274
  537.8 26.5 %scan_end_b.1 = f32[4,16,1536]{2,1,0:T(8,128)S(1)} custom-call(f32[4,256,1536]{2,1,0:T(8,128)} %get-tuple-element.122.s_ref, f32[4,256,1536]{2,1,0:T(8,128)} %get-tuple-element.118.x_ref.g_ref, f32[4,16,32,16]{3,2,1,0:T(8,128)S(1)} %bitcast.145, f32[16,1536]{1,0:T(8,128)S(1)} %get-tuple-element.188.r_ref), custom_call_target="tpu_custom_call" | custom-call | flops 150994944 | bytes 12582912 | tf_op jit(solution)/shard_map/scan_end_b/pallas_call | solution.py:51
  576.6 102.5 %scan_bwd.1 = (f32[4,256,1536]{2,1,0:T(8,128)}, f32[4,256,1536]{2,1,0:T(8,128)}, f32[4,16,1536]{2,1,0:T(8,128)S(1)}, f32[4,256,256]{2,1,0:T(8,128)S(1)}, f32[4,256,256]{2,1,0:T(8,128)S(1)}) custom-call(f32[4,256,1536]{2,1,0:T(8,128)} %get-tuple-element.122.s_ref, bf16[4,256,1536]{2,1,0:T(8,128)(2,1)} %copy-done, ...), custom_call_target="tpu_custom_call" | custom-call | flops 402653184 | bytes 78643200 | tf_op jit(solution)/shard_map/scan_bwd/pallas_call | solution.py:143
  679.1 8.5 fusion.105
  701.3 11.2 %multiply_multiply_fusion.2 = f32[4,256,1536]{2,1,0:T(8,128)S(1)} fusion(f32[4,256,1536]{2,1,0:T(8,128)} %get-tuple-element.124, f32[4,256,1536]{2,1,0:T(8,128)} %get-tuple-element.122.s_ref, f32[4,256,1536]{2,1,0:T(8,128)} %get-tuple-element.25, f32[4,256,1536]{2,1,0:T(8,128)} %get-tuple-element.118.x_ref.g_ref, f32[1536]{0:T(1024)S(1)} %copy-done.101, ...), kind=kOutput, calls=%fused_computation.36 | convolution fusion | flops 271024128 | bytes 32020480 | tf_op jit(solution)/shard_map/dot_general | solution.py:274
  722.5 20.4 %multiply_reduce_fusion = (f32[1536]{0:T(1024)}, f32[1536]{0:T(1024)}, f32[1536]{0:T(1024)}, f32[1536]{0:T(1024)}, f32[1536]{0:T(1024)}, /*index=5*/bf16[4,256,1536]{2,1,0:T(8,128)(2,1)S(1)}) fusion(f32[4,256,1536]{2,1,0:T(8,128)} %copy-done.34, f32[4,264,1536]{2,1,0:T(8,128)} %copy-done.11, f32[1536]{0:T(1024)S(1)} %copy-done.74, f32[1536]{0:T(1024)S(1)} %copy-done.76, ...), kind=kLoop, calls=%fused_computation.31 | loop fusion | flops 31449600 | bytes 34854912 | tf_op jit(solution)/shard_map/reduce_sum | solution.py:496
  796.8 17.1 %collective-permute-done.54 = f32[2,1,2,2,1,48,256]{6,5,4,3,2,1,0:T(8,128)S(1)} collective-permute-done((f32[2,1,2,2,1,48,256]{6,5,4,3,2,1,0:T(8,128)S(1)}, f32[2,1,2,2,1,48,256]{6,5,4,3,2,1,0:T(8,128)S(1)}, u32[]{:S(2)}, u32[]{:S(2)}) %collective-permute-start.54) | collective-permute-done | bytes 393248 | tf_op jit(solution)/shard_map/ppermute | solution.py:176
  816.5 7.6 collective-permute-done.55
  830.7 11.5 %collective-permute-done.60 = bf16[1,1,2,2,1,48,768]{6,5,4,3,2,1,0:T(8,128)(2,1)S(1)} collective-permute-done((bf16[1,1,2,2,1,48,768]{6,5,4,3,2,1,0:T(8,128)(2,1)S(1)}, bf16[1,1,2,2,1,48,768]{6,5,4,3,2,1,0:T(8,128)(2,1)S(1)}, u32[]{:S(2)}, u32[]{:S(2)}) %collective-permute-start.60) | collective-permute-done | bytes 294944 | tf_op jit(solution)/shard_map/ppermute | solution.py:176
  (575 shorter events, 335.4 us)
Async XLA Ops:
  5.4 23.3 %collective-permute-start = (bf16[1,1,1,1,1,48,256]{6,5,4,3,2,1,0:T(8,128)(2,1)S(1)}, bf16[1,1,1,1,1,48,256]{6,5,4,3,2,1,0:T(8,128)(2,1)S(1)}, u32[]{:S(2)}, u32[]{:S(2)}) collective-permute-start(bf16[1,1,1,1,1,48,256]{6,5,4,3,2,1,0:T(8,128)(2,1)S(1)} %pad_bitcast_fusion), channel_id=1, source_target_pairs={{0,4},{4,0},{8,12},{12,8},{16,20},{20,16},{24,28},{28,24},{1,5},{5... | collective-permute-start | bytes 73736 | tf_op jit(solution)/shard_map/ppermute | solution.py:176
  15.3 22.1 %collective-permute-start.19 = (bf16[1,1,1,1,1,24,1536]{6,5,4,3,2,1,0:T(8,128)(2,1)S(1)}, bf16[1,1,1,1,1,24,1536]{6,5,4,3,2,1,0:T(8,128)(2,1)S(1)}, u32[]{:S(2)}, u32[]{:S(2)}) collective-permute-start(bf16[1,1,1,1,1,24,1536]{6,5,4,3,2,1,0:T(8,128)(2,1)S(1)} %get-tuple-element.175), channel_id=1, source_target_pairs={{0,2},{1,3},{2,0},{3,1},{4,6},{5,7},{6,4},{7,5},{8,10},{9,11},{10,... | collective-permute-start | bytes 221192 | tf_op jit(solution)/shard_map/ppermute | solution.py:176
  16.5 20.9 %collective-permute-start.11 = (bf16[1,1,1,1,1,24,1536]{6,5,4,3,2,1,0:T(8,128)(2,1)S(1)}, bf16[1,1,1,1,1,24,1536]{6,5,4,3,2,1,0:T(8,128)(2,1)S(1)}, u32[]{:S(2)}, u32[]{:S(2)}) collective-permute-start(bf16[1,1,1,1,1,24,1536]{6,5,4,3,2,1,0:T(8,128)(2,1)S(1)} %get-tuple-element.176), channel_id=1, source_target_pairs={{0,16},{4,20},{8,24},{12,28},{16,0},{20,4},{24,8},{28,12},{1,17},{... | collective-permute-start | bytes 221192 | tf_op jit(solution)/shard_map/ppermute | solution.py:176
  81.2 22.4 %collective-permute-start.23 = (bf16[2,2,2,2,1,24,1536]{6,5,4,3,2,1,0:T(8,128)(2,1)}, bf16[2,2,2,2,1,24,1536]{6,5,4,3,2,1,0:T(8,128)(2,1)S(1)}, u32[]{:S(2)}, u32[]{:S(2)}) collective-permute-start(bf16[2,2,2,2,1,24,1536]{6,5,4,3,2,1,0:T(8,128)(2,1)} %pad_maximum_fusion.9), channel_id=1, source_target_pairs={{0,1},{1,0},{2,3},{3,2},{4,5},{5,4},{6,7},{7,6},{8,9},{9,8},{10,11... | collective-permute-start | bytes 3538952 | tf_op jit(solution)/shard_map/ppermute | solution.py:176
  83.6 21.8 %collective-permute-start.28 = (bf16[2,2,2,2,1,48,768]{6,5,4,3,2,1,0:T(8,128)(2,1)}, bf16[2,2,2,2,1,48,768]{6,5,4,3,2,1,0:T(8,128)(2,1)S(1)}, u32[]{:S(2)}, u32[]{:S(2)}) collective-permute-start(bf16[2,2,2,2,1,48,768]{6,5,4,3,2,1,0:T(8,128)(2,1)} %pad_maximum_fusion.10), channel_id=1, source_target_pairs={{0,1},{1,0},{2,3},{3,2},{4,5},{5,4},{6,7},{7,6},{8,9},{9,8},{10,11... | collective-permute-start | bytes 3538952 | tf_op jit(solution)/shard_map/ppermute | solution.py:176
  103.4 46.8 %collective-permute-start.17 = (f32[4,1536]{1,0:T(4,128)}, f32[4,1536]{1,0:T(4,128)}, u32[]{:S(2)}, u32[]{:S(2)}) collective-permute-start(f32[4,1536]{1,0:T(4,128)} %get-tuple-element.121), channel_id=1, source_target_pairs={{0,1},{1,0},{2,3},{3,2},{4,5},{5,4},{6,7},{7,6},{8,9},{9,8},{10,11... | collective-permute-start | bytes 73736 | tf_op jit(solution)/shard_map/ppermute | solution.py:176
  238.1 91.8 %all-to-all-start = ((bf16[8,4,40,1536]{3,2,1,0:T(8,128)(2,1)}), bf16[8,4,40,1536]{3,2,1,0:T(8,128)(2,1)}, u32[]{:S(2)}, u32[]{:S(2)}) async-start(bf16[8,4,40,1536]{3,2,1,0:T(8,128)(2,1)} %bitcast.155), calls=%async_computation | async-start | bytes 7864320 | tf_op jit(solution)/shard_map/all_to_all | solution.py:434
  242.7 29.2 %collective-permute-start.30 = (bf16[768,768]{1,0:T(8,128)(2,1)}, bf16[768,768]{1,0:T(8,128)(2,1)S(1)}, u32[]{:S(2)}, u32[]{:S(2)}) collective-permute-start(bf16[768,768]{1,0:T(8,128)(2,1)} %bitcast.194), channel_id=1, source_target_pairs={{0,2},{1,3},{2,0},{3,1},{4,6},{5,7},{6,4},{7,5},{8,10},{9,11},{10,... | collective-permute-start | bytes 3538952 | tf_op jit(solution)/shard_map/ppermute | solution.py:176
  244.1 51.4 %collective-permute-start.33 = (bf16[768,768]{1,0:T(8,128)(2,1)}, bf16[768,768]{1,0:T(8,128)(2,1)}, u32[]{:S(2)}, u32[]{:S(2)}) collective-permute-start(bf16[768,768]{1,0:T(8,128)(2,1)} %bitcast.190), channel_id=1, source_target_pairs={{0,2},{1,3},{2,0},{3,1},{4,6},{5,7},{6,4},{7,5},{8,10},{9,11},{10,... | collective-permute-start | bytes 3538952 | tf_op jit(solution)/shard_map/ppermute | solution.py:176
  244.8 50.7 %collective-permute-start.29 = (bf16[768,768]{1,0:T(8,128)(2,1)}, bf16[768,768]{1,0:T(8,128)(2,1)}, u32[]{:S(2)}, u32[]{:S(2)}) collective-permute-start(bf16[768,768]{1,0:T(8,128)(2,1)} %bitcast.195), channel_id=1, source_target_pairs={{0,1},{1,0},{2,3},{3,2},{4,5},{5,4},{6,7},{7,6},{8,9},{9,8},{10,11... | collective-permute-start | bytes 3538952 | tf_op jit(solution)/shard_map/ppermute | solution.py:176
  272.9 22.6 %collective-permute-start.31 = (bf16[768,768]{1,0:T(8,128)(2,1)S(1)}, bf16[768,768]{1,0:T(8,128)(2,1)}, u32[]{:S(2)}, u32[]{:S(2)}) collective-permute-start(bf16[768,768]{1,0:T(8,128)(2,1)S(1)} %collective-permute-done.30), channel_id=1, source_target_pairs={{0,1},{1,0},{2,3},{3,2},{4,5},{5,4},{6,7},{7,6},{8,9},{9,8},{10,11... | collective-permute-start | bytes 3538952 | tf_op jit(solution)/shard_map/ppermute | solution.py:176
  272.9 71.6 %collective-permute-start.32 = (bf16[768,768]{1,0:T(8,128)(2,1)}, bf16[768,768]{1,0:T(8,128)(2,1)}, u32[]{:S(2)}, u32[]{:S(2)}) collective-permute-start(bf16[768,768]{1,0:T(8,128)(2,1)} %bitcast.191), channel_id=1, source_target_pairs={{0,1},{1,0},{2,3},{3,2},{4,5},{5,4},{6,7},{7,6},{8,9},{9,8},{10,11... | collective-permute-start | bytes 3538952 | tf_op jit(solution)/shard_map/ppermute | solution.py:176
  295.4 49.1 %collective-permute-start.34 = (bf16[768,768]{1,0:T(8,128)(2,1)}, bf16[768,768]{1,0:T(8,128)(2,1)}, u32[]{:S(2)}, u32[]{:S(2)}) collective-permute-start(bf16[768,768]{1,0:T(8,128)(2,1)} %collective-permute-done.33), channel_id=1, source_target_pairs={{0,1},{1,0},{2,3},{3,2},{4,5},{5,4},{6,7},{7,6},{8,9},{9,8},{10,11... | collective-permute-start | bytes 3538952 | tf_op jit(solution)/shard_map/ppermute | solution.py:176
  402.4 95.1 %all-to-all-start.1 = ((bf16[8,4,40,1536]{3,2,1,0:T(8,128)(2,1)}), bf16[8,4,40,1536]{3,2,1,0:T(8,128)(2,1)}, u32[]{:S(2)}, u32[]{:S(2)}) async-start(bf16[8,4,40,1536]{3,2,1,0:T(8,128)(2,1)} %bitcast.154), calls=%async_computation.1 | async-start | bytes 7864320 | tf_op jit(solution)/shard_map/all_to_all | solution.py:447
  439.9 29.1 %collective-permute-start.65 = (bf16[768,768]{1,0:T(8,128)(2,1)}, bf16[768,768]{1,0:T(8,128)(2,1)}, u32[]{:S(2)}, u32[]{:S(2)}) collective-permute-start(bf16[768,768]{1,0:T(8,128)(2,1)} %fusion.38), channel_id=1, source_target_pairs={{0,2},{1,3},{2,0},{3,1},{4,6},{5,7},{6,4},{7,5},{8,10},{9,11},{10,... | collective-permute-start | bytes 3538952 | tf_op jit(solution)/shard_map/ppermute | solution.py:176
  441.3 31.9 %collective-permute-start.66 = (bf16[768,768]{1,0:T(8,128)(2,1)}, bf16[768,768]{1,0:T(8,128)(2,1)}, u32[]{:S(2)}, u32[]{:S(2)}) collective-permute-start(bf16[768,768]{1,0:T(8,128)(2,1)} %get-tuple-element.129), channel_id=1, source_target_pairs={{0,1},{1,0},{2,3},{3,2},{4,5},{5,4},{6,7},{7,6},{8,9},{9,8},{10,11... | collective-permute-start | bytes 3538952 | tf_op jit(solution)/shard_map/ppermute | solution.py:176
  444.3 49.1 %collective-permute-start.68 = (bf16[768,768]{1,0:T(8,128)(2,1)}, bf16[768,768]{1,0:T(8,128)(2,1)}, u32[]{:S(2)}, u32[]{:S(2)}) collective-permute-start(bf16[768,768]{1,0:T(8,128)(2,1)} %fusion.35), channel_id=1, source_target_pairs={{0,2},{1,3},{2,0},{3,1},{4,6},{5,7},{6,4},{7,5},{8,10},{9,11},{10,... | collective-permute-start | bytes 3538952 | tf_op jit(solution)/shard_map/ppermute | solution.py:176
  565.7 218.5 %collective-permute-start.48 = (bf16[2,2,2,2,1,24,1536]{6,5,4,3,2,1,0:T(8,128)(2,1)}, bf16[2,2,2,2,1,24,1536]{6,5,4,3,2,1,0:T(8,128)(2,1)}, u32[]{:S(2)}, u32[]{:S(2)}) collective-permute-start(bf16[2,2,2,2,1,24,1536]{6,5,4,3,2,1,0:T(8,128)(2,1)} %dynamic-slice_convert_fusion.1), channel_id=1, source_target_pairs={{0,1},{1,0},{2,3},{3,2},{4,5},{5,4},{6,7},{7,6},{8,9},{9,8},{10,11... | collective-permute-start | bytes 3538952 | tf_op jit(solution)/shard_map/ppermute | solution.py:176
  571.7 216.7 %collective-permute-start.58 = (bf16[2,2,2,2,1,48,768]{6,5,4,3,2,1,0:T(8,128)(2,1)}, bf16[2,2,2,2,1,48,768]{6,5,4,3,2,1,0:T(8,128)(2,1)}, u32[]{:S(2)}, u32[]{:S(2)}) collective-permute-start(bf16[2,2,2,2,1,48,768]{6,5,4,3,2,1,0:T(8,128)(2,1)} %dynamic-slice_convert_fusion), channel_id=1, source_target_pairs={{0,1},{1,0},{2,3},{3,2},{4,5},{5,4},{6,7},{7,6},{8,9},{9,8},{10,11... | collective-permute-start | bytes 3538952 | tf_op jit(solution)/shard_map/ppermute | solution.py:176
  763.7 30.5 %collective-permute-start.43 = (bf16[2,2,2,2,1,24,1536]{6,5,4,3,2,1,0:T(8,128)(2,1)}, bf16[2,2,2,2,1,24,1536]{6,5,4,3,2,1,0:T(8,128)(2,1)}, u32[]{:S(2)}, u32[]{:S(2)}) collective-permute-start(bf16[2,2,2,2,1,24,1536]{6,5,4,3,2,1,0:T(8,128)(2,1)} %dynamic-slice_convert_fusion.2), channel_id=1, source_target_pairs={{0,1},{1,0},{2,3},{3,2},{4,5},{5,4},{6,7},{7,6},{8,9},{9,8},{10,11... | collective-permute-start | bytes 3538952 | tf_op jit(solution)/shard_map/ppermute | solution.py:176
  786.6 29.0 %collective-permute-start.49 = (bf16[2,2,1,2,1,24,1536]{6,5,4,3,2,1,0:T(8,128)(2,1)S(1)}, bf16[2,2,1,2,1,24,1536]{6,5,4,3,2,1,0:T(8,128)(2,1)S(1)}, u32[]{:S(2)}, u32[]{:S(2)}) collective-permute-start(bf16[2,2,1,2,1,24,1536]{6,5,4,3,2,1,0:T(8,128)(2,1)S(1)} %dynamic-slice_convert_fusion.4), channel_id=1, source_target_pairs={{0,4},{4,0},{8,12},{12,8},{16,20},{20,16},{24,28},{28,24},{1,5},{5... | collective-permute-start | bytes 1769480 | tf_op jit(solution)/shard_map/ppermute | solution.py:176
  790.8 25.6 %collective-permute-start.59 = (bf16[2,1,2,2,1,48,768]{6,5,4,3,2,1,0:T(8,128)(2,1)S(1)}, bf16[2,1,2,2,1,48,768]{6,5,4,3,2,1,0:T(8,128)(2,1)S(1)}, u32[]{:S(2)}, u32[]{:S(2)}) collective-permute-start(bf16[2,1,2,2,1,48,768]{6,5,4,3,2,1,0:T(8,128)(2,1)S(1)} %dynamic-slice_convert_fusion.3), channel_id=1, source_target_pairs={{0,8},{4,12},{8,0},{12,4},{16,24},{20,28},{24,16},{28,20},{1,9},{5... | collective-permute-start | bytes 1769480 | tf_op jit(solution)/shard_map/ppermute | solution.py:176
  792.4 21.5 %collective-permute-start.54 = (f32[2,1,2,2,1,48,256]{6,5,4,3,2,1,0:T(8,128)S(1)}, f32[2,1,2,2,1,48,256]{6,5,4,3,2,1,0:T(8,128)S(1)}, u32[]{:S(2)}, u32[]{:S(2)}) collective-permute-start(f32[2,1,2,2,1,48,256]{6,5,4,3,2,1,0:T(8,128)S(1)} %constant_dynamic-slice_fusion.3), channel_id=1, source_target_pairs={{0,8},{4,12},{8,0},{12,4},{16,24},{20,28},{24,16},{28,20},{1,9},{5... | collective-permute-start | bytes 1179656 | tf_op jit(solution)/shard_map/ppermute | solution.py:176
  796.7 56.2 %collective-permute-start.44 = (bf16[2,2,2,1,1,24,1536]{6,5,4,3,2,1,0:T(8,128)(2,1)}, bf16[2,2,2,1,1,24,1536]{6,5,4,3,2,1,0:T(8,128)(2,1)}, u32[]{:S(2)}, u32[]{:S(2)}) collective-permute-start(bf16[2,2,2,1,1,24,1536]{6,5,4,3,2,1,0:T(8,128)(2,1)} %dynamic-slice_convert_fusion.5), channel_id=1, source_target_pairs={{0,2},{1,3},{2,0},{3,1},{4,6},{5,7},{6,4},{7,5},{8,10},{9,11},{10,... | collective-permute-start | bytes 1769480 | tf_op jit(solution)/shard_map/ppermute | solution.py:176
  (156 other events, 2417.0 us)

commit v2 on v1

v2 whole, which is shorter than its diff:
```python
import functools
import math

import jax
import jax.numpy as jnp
from jax import lax
from jax.experimental import pallas as pl
from jax.experimental.pallas import tpu as pltpu
from jax.sharding import PartitionSpec as P

DI = 1536
STATE = 16
DT_RANK = 48
CONV = 4
SEQ_MB = 1
EPSILON = 1e-05
F32 = jnp.float32
BF = jnp.bfloat16
U = 16
CB = 512
CE = 768
VM = 48 << 20
COST = 1
LOG2E = 1.0 / math.log(2.0)
LN2 = math.log(2.0)
HALO = 8


def end_f_kernel(chunks, s_ref, x_ref, bt_ref, r_ref, h_ref):
    r = r_ref[...]
    width = r.shape[1]
    def chunk(c, h):
        rows = pl.ds(pl.multiple_of(c*U,U),U)
        s8 = s_ref[0, rows, :]
        d8 = x_ref[0, rows, :].astype(F32)*s8
        bt = bt_ref[0, c]
        for k in range(U):
            s = jnp.broadcast_to(s8[k:k+1], (STATE,width))
            d = jnp.broadcast_to(d8[k:k+1], (STATE,width))
            b = jnp.broadcast_to(bt[0:STATE, k:k+1], (STATE,width))
            h = jnp.exp2(s*r)*h + d*b
        return h
    h_ref[0] = lax.fori_loop(0, chunks, chunk, jnp.zeros((STATE,width),F32))


def scan_end_f(s, x, bt, r):
    S,T,C = s.shape
    cb=min(CE,C)
    row=pl.BlockSpec((1,T,cb), lambda i,j:(i,0,j))
    return pl.pallas_call(functools.partial(end_f_kernel, T//U),
        grid=(S,C//cb),
        in_specs=[row,row,pl.BlockSpec((1,T//U,2*STATE,U),lambda i,j:(i,0,0,0)),pl.BlockSpec((STATE,cb),lambda i,j:(0,j))],
        out_specs=pl.BlockSpec((1,STATE,cb),lambda i,j:(i,0,j)),
        out_shape=jax.ShapeDtypeStruct((S,STATE,C),F32),
        compiler_params=pltpu.CompilerParams(vmem_limit_bytes=VM),
        cost_estimate=pl.CostEstimate(flops=COST*S*T*C,bytes_accessed=COST*S*T*C,transcendentals=0),
        name="scan_end_f",
    )(s,x,bt,r)


def end_b_kernel(chunks, s_ref, g_ref, bt_ref, r_ref, h_ref, out_ref, go_ref):
    r = r_ref[...]
    width = r.shape[1]
    @pl.when(pl.program_id(1)==0)
    def _():
        go_ref[...]=jnp.zeros_like(go_ref)
    def chunk(c, h):
        c = chunks-1-c
        rows = pl.ds(pl.multiple_of(c*U,U),U)
        s8 = s_ref[0, rows, :]
        g8 = g_ref[0, rows, :]
        bt = bt_ref[0, c]
        go_ref[0, rows, :] += lax.dot_general(g8.astype(BF), h_ref[0, pl.ds(pl.multiple_of(c*U*STATE,U*STATE),U*STATE), :], (((1,),(1,)),((),())), preferred_element_type=F32)
        for k in range(U-1,-1,-1):
            s = jnp.broadcast_to(s8[k:k+1], (STATE,width))
            g = jnp.broadcast_to(g8[k:k+1], (STATE,width))
            cc = jnp.broadcast_to(bt[STATE:2*STATE, k:k+1], (STATE,width))
            h = jnp.exp2(s*r)*(h + g*cc)
        return h
    out_ref[0] = lax.fori_loop(0, chunks, chunk, jnp.zeros((STATE,width),F32))


def scan_end_b(s, g, bt, r, h):
    S,T,C = s.shape
    cb=min(CE,C)
    row=pl.BlockSpec((1,T,cb), lambda i,j:(i,0,j))
    return pl.pallas_call(functools.partial(end_b_kernel, T//U),
        grid=(S,C//cb),
        in_specs=[row,row,pl.BlockSpec((1,T//U,2*STATE,U),lambda i,j:(i,0,0,0)),pl.BlockSpec((STATE,cb),lambda i,j:(0,j)),pl.BlockSpec((1,T*STATE,cb),lambda i,j:(i,0,j))],
        out_specs=[pl.BlockSpec((1,STATE,cb),lambda i,j:(i,0,j)),pl.BlockSpec((1,T,U*STATE),lambda i,j:(i,0,0))],
        out_shape=[jax.ShapeDtypeStruct((S,STATE,C),F32),jax.ShapeDtypeStruct((S,T,U*STATE),F32)],
        compiler_params=pltpu.CompilerParams(vmem_limit_bytes=VM),
        cost_estimate=pl.CostEstimate(flops=COST*S*T*C,bytes_accessed=COST*S*T*C,transcendentals=0),
        name="scan_end_b",
    )(s,g,bt,r,h)


def fwd_kernel(chunks, s_ref, x_ref, bt_ref, l_ref, r_ref, h0_ref, y_ref, h_ref, even, odd):
    r = r_ref[...]
    width = r.shape[1]
    def rows_at(c, size):
        return pl.ds(pl.multiple_of(c*size,size),size)
    def chunk(c, h, mine, other):
        before = jnp.maximum(c-1,0)
        y_ref[0, rows_at(before,U), :] = jnp.dot(l_ref[0, rows_at(before,U), :], other[...], preferred_element_type=F32)
        rows = rows_at(c,U)
        s8 = s_ref[0, rows, :]
        d8 = x_ref[0, rows, :].astype(F32)*s8
        bt = bt_ref[0, c]
        for k in range(U):
            s = jnp.broadcast_to(s8[k:k+1], (STATE,width))
            d = jnp.broadcast_to(d8[k:k+1], (STATE,width))
            b = jnp.broadcast_to(bt[0:STATE, k:k+1], (STATE,width))
            h = jnp.exp2(s*r)*h + d*b
            low = h.astype(BF)
            mine[k*STATE:(k+1)*STATE, :] = low
            h_ref[0, pl.ds(pl.multiple_of(c*U*STATE+k*STATE,STATE),STATE), :] = low
        return h
    def pair(i, h):
        h = chunk(2*i, h, even, odd)
        return chunk(2*i+1, h, odd, even)
    odd[...] = jnp.zeros_like(odd)
    lax.fori_loop(0, chunks//2, pair, h0_ref[0])
    last = pl.ds((chunks-1)*U,U)
    y_ref[0, last, :] = jnp.dot(l_ref[0, last, :], odd[...], preferred_element_type=F32)

def scan_fwd(s, x, bt, l, r, h0):
    S,T,C = s.shape
    cb=min(CB,C)
    row=pl.BlockSpec((1,T,cb), lambda i,j:(i,0,j))
    st=pl.BlockSpec((1,STATE,cb),lambda i,j:(i,0,j))
    return pl.pallas_call(functools.partial(fwd_kernel, T//U),
        grid=(S,C//cb),
        in_specs=[row,row,pl.BlockSpec((1,T//U,2*STATE,U),lambda i,j:(i,0,0,0)),pl.BlockSpec((1,T,U*STATE),lambda i,j:(i,0,0)),pl.BlockSpec((STATE,cb),lambda i,j:(0,j)),st],
        out_specs=[row,pl.BlockSpec((1,T*STATE,cb),lambda i,j:(i,0,j))],
        out_shape=[jax.ShapeDtypeStruct((S,T,C),F32),jax.ShapeDtypeStruct((S,T*STATE,C),BF)],
        scratch_shapes=[pltpu.VMEM((U*STATE,cb),BF)]*2,
        compiler_params=pltpu.CompilerParams(vmem_limit_bytes=VM),
        cost_estimate=pl.CostEstimate(flops=COST*S*T*C,bytes_accessed=COST*S*T*C,transcendentals=0),
        name="scan_fwd",
    )(s,x,bt,l,r,h0)


def bwd_kernel(chunks, s_ref, x_ref, g_ref, bt_ref, l_ref, one_ref, r_ref, h0_ref, m0_ref, h_ref,
               pull_ref, gs_ref, alog_ref, gi_ref, lam_e, fr_e, lam_o, fr_o):
    r = r_ref[...]
    width = r.shape[1]
    j = pl.program_id(1)
    nt=(((1,),(1,)),((),()))
    def rows_at(c, size):
        return pl.ds(pl.multiple_of(c*size,size),size)
    @pl.when(j==0)
    def _():
        gi_ref[...]=jnp.zeros_like(gi_ref)
    lam_o[...] = jnp.zeros_like(lam_o)
    fr_o[...] = jnp.zeros_like(fr_o)
    def sums(c, lam_s, fr_s, first=None):
        rows = rows_at(c,U)
        d8 = (x_ref[0, rows, :].astype(F32)*s_ref[0, rows, :]).astype(BF)
        lam_all = lam_s[...]
        pull_ref[0, rows, :] = jnp.dot(l_ref[0, rows, :], lam_all, preferred_element_type=F32)
        gs_ref[0, rows, :] = jnp.dot(one_ref[...], fr_s[...], preferred_element_type=F32)
        gi = lax.dot_general(d8, lam_all, nt, preferred_element_type=F32)
        if first is not None:
            gi = jnp.where(first, 0.0, gi)
        gi_ref[0, rows, :] += gi
    def chunk(c, carry, mine, other, first=None):
        lam_c, alog = carry
        sums(jnp.minimum(c+1,chunks-1), *other, first)
        lam_s, fr_s = mine
        rows = rows_at(c,U)
        s8 = s_ref[0, rows, :]
        g8 = g_ref[0, rows, :]
        bt = bt_ref[0, c]
        for k in range(U-1,-1,-1):
            s = jnp.broadcast_to(s8[k:k+1], (STATE,width))
            g = jnp.broadcast_to(g8[k:k+1], (STATE,width))
            cc = jnp.broadcast_to(bt[STATE:2*STATE, k:k+1], (STATE,width))
            if k:
                hp = h_ref[0, pl.ds(pl.multiple_of(c*U*STATE+(k-1)*STATE,STATE),STATE), :].astype(F32)
            else:
                hp = h_ref[0, pl.ds(pl.multiple_of(jnp.maximum(c*U*STATE-STATE,0),STATE),STATE), :].astype(F32)
                hp = jnp.where(c==0, h0_ref[0], hp)
            lam = lam_c + g*cc
            lam_c = jnp.exp2(s*r)*lam
            fr = lam_c*hp*r
            alog = alog + fr*s
            lam_s[k*STATE:(k+1)*STATE,:] = lam.astype(BF)
            fr_s[k*STATE:(k+1)*STATE,:] = fr.astype(BF)
        return lam_c, alog
    E=(lam_e,fr_e); O=(lam_o,fr_o)
    def pair(i, carry):
        c = chunks-1-2*i
        carry = chunk(c, carry, E, O, i==0)
        return chunk(c-1, carry, O, E)
    _, alog = lax.fori_loop(0, chunks//2, pair, (m0_ref[0], jnp.zeros((STATE,width),F32)))
    sums(0, *O)
    alog_ref[0] = alog

def scan_bwd(s, x, g, bt, l, one, r, h0, m0, h):
    S,T,C = s.shape
    cb=min(CB,C)
    row=pl.BlockSpec((1,T,cb), lambda i,j:(i,0,j))
    st=pl.BlockSpec((1,STATE,cb),lambda i,j:(i,0,j))
    lo=pl.BlockSpec((1,T,U*STATE),lambda i,j:(i,0,0))
    return pl.pallas_call(functools.partial(bwd_kernel, T//U),
        grid=(S,C//cb),
        in_specs=[row,row,row,pl.BlockSpec((1,T//U,2*STATE,U),lambda i,j:(i,0,0,0)),lo,pl.BlockSpec((U,U*STATE),lambda i,j:(0,0)),pl.BlockSpec((STATE,cb),lambda i,j:(0,j)),st,st,pl.BlockSpec((1,T*STATE,cb),lambda i,j:(i,0,j))],
        out_specs=[row,row,st,lo],
        out_shape=[jax.ShapeDtypeStruct((S,T,C),F32),jax.ShapeDtypeStruct((S,T,C),F32),jax.ShapeDtypeStruct((S,STATE,C),F32),jax.ShapeDtypeStruct((S,T,U*STATE),F32)],
        scratch_shapes=[pltpu.VMEM((U*STATE,cb),BF)]*4,
        compiler_params=pltpu.CompilerParams(vmem_limit_bytes=VM),
        cost_estimate=pl.CostEstimate(flops=COST*S*T*C,bytes_accessed=COST*S*T*C,transcendentals=0),
        name="scan_bwd",
    )(s,x,g,bt,l,one,r,h0,m0,h)


def gelu_and_slope(x):
    root = math.sqrt(2.0 / math.pi)
    square = x * x
    t = jnp.tanh(x * (root + (root * 0.044715) * square))
    half = 0.5 + 0.5 * t
    slope = half + (0.5 * x) * (1.0 - t * t) * (root + (3.0 * root * 0.044715) * square)
    return x * half, slope


def expert_kernel(pieces, tile, x_ref, *refs):
    w_refs = refs[: 2 * pieces]
    back_ref, value_ref, grad_ref, first_s, second_s, out_s, gin_s, sems = refs[-8:]
    j = pl.program_id(0)
    rows, width = out_s.shape
    copies = [
        pltpu.make_async_copy(w_refs[q], (first_s if q < pieces else second_s).at[q % pieces], sems.at[q])
        for q in range(2 * pieces)
    ]

    @pl.when(j == 0)
    def _():
        for q in range(pieces):
            copies[q].start()
            copies[q + pieces].start()

    for q in range(pieces):
        @pl.when(j == q)
        def _():
            copies[q].wait()
            copies[q + pieces].wait()

    def mm(a, b, dims):
        return lax.dot_general(a, b, (dims, ((), ())), preferred_element_type=F32)

    first = first_s[j]
    second = second_s[j]
    for i in range(rows // tile):
        at = slice(i * tile, (i + 1) * tile)
        hidden = mm(x_ref[at, :width], first, ((1,), (0,)))
        grad = mm(x_ref[at, width:], second, ((1,), (1,)))
        value, slope = gelu_and_slope(hidden)
        value = value.astype(BF)
        grad = (grad * slope).astype(BF)
        value_ref[at, :] = value
        grad_ref[at, :] = grad
        out = mm(value, second, ((1,), (0,)))
        gin = mm(grad, first, ((1,), (1,)))

        @pl.when(j == 0)
        def _():
            out_s[at, :] = out
            gin_s[at, :] = gin

        @pl.when(j > 0)
        def _():
            out_s[at, :] += out
            gin_s[at, :] += gin

    @pl.when(j == pieces - 1)
    def _():
        back_ref[:, :width] = out_s[...].astype(BF)
        back_ref[:, width:] = gin_s[...].astype(BF)


def expert_call(x, firsts, seconds, part, groups, shared):
    rows, width = x.shape[0], x.shape[1] // 2
    pieces = len(firsts)
    quarter = firsts[0].shape[1]
    tile = math.gcd(rows, 320)
    wide = pl.BlockSpec((rows, quarter), lambda j: (part, j))
    anywhere = pl.BlockSpec(memory_space=pl.ANY)
    whole = pl.BlockSpec((rows, 2 * width), lambda j: (0, 0))
    big = jax.ShapeDtypeStruct((groups * rows, pieces * quarter), BF)
    count = 1 + 2 * pieces
    return pl.pallas_call(
        functools.partial(expert_kernel, pieces, tile),
        grid=(pieces,),
        in_specs=[whole] + [anywhere] * (2 * pieces + len(shared)),
        out_specs=[whole, wide, wide],
        out_shape=[jax.ShapeDtypeStruct((rows, 2 * width), BF), big, big],
        scratch_shapes=[
            pltpu.VMEM((pieces, width, quarter), BF),
            pltpu.VMEM((pieces, quarter, width), BF),
            pltpu.VMEM((rows, width), F32),
            pltpu.VMEM((rows, width), F32),
            pltpu.SemaphoreType.DMA((2 * pieces,)),
        ],
        input_output_aliases={count: 1, count + 1: 2} if shared else {},
        compiler_params=pltpu.CompilerParams(vmem_limit_bytes=VM),
        cost_estimate=pl.CostEstimate(
            flops=8 * rows * width * quarter * pieces,
            bytes_accessed=4 * pieces * width * quarter + 16 * rows * width,
            transcendentals=rows * quarter * pieces,
        ),
        name="expert",
    )(x, *firsts, *seconds, *shared)


def own_rows(span):
    return jnp.arange(span)[:, None] % U == jnp.arange(U * STATE)[None] // STATE


def state_picker():
    return (jnp.arange(STATE)[:, None] == jnp.arange(U * STATE)[None] % STATE).astype(BF)


def fold(z):
    z = jnp.where(own_rows(z.shape[1]), z, 0).astype(BF)
    return nt(z, state_picker())


def spread_rows(m):
    wide = nn(m.astype(BF), state_picker())
    return jnp.where(own_rows(m.shape[1]), wide, 0).astype(BF)


def bits_of(axis):
    return lax.axis_size(axis).bit_length() - 1


def my_bit(axis, k):
    return (lax.axis_index(axis) >> k) & 1


def swap(x, axis, k):
    count = lax.axis_size(axis)
    return lax.ppermute(x, axis, [(i, i ^ (1 << k)) for i in range(count)])


def shift(x, axis, distance):
    count = lax.axis_size(axis)
    return lax.ppermute(
        x, axis, [(i, i + distance) for i in range(count) if 0 <= i + distance < count]
    )


def joined_pair(x, other, axis, k, place):
    high = my_bit(axis, k) == 1
    return jnp.where(
        high,
        jnp.concatenate([other, x], axis=place),
        jnp.concatenate([x, other], axis=place),
    )


def from_batch(x):
    copies = jnp.broadcast_to(x[None], (lax.axis_size("batch"),) + x.shape)
    return lax.all_to_all(copies, "batch", split_axis=0, concat_axis=0, tiled=True)


def over_seq(x):
    bits = bits_of("seq")
    out = x.reshape(x.shape[:1] + (1,) * bits + x.shape[1:])
    for k in reversed(range(bits)):
        out = joined_pair(out, swap(out, "seq", k), "seq", k, bits - k)
    return out.reshape((-1,) + x.shape[2:])


def over_batch(x):
    got = lax.all_to_all(x.astype(BF), "batch", split_axis=0, concat_axis=0, tiled=True)
    return jnp.sum(got.astype(F32), axis=0)


def halved(x, k, place):
    bit = my_bit("seq", k)
    mine = lax.dynamic_index_in_dim(x, bit, place, True)
    theirs = lax.dynamic_index_in_dim(x, 1 - bit, place, True).astype(BF)
    return mine + swap(theirs, "seq", k).astype(F32)


def scatter_sum(x):
    bits = bits_of("seq")
    rows = x.shape[0] // (lax.axis_size("batch") << bits)
    out = x.reshape((lax.axis_size("batch"),) + (2,) * bits + (rows,) + x.shape[1:])
    for k in range(bits):
        out = halved(out, k, bits - k)
    return over_batch(out).reshape((rows,) + x.shape[1:])


def gather_seq(x, event):
    parts = [x]
    for k in reversed(range(bits_of("seq"))):
        more = [swap(p, "seq", k) for p in parts]
        parts = parts + (after(more, event) if k else more)
    count = len(parts)
    order = []
    for k in reversed(range(bits_of("seq"))):
        order = (order or [0]) + [o ^ (1 << k) for o in (order or [0])]
    return [parts[order.index(j)] for j in range(count)]


def scatter_seq(parts, k, event):
    bit = 1 << k
    moved = {j ^ bit: swap(p.astype(BF), "seq", k) for j, p in parts.items() if j & bit}
    moved = after(moved, event)
    return {j: p + moved[j].astype(F32) for j, p in parts.items() if not j & bit}


def totals_of(total):
    levels = []
    for k in range(bits_of("seq")):
        other = swap(total, "seq", k)
        levels.append((total, other))
        total = total + other
    return levels


def prefix(levels, state, rate, backward):
    before = jnp.zeros_like(state)
    before_total = jnp.zeros_like(levels[0][0])
    for k, (total, other_total) in enumerate(levels):
        other = swap(state.astype(BF), "seq", k).astype(F32)
        first = my_bit("seq", k) == (0 if backward else 1)
        before = jnp.where(
            first, before + jnp.exp2(before_total[:, None, :] * rate) * other, before
        )
        before_total = jnp.where(first, before_total + other_total, before_total)
        if k + 1 < len(levels):
            near = jnp.where(first, state, other)
            far = jnp.where(first, other, state)
            near_total = jnp.where(first, total, other_total)
            state = near + jnp.exp2(near_total[:, None, :] * rate) * far
    return before


def after(value, event):
    return lax.optimization_barrier((value, event))[0]


def mm(left, right, dims):
    return lax.dot_general(left, right, (dims, ((), ())), preferred_element_type=F32)


def nn(left, right):
    return mm(left, right, ((left.ndim - 1,), (0,)))


def nt(left, right):
    return mm(left, right, ((left.ndim - 1,), (1,)))


def tn(left, right):
    lead = tuple(range(left.ndim - 1))
    return mm(left, right, (lead, lead))


def silu_slope(v):
    s = jax.nn.sigmoid(v)
    return s * (1.0 + v * (1.0 - s))


def norm_back(grad_norm, x, scale):
    return scale * grad_norm - x * scale**3 * jnp.mean(grad_norm * x, axis=-1, keepdims=True)


def gelu_tanh(v):
    return jax.nn.gelu(v, approximate=True)


def rms(x):
    return lax.rsqrt(jnp.mean(x * x, axis=-1, keepdims=True) + EPSILON)


def pad_cols(x, width):
    return jnp.pad(x, ((0, 0), (0, width - x.shape[1])))


def shards(
    tokens,
    cotangent,
    lengths,
    order,
    expert_route,
    slot_index,
    norm_gain,
    in_proj,
    conv_weight,
    conv_bias,
    x_proj,
    dt_proj,
    dt_bias,
    a_log,
    skip_gain,
    out_proj,
    moe_gain,
    router,
    expert_in,
    expert_out,
):
    seqs, span, width = tokens.shape
    batch = lax.axis_size("batch")
    experts = expert_in.shape[0] * batch
    capacity = max(2, (5 * SEQ_MB * span + 4 * experts - 1) // (4 * experts))
    maps = DT_RANK + 2 * STATE
    lo = HALO - (CONV - 1)
    groups = 2
    size = seqs // groups

    rows = in_proj.shape[0]
    chan = jnp.concatenate(
        [
            x_proj,
            dt_proj,
            a_log,
            conv_weight,
            conv_bias[:, None],
            dt_bias[:, None],
            skip_gain[:, None],
        ],
        axis=1,
    )
    feat = jnp.concatenate([norm_gain[:, None], moe_gain[:, None], router], axis=1)
    cut = 1024
    first_set = from_batch(in_proj[:, :cut])
    later = jnp.concatenate([in_proj[:, DI:], out_proj.reshape(rows, 2 * width)], axis=1)
    later = after(later, first_set)
    later = lax.all_gather(later, ("batch", "seq"), axis=0, tiled=True)
    w_gate_in = later[:, :DI]
    w_back = later[:, DI:].reshape(DI, width)
    first_set = over_seq(first_set)
    second_set = over_seq(
        from_batch(
            jnp.concatenate(
                [in_proj[:, cut:DI], pad_cols(chan, 256).reshape(rows, 512), pad_cols(feat, 128)],
                axis=1,
            )
        )
    )
    w_conv_in = jnp.concatenate([first_set, second_set[:, : DI - cut]], axis=1)
    chan = second_set[:, DI - cut : DI - cut + 512].reshape(-1, 256)
    feat = second_set[:, DI - cut + 512 :]
    gain_one = feat[:, 0].astype(F32)
    gain_two = feat[:, 1].astype(F32)
    router_weight = feat[:, 2 : 2 + experts]
    w_proj = chan[:, :maps]
    at = maps + DT_RANK
    w_step = chan[:, maps:at]
    rate = -jnp.exp(chan[:, at : at + STATE].astype(F32)).T * LOG2E
    at = at + STATE
    taps = chan[:, at : at + CONV].astype(F32).T
    bias_conv = chan[:, at + CONV].astype(F32)
    bias_step = chan[:, at + CONV + 1].astype(F32)
    skip = chan[:, at + CONV + 2].astype(F32)

    halo_all = shift(tokens[:, span - HALO :, :], "seq", 1)
    tail = jnp.arange(HALO)[:, None] >= lo
    halo_all = jnp.where(tail, halo_all, 0)


    positions = lax.axis_index("seq") * span + jnp.arange(span, dtype=jnp.int32)
    row_length = jnp.sum(
        jnp.where(
            order[:, None] == jnp.arange(lengths.shape[0], dtype=jnp.int32)[None, :],
            lengths[None, :],
            0,
        ),
        axis=1,
    )
    keep_all = (positions[None, :] < row_length[:, None]).astype(F32)
    ones = (jnp.arange(U)[:, None] == jnp.arange(U * STATE)[None] // STATE).astype(BF)
    slots = jnp.arange(experts * capacity, dtype=jnp.int32)
    expert_ids = jnp.arange(experts, dtype=jnp.int32)

    class Part:
        pass

    def forward(m, event, second_event):
        p = Part()
        here = slice(m * size, (m + 1) * size)
        own = tokens[here]
        if event is not None:
            own = after(own, event)
        p.block = own.astype(F32)
        p.scale_one = rms(p.block)
        ext = jnp.concatenate([halo_all[here], own], axis=1).astype(F32)
        normed_ext = (ext * rms(ext) * gain_one).astype(BF)
        p.normed = normed_ext[:, HALO:]
        p.conv_ext = nn(normed_ext, w_conv_in)
        p.conv_out = bias_conv + sum(
            p.conv_ext[:, lo + k : lo + k + span, :] * taps[k] for k in range(CONV)
        )
        p.act = jax.nn.silu(p.conv_out).astype(BF)
        projected = nn(p.act, w_proj)
        p.delta = projected[..., :DT_RANK].astype(BF)
        input_map = projected[..., DT_RANK : DT_RANK + STATE]
        output_map = projected[..., DT_RANK + STATE :]
        p.step_arg = nt(p.delta, w_step) + bias_step
        p.step = jax.nn.softplus(p.step_arg)
        p.levels = totals_of(jnp.sum(p.step, axis=1))
        p.both = jnp.swapaxes(
            projected[..., DT_RANK:].reshape(size, span // U, U, 2 * STATE), 2, 3
        )
        p.in_rows = spread_rows(input_map)
        out_rows = spread_rows(output_map)
        end = scan_end_f(p.step, p.act, p.both, rate)
        p.init = prefix(p.levels, end, rate, False)
        if second_event is not None:
            p.init = after(p.init, second_event)
        p.gate_in = nn(p.normed, w_gate_in)
        y, p.states = scan_fwd(p.step, p.act, p.both, out_rows, rate, p.init)
        p.actf = p.act.astype(F32)
        p.mix = y + skip * p.actf
        p.gate_act = jax.nn.silu(p.gate_in)
        p.gated = (p.mix * p.gate_act).astype(BF)
        p.mixed = p.block + nn(p.gated, w_back)
        p.scale_two = rms(p.mixed)
        p.routed = (p.mixed * p.scale_two * gain_two).astype(BF)
        p.probs = jax.nn.softmax(nn(p.routed, router_weight), axis=-1)
        route = expert_route[here]
        slot = slot_index[here]
        kept = slot >= 0
        target = jnp.where(kept, route * capacity + slot, -1)
        p.selector = (target[..., None] == slots).astype(BF)
        p.chosen = jnp.logical_and(route[..., None] == expert_ids, kept[..., None])
        p.gate = jnp.sum(jnp.where(p.chosen, p.probs, 0.0), axis=-1)[..., None]
        p.grad_out = cotangent[here].astype(F32) * keep_all[here][..., None]
        grad_value = (p.gate * p.grad_out).astype(BF)
        packed = jnp.concatenate([p.routed, grad_value], axis=-1)
        send = jnp.einsum("stc,std->scd", p.selector, packed, preferred_element_type=F32)
        send = jnp.swapaxes(send.astype(BF).reshape(size, batch, capacity, 2 * width), 0, 1)
        p.send = send
        p.arrived = lax.all_to_all(send, "batch", split_axis=0, concat_axis=0, tiled=True)
        return p

    def expert(m, shared):
        p = parts[m]
        p.rows_in = p.arrived.reshape(batch * size * capacity, 2 * width)
        p.back, *shared = expert_call(
            p.rows_in, first_parts, second_parts, m, groups, shared
        )
        back = p.back.reshape(batch, size, capacity, 2 * width)
        back = lax.all_to_all(back, "batch", split_axis=0, concat_axis=0, tiled=True)
        p.returned = jnp.swapaxes(back, 0, 1).reshape(size, experts * capacity, 2 * width)
        return shared

    def backward_router(p):
        picked = jnp.einsum("stc,scd->std", p.selector, p.returned, preferred_element_type=F32)
        expert_tok = picked[..., :width]
        p.activations = (p.mixed + p.gate * expert_tok).astype(BF)
        grad_gate = jnp.sum(expert_tok * p.grad_out, axis=-1, keepdims=True)
        grad_prob = jnp.where(p.chosen, grad_gate, 0.0)
        grad_logits = (
            p.probs * (grad_prob - jnp.sum(p.probs * grad_prob, axis=-1, keepdims=True))
        ).astype(BF)
        p.g_router = tn(p.routed, grad_logits)
        grad_routed = picked[..., width:] + nt(grad_logits, router_weight)
        p.g_gain_two = jnp.sum(grad_routed * p.mixed * p.scale_two, axis=(0, 1))
        p.grad_mixed = p.grad_out + norm_back(grad_routed * gain_two, p.mixed, p.scale_two)
        p.grad_branch = p.grad_mixed.astype(BF)
        grad_gated = nt(p.grad_branch, w_back)
        p.grad_mix = grad_gated * p.gate_act
        p.grad_gate_in = (grad_gated * p.mix * silu_slope(p.gate_in)).astype(BF)
        p.behind, p.grad_out_map = scan_end_b(p.step, p.grad_mix, p.both, rate, p.states)
        p.after = prefix(p.levels, p.behind, rate, True)
        p.g_skip = jnp.sum(p.grad_mix * p.actf, axis=(0, 1))

    def backward_mixer(p):
        pull, grad_rate, g_log, grad_in_map = scan_bwd(
            p.step, p.act, p.grad_mix, p.both, p.in_rows, ones, rate, p.init, p.after, p.states
        )
        p.pull = pull
        p.g_log = jnp.sum(g_log, axis=0).T * LN2
        grad_arg = (grad_rate * LN2 + p.actf * pull) * jax.nn.sigmoid(p.step_arg)
        p.g_step_bias = jnp.sum(grad_arg, axis=(0, 1))
        grad_pre = grad_arg.astype(BF)
        p.g_step = tn(grad_pre, p.delta)
        grad_proj = jnp.concatenate(
            [nn(grad_pre, w_step), fold(grad_in_map), fold(p.grad_out_map)], axis=-1
        ).astype(BF)
        p.g_proj = tn(p.act, grad_proj)
        grad_act = skip * p.grad_mix + p.step * pull + nt(grad_proj, w_proj)
        grad_conv = grad_act * silu_slope(p.conv_out)
        p.g_conv_bias = jnp.sum(grad_conv, axis=(0, 1))
        p.g_taps = jnp.stack(
            [
                jnp.sum(grad_conv * p.conv_ext[:, lo + k : lo + k + span, :], axis=(0, 1))
                for k in range(CONV)
            ],
            axis=-1,
        )
        rim = shift(grad_conv[:, :HALO, :], "seq", -1)
        longer = jnp.concatenate([grad_conv, rim], axis=1)
        p.grad_conv_in = sum(
            longer[:, CONV - 1 - k : CONV - 1 - k + span, :] * taps[k] for k in range(CONV)
        ).astype(BF)

    def backward_input(p):
        grad_normed = nt(p.grad_conv_in, w_conv_in) + nt(p.grad_gate_in, w_gate_in)
        p.input_grad = p.grad_mixed + norm_back(grad_normed * gain_one, p.block, p.scale_one)

    parts = []
    parts.append(forward(0, None, None))
    first_parts = gather_seq(after(expert_in[0], parts[0].init), parts[0].send)
    for m in range(1, groups):
        parts.append(forward(m, parts[-1].send, parts[-1].arrived))
    second_parts = gather_seq(after(expert_out[0], parts[-1].init), parts[-1].mixed)
    shared = ()
    for m in range(groups):
        shared = expert(m, shared)
    values, grad_hidden = shared

    def joined(name):
        return jnp.concatenate([getattr(p, name) for p in parts], axis=0)

    def added(name):
        return functools.reduce(jnp.add, [getattr(p, name) for p in parts])

    def added_products(left, right):
        return functools.reduce(
            jnp.add, [tn(getattr(p, left), getattr(p, right)) for p in parts]
        )

    quarter = expert_in.shape[2]
    rows_in = joined("rows_in")
    rows_in, values, grad_hidden = after((rows_in, values, grad_hidden), parts[-1].back)
    grad_first = []
    grad_second = []
    for q in range(len(first_parts)):
        at = slice(q * quarter, (q + 1) * quarter)
        grad_first.append(tn(rows_in[:, :width], grad_hidden[:, at]))
        grad_second.append(tn(values[:, at], rows_in[:, width:]))

    parts[0].returned = after(parts[0].returned, parts[-1].back)
    backward_router(parts[0])
    for p, earlier in zip(parts[1:], parts):
        p.returned = after(p.returned, earlier.grad_mix)
        backward_router(p)
    g_feat = jnp.concatenate([added("g_gain_two")[:, None], added("g_router")], axis=1)
    background = jnp.concatenate(
        [
            added_products("normed", "grad_gate_in").astype(BF),
            added_products("gated", "grad_branch").astype(BF).reshape(-1, 2 * width),
            pad_cols(g_feat, 128).astype(BF),
        ],
        axis=1,
    )
    background = lax.psum_scatter(background, ("batch", "seq"), scatter_dimension=0, tiled=True)
    background = background.astype(F32)
    g_gate_half = background[:, :DI]
    g_back = background[:, DI : 2 * DI].reshape(-1, width)
    g_feat = background[:, 2 * DI :]
    grad_first = dict(enumerate(grad_first))
    grad_second = dict(enumerate(grad_second))
    grad_first = scatter_seq(grad_first, 0, parts[0].grad_mix)
    grad_second = scatter_seq(grad_second, 0, parts[0].grad_mix)
    for p in parts:
        backward_mixer(p)
    g_chan = jnp.concatenate(
        [
            added("g_proj"),
            added("g_step"),
            added("g_log"),
            added("g_taps"),
            added("g_conv_bias")[:, None],
            added("g_step_bias")[:, None],
            added("g_skip")[:, None],
        ],
        axis=1,
    )
    g_chan = pad_cols(g_chan, 256).reshape(-1, 512)
    g_conv_half = added_products("normed", "grad_conv_in")
    g_rest = scatter_sum(jnp.concatenate([g_conv_half, g_chan], axis=1))
    for p in parts:
        p.grad_conv_in = after(p.grad_conv_in, g_conv_half)
    for k in range(1, bits_of("seq")):
        grad_first = scatter_seq(grad_first, k, g_conv_half)
        grad_second = scatter_seq(grad_second, k, g_conv_half)
    g_conv_half = g_rest[:, :DI]
    g_chan = g_rest[:, DI:].reshape(-1, 256)
    grad_first = grad_first[0]
    grad_second = grad_second[0]
    for p in parts:
        backward_input(p)
    g_in = jnp.concatenate([g_conv_half, g_gate_half], axis=1)
    g_gain_one = jnp.sum(g_in * in_proj.astype(F32), axis=1) / norm_gain.astype(F32)
    at = maps + DT_RANK
    return (
        joined("activations"),
        joined("input_grad"),
        g_gain_one,
        g_in,
        g_chan[:, at + STATE : at + STATE + CONV],
        g_chan[:, at + STATE + CONV],
        g_chan[:, :maps],
        g_chan[:, maps:at],
        g_chan[:, at + STATE + CONV + 1],
        g_chan[:, at : at + STATE],
        g_chan[:, at + STATE + CONV + 2],
        g_back,
        g_feat[:, 0],
        g_feat[:, 1 : 1 + experts],
        grad_first[None],
        grad_second[None],
    )


def solution(mesh):
    return jax.shard_map(
        shards,
        mesh=mesh,
        in_specs=(
            P("batch", "seq", None),
            P("batch", "seq", None),
            P(),
            P("batch"),
            P("batch", "seq"),
            P("batch", "seq"),
            P(("batch", "seq")),
            P(("batch", "seq"), None),
            P(("batch", "seq"), None),
            P(("batch", "seq")),
            P(("batch", "seq"), None),
            P(("batch", "seq"), None),
            P(("batch", "seq")),
            P(("batch", "seq"), None),
            P(("batch", "seq")),
            P(("batch", "seq"), None),
            P(("batch", "seq")),
            P(("batch", "seq"), None),
            P("batch", None, "seq"),
            P("batch", "seq", None),
        ),
        out_specs=(
            P("batch", "seq", None),
            P("batch", "seq", None),
            P(("batch", "seq")),
            P(("batch", "seq"), None),
            P(("batch", "seq"), None),
            P(("batch", "seq")),
            P(("batch", "seq"), None),
            P(("batch", "seq"), None),
            P(("batch", "seq")),
            P(("batch", "seq"), None),
            P(("batch", "seq")),
            P(("batch", "seq"), None),
            P(("batch", "seq")),
            P(("batch", "seq"), None),
            P("batch", None, "seq"),
            P("batch", "seq", None),
        ),
        check_vma=False,
    )
```

time: 886 us -> 701 us (0.79)
  waiting for transfers between devices: 214 us -> 81.5 us
  matrix products: 172 us -> 151 us
  other arithmetic: 111 us -> 95.1 us
  between operations: 3.03 us -> 16.8 us
  local copies, waits for them, and re-layouts: 87.8 us -> 76.6 us
    ppermute x67 -> x28, waiting for transfers between devices: 179 us -> 59.4 us  [swap(): return lax.ppermute(x, axis, [(i, i ^ 1 << k) for i in range(count)])]
    pallas_call x2 -> x6, Pallas kernels: 55.1 us -> 109 us  [the longest x2 43.2 us: expert_call(): pl.pallas_call(functools.partial(expert_kernel, pieces, tile), grid=(piec...]
    ppermute x67 -> x28, starting transfers between devices: 57.3 us -> 17.7 us  [swap(): return lax.ppermute(x, axis, [(i, i ^ 1 << k) for i in range(count)])]
    pallas_call x1 -> x2, Pallas kernels: 102 us -> 65.9 us  [scan_bwd(): pl.pallas_call(functools.partial(bwd_kernel, T // U), grid=(S, C // cb),...]
    all_to_all x2 -> x7, starting transfers between devices: 9.3 us -> 38.3 us  [the longest x2 12.4 us: from_batch(): lax.all_to_all(copies, 'batch', split_axis=0, concat_axis=0, tiled=True)]
    pallas_call x1 -> x2, Pallas kernels: 61.6 us -> 36.1 us  [scan_fwd(): pl.pallas_call(functools.partial(fwd_kernel, T // U), grid=(S, C // cb),...]
    dot_general x24 -> x52, matrix products: 169 us -> 148 us  [mm(): lax.dot_general(left, right, (dims, ((), ())), preferred_element_type=F32)]
    all_to_all x2 -> x7, waiting for transfers between devices: 34.5 us -> 21.4 us  [the longest x2 9.27 us: from_batch(): lax.all_to_all(copies, 'batch', split_axis=0, concat_axis=0, tiled=True)]
  transfers between devices with their start and end apart: 71 -> 40, of which waited for: 24 -> 14; matrix products, arithmetic and copies ran while one was open for 28% -> 39% of each run, Pallas kernels for 15% -> 30%
where the time goes in v2:
time: 701 us; the launch traced here: 693 us
  Pallas kernels  211 us (30%)
  matrix products  151 us (22%)
  other arithmetic  95.1 us (14%)
  waiting for transfers between devices  81.5 us (12%)
  local copies, waits for them, and re-layouts  76.6 us (11%)
  starting transfers between devices  60.5 us (9%)
  between operations  16.8 us (2%)
    dot_general x52, matrix products, mm(): lax.dot_general(left, right, (dims, ((), ())), preferred_element_type=F32)  148 us
    pallas_call x2, Pallas kernels, scan_bwd(): pl.pallas_call(functools.partial(bwd_kernel, T // U), grid=(S, C // cb),...  65.9 us
    ppermute x28, waiting for transfers between devices, swap(): return lax.ppermute(x, axis, [(i, i ^ 1 << k) for i in range(count)])  59.4 us
    pallas_call x2, Pallas kernels, expert_call(): pl.pallas_call(functools.partial(expert_kernel, pieces, tile), grid=(piec...  43.2 us
    pallas_call x2, Pallas kernels, scan_end_b(): pl.pallas_call(functools.partial(end_b_kernel, T // U), grid=(S, C // cb)...  41.2 us
    pallas_call x2, Pallas kernels, scan_fwd(): pl.pallas_call(functools.partial(fwd_kernel, T // U), grid=(S, C // cb),...  36.1 us
    unnamed x396, local copies, waits for them, and re-layouts  28.8 us
    pallas_call x2, Pallas kernels, scan_end_f(): pl.pallas_call(functools.partial(end_f_kernel, T // U), grid=(S, C // cb)...  24.7 us
  transfers between devices with their start and end apart: 40, of which 14 were waited for; matrix products, arithmetic and copies ran while one was open for 39% of the time, Pallas kernels for 30%

profile of v2, /device:TPU:0, one launch (start us, length us, event | category | flops | bytes accessed | tf_op | source)
XLA Modules:
  0.0 692.9 jit_solution(14263570068905285624)
XLA Ops:
  8.8 7.3 %all-to-all-start.1 = ((bf16[8,24,1024]{2,1,0:T(8,128)(2,1)}), bf16[8,24,1024]{2,1,0:T(8,128)(2,1)S(1)}, u32[]{:S(2)}, u32[]{:S(2)}) async-start(bf16[8,24,1024]{2,1,0:T(8,128)(2,1)} %broadcast_in_dim.108), calls=%async_computation.1 | async-start | bytes 786432 | tf_op jit(solution)/shard_map/all_to_all | solution.py:365
  38.4 8.6 %all-to-all-done = bf16[8,24,1152]{2,1,0:T(8,128)(2,1)S(1)} async-done(((bf16[8,24,1152]{2,1,0:T(8,128)(2,1)}), bf16[8,24,1152]{2,1,0:T(8,128)(2,1)S(1)}, u32[]{:S(2)}, u32[]{:S(2)}) %all-to-all-start) | async-done | bytes 442400 | tf_op jit(solution)/shard_map/all_to_all | solution.py:365
  51.2 9.8 %collective-permute-done = bf16[8,1,1,24,1152]{4,3,2,1,0:T(8,128)(2,1)} collective-permute-done((bf16[8,1,1,24,1152]{4,3,2,1,0:T(8,128)(2,1)S(1)}, bf16[8,1,1,24,1152]{4,3,2,1,0:T(8,128)(2,1)}, u32[]{:S(2)}, u32[]{:S(2)}) %collective-permute-start) | collective-permute-done | bytes 442400 | tf_op jit(solution)/shard_map/ppermute | solution.py:344
  86.0 12.3 %scan_end_f.2 = f32[2,16,1536]{2,1,0:T(8,128)S(1)} custom-call(f32[2,256,1536]{2,1,0:T(8,128)S(1)} %copy-done, bf16[2,256,1536]{2,1,0:T(8,128)(2,1)S(1)} %get-tuple-element.226.x_ref, f32[2,16,32,16]{3,2,1,0:T(8,128)S(1)} %bitcast.189, f32[16,1536]{1,0:T(8,128)S(1)} %get-tuple-element.253.r_ref), custom_call_target="tpu_custom_call" | custom-call | flops 786432 | bytes 786432 | tf_op jit(solution)/shard_map/scan_end_f/pallas_call | solution.py:50
  105.2 18.1 %scan_fwd.2 = (f32[2,256,1536]{2,1,0:T(8,128)S(1)}, bf16[2,4096,1536]{2,1,0:T(8,128)(2,1)}) custom-call(f32[2,256,1536]{2,1,0:T(8,128)} %get-tuple-element.239.s_ref, bf16[2,256,1536]{2,1,0:T(8,128)(2,1)S(1)} %get-tuple-element.226.x_ref, f32[2,16,32,16]{3,2,1,0:T(8,128)S(1)} %bitcast.190, bf16[2,256,256]{2,1,0:T(8,128)(2,1)S(1)} %fusion.100.l_ref, ...), custom_call_target="tpu_custom_call" | custom-call | flops 786432 | bytes 786432 | tf_op jit(solution)/shard_map/scan_fwd/pallas_call | solution.py:132
  133.6 6.4 multiply_convert_fusion.4
  171.0 12.3 %scan_end_f.3 = f32[2,16,1536]{2,1,0:T(8,128)S(1)} custom-call(f32[2,256,1536]{2,1,0:T(8,128)S(1)} %copy-done.2, bf16[2,256,1536]{2,1,0:T(8,128)(2,1)S(1)} %get-tuple-element.222.x_ref, f32[2,16,32,16]{3,2,1,0:T(8,128)S(1)} %bitcast.193, f32[16,1536]{1,0:T(8,128)S(1)} %get-tuple-element.253.r_ref), custom_call_target="tpu_custom_call" | custom-call | flops 786432 | bytes 786432 | tf_op jit(solution)/shard_map/scan_end_f/pallas_call | solution.py:50
  199.0 18.0 %scan_fwd.3 = (f32[2,256,1536]{2,1,0:T(8,128)S(1)}, bf16[2,4096,1536]{2,1,0:T(8,128)(2,1)}) custom-call(f32[2,256,1536]{2,1,0:T(8,128)} %get-tuple-element.237.s_ref, bf16[2,256,1536]{2,1,0:T(8,128)(2,1)S(1)} %get-tuple-element.222.x_ref, f32[2,16,32,16]{3,2,1,0:T(8,128)S(1)} %bitcast.194, bf16[2,256,256]{2,1,0:T(8,128)(2,1)S(1)} %copy-done.19, ...), custom_call_target="tpu_custom_call" | custom-call | flops 786432 | bytes 786432 | tf_op jit(solution)/shard_map/scan_fwd/pallas_call | solution.py:132
  217.0 6.4 multiply_convert_fusion.2
  236.5 18.2 %collective-permute-done.15.refs_6_ = bf16[768,768]{1,0:T(8,128)(2,1)} collective-permute-done((bf16[768,768]{1,0:T(8,128)(2,1)}, bf16[768,768]{1,0:T(8,128)(2,1)}, u32[]{:S(2)}, u32[]{:S(2)}) %collective-permute-start.15) | collective-permute-done | bytes 1179680 | tf_op jit(solution)/shard_map/ppermute | solution.py:344
  258.7 21.4 %expert.2 = (bf16[640,1536]{1,0:T(8,128)(2,1)}, bf16[1280,3072]{1,0:T(8,128)(2,1)}, bf16[1280,3072]{1,0:T(8,128)(2,1)}) custom-call(bf16[640,1536]{1,0:T(8,128)(2,1)} %bitcast.22.x_ref, bf16[768,768]{1,0:T(8,128)(2,1)} %bitcast.23.refs_0_, bf16[768,768]{1,0:T(8,128)(2,1)} %collective-permute-done.8.refs_1_, bf16[768,768]{1,0:T(8,128)(2,1)} %collective-permute-done.9.refs_2_, ...), custom_call_target="tpu_custom_call" | custom-call | flops 12079595520 | bytes 17301504 | tf_op jit(solution)/shard_map/expert/pallas_call | solution.py:292
  287.6 21.9 %expert.3 = (bf16[640,1536]{1,0:T(8,128)(2,1)}, bf16[1280,3072]{1,0:T(8,128)(2,1)}, bf16[1280,3072]{1,0:T(8,128)(2,1)}) custom-call(bf16[640,1536]{1,0:T(8,128)(2,1)} %bitcast.33.x_ref, bf16[768,768]{1,0:T(8,128)(2,1)} %bitcast.23.refs_0_, bf16[768,768]{1,0:T(8,128)(2,1)} %collective-permute-done.8.refs_1_, ...), custom_call_target="tpu_custom_call", output_to_operand_aliasing={{1}: (9, {}), {2}: (10, {})} | custom-call | flops 12079595520 | bytes 17301504 | tf_op jit(solution)/shard_map/expert/pallas_call | solution.py:292
  338.2 6.1 all-to-all-start.5
  360.2 6.5 fusion.27
  366.7 20.4 %scan_end_b.2 = (f32[2,16,1536]{2,1,0:T(8,128)S(1)}, f32[2,256,256]{2,1,0:T(8,128)S(1)}) custom-call(f32[2,256,1536]{2,1,0:T(8,128)S(1)} %copy-done.1, f32[2,256,1536]{2,1,0:T(8,128)} %get-tuple-element.215.g_ref, f32[2,16,32,16]{3,2,1,0:T(8,128)S(1)} %bitcast.191, f32[16,1536]{1,0:T(8,128)S(1)} %get-tuple-element.253.r_ref, ...), custom_call_target="tpu_custom_call" | custom-call | flops 786432 | bytes 786432 | tf_op jit(solution)/shard_map/scan_end_b/pallas_call | solution.py:87
  427.4 6.5 fusion.31
  433.9 20.7 %scan_end_b.3 = (f32[2,16,1536]{2,1,0:T(8,128)S(1)}, f32[2,256,256]{2,1,0:T(8,128)S(1)}) custom-call(f32[2,256,1536]{2,1,0:T(8,128)S(1)} %copy-done.3, f32[2,256,1536]{2,1,0:T(8,128)} %get-tuple-element.213.g_ref, f32[2,16,32,16]{3,2,1,0:T(8,128)S(1)} %bitcast.195, f32[16,1536]{1,0:T(8,128)S(1)} %get-tuple-element.253.r_ref, ...), custom_call_target="tpu_custom_call" | custom-call | flops 786432 | bytes 786432 | tf_op jit(solution)/shard_map/scan_end_b/pallas_call | solution.py:87
  461.0 6.1 fusion.4
  491.7 33.0 %scan_bwd.2 = (f32[2,256,1536]{2,1,0:T(8,128)}, f32[2,256,1536]{2,1,0:T(8,128)}, f32[2,16,1536]{2,1,0:T(8,128)S(1)}, f32[2,256,256]{2,1,0:T(8,128)S(1)}) custom-call(f32[2,256,1536]{2,1,0:T(8,128)} %get-tuple-element.239.s_ref, bf16[2,256,1536]{2,1,0:T(8,128)(2,1)S(1)} %get-tuple-element.226.x_ref, f32[2,256,1536]{2,1,0:T(8,128)} %get-tuple-element.215.g_ref, ...), custom_call_target="tpu_custom_call" | custom-call | flops 786432 | bytes 786432 | tf_op jit(solution)/shard_map/scan_bwd/pallas_call | solution.py:206
  531.5 32.9 %scan_bwd.3 = (f32[2,256,1536]{2,1,0:T(8,128)}, f32[2,256,1536]{2,1,0:T(8,128)}, f32[2,16,1536]{2,1,0:T(8,128)S(1)}, f32[2,256,256]{2,1,0:T(8,128)S(1)}) custom-call(f32[2,256,1536]{2,1,0:T(8,128)} %get-tuple-element.237.s_ref, bf16[2,256,1536]{2,1,0:T(8,128)(2,1)S(1)} %get-tuple-element.222.x_ref, f32[2,256,1536]{2,1,0:T(8,128)} %get-tuple-element.213.g_ref, ...), custom_call_target="tpu_custom_call" | custom-call | flops 786432 | bytes 786432 | tf_op jit(solution)/shard_map/scan_bwd/pallas_call | solution.py:206
  585.5 12.0 %multiply_reduce_fusion.7 = (f32[1536]{0:T(1024)S(1)}, f32[1536]{0:T(1024)S(1)}, f32[1536]{0:T(1024)S(1)}, f32[1536]{0:T(1024)S(1)}, f32[1536]{0:T(1024)S(1)}, /*index=5*/bf16[2,256,1536]{2,1,0:T(8,128)(2,1)S(1)}) fusion(f32[2,256,1536]{2,1,0:T(8,128)} %copy-done.71, f32[2,264,1536]{2,1,0:T(8,128)} %copy-done.28, f32[1536]{0:T(1024)S(1)} %copy-done.112, ...), kind=kLoop, calls=%fused_computation.75 | loop fusion | flops 15720960 | bytes 17455104 | tf_op jit(solution)/shard_map/reduce_sum | solution.py:693
  629.6 17.8 %collective-permute-done.24 = bf16[8,1,1,24,2048]{4,3,2,1,0:T(8,128)(2,1)S(1)} collective-permute-done((bf16[8,1,1,24,2048]{4,3,2,1,0:T(8,128)(2,1)S(1)}, bf16[8,1,1,24,2048]{4,3,2,1,0:T(8,128)(2,1)S(1)}, u32[]{:S(2)}, u32[]{:S(2)}) %collective-permute-start.24) | collective-permute-done | bytes 786464 | tf_op jit(solution)/shard_map/ppermute | solution.py:344
  648.6 5.9 all-to-all-start.6
  666.2 8.9 %all-to-all-done.6 = bf16[8,1,1,24,2048]{4,3,2,1,0:T(8,128)(2,1)} async-done(((bf16[8,1,1,24,2048]{4,3,2,1,0:T(8,128)(2,1)}), bf16[8,1,1,24,2048]{4,3,2,1,0:T(8,128)(2,1)}, u32[]{:S(2)}, u32[]{:S(2)}) %all-to-all-start.6) | async-done | bytes 786464 | tf_op jit(solution)/shard_map/all_to_all | solution.py:377
  (678 shorter events, 338.7 us)
Async XLA Ops:
  16.9 45.5 %collective-permute-start.2 = (bf16[4,8,768]{2,1,0:T(8,128)(2,1)S(1)}, bf16[4,8,768]{2,1,0:T(8,128)(2,1)S(1)}, u32[]{:S(2)}, u32[]{:S(2)}) collective-permute-start(bf16[4,8,768]{2,1,0:T(8,128)(2,1)S(1)} %slice.304), channel_id=1, source_target_pairs={{0,1},{1,2},{2,3},{4,5},{5,6},{6,7},{8,9},{9,10},{10,11},{12,13},{... | collective-permute-start | bytes 147464 | tf_op jit(solution)/shard_map/ppermute | solution.py:349
  33.8 91.8 %all-gather.2.cloned.1.call-start = ((), (), s32[]{:S(2)}) async-start(), calls=%async_computation.8 | async-start | bytes 4866048 | tf_op jit(solution)/shard_map/all_gather | solution.py:534
  147.1 49.9 %all-to-all-start.2 = ((bf16[8,2,40,1536]{3,2,1,0:T(8,128)(2,1)}), bf16[8,2,40,1536]{3,2,1,0:T(8,128)(2,1)}, u32[]{:S(2)}, u32[]{:S(2)}) async-start(bf16[8,2,40,1536]{3,2,1,0:T(8,128)(2,1)} %bitcast.205), calls=%async_computation.2 | async-start | bytes 3932160 | tf_op jit(solution)/shard_map/all_to_all | solution.py:639
  163.4 20.2 %collective-permute-start.12 = (f32[2,1536]{1,0:T(2,128)S(1)}, f32[2,1536]{1,0:T(2,128)S(1)}, u32[]{:S(2)}, u32[]{:S(2)}) collective-permute-start(f32[2,1536]{1,0:T(2,128)S(1)} %get-tuple-element.236), channel_id=1, source_target_pairs={{0,1},{1,0},{2,3},{3,2},{4,5},{5,4},{6,7},{7,6},{8,9},{9,8},{10,11... | collective-permute-start | bytes 36872 | tf_op jit(solution)/shard_map/ppermute | solution.py:344
  163.4 72.5 %collective-permute-start.9 = (bf16[768,768]{1,0:T(8,128)(2,1)}, bf16[768,768]{1,0:T(8,128)(2,1)}, u32[]{:S(2)}, u32[]{:S(2)}) collective-permute-start(bf16[768,768]{1,0:T(8,128)(2,1)} %bitcast.23.refs_0_), channel_id=1, source_target_pairs={{0,2},{1,3},{2,0},{3,1},{4,6},{5,7},{6,4},{7,5},{8,10},{9,11},{10,... | collective-permute-start | bytes 3538952 | tf_op jit(solution)/shard_map/ppermute | solution.py:344
  227.9 26.7 %collective-permute-start.15 = (bf16[768,768]{1,0:T(8,128)(2,1)}, bf16[768,768]{1,0:T(8,128)(2,1)}, u32[]{:S(2)}, u32[]{:S(2)}) collective-permute-start(bf16[768,768]{1,0:T(8,128)(2,1)} %bitcast.24.refs_4_), channel_id=1, source_target_pairs={{0,2},{1,3},{2,0},{3,1},{4,6},{5,7},{6,4},{7,5},{8,10},{9,11},{10,... | collective-permute-start | bytes 3538952 | tf_op jit(solution)/shard_map/ppermute | solution.py:344
  231.3 49.2 %all-to-all-start.4 = ((bf16[8,2,40,1536]{3,2,1,0:T(8,128)(2,1)}), bf16[8,2,40,1536]{3,2,1,0:T(8,128)(2,1)}, u32[]{:S(2)}, u32[]{:S(2)}) async-start(bf16[8,2,40,1536]{3,2,1,0:T(8,128)(2,1)} %bitcast.206), calls=%async_computation.4 | async-start | bytes 3932160 | tf_op jit(solution)/shard_map/all_to_all | solution.py:639
  235.8 22.9 %collective-permute-start.8 = (bf16[768,768]{1,0:T(8,128)(2,1)}, bf16[768,768]{1,0:T(8,128)(2,1)}, u32[]{:S(2)}, u32[]{:S(2)}) collective-permute-start(bf16[768,768]{1,0:T(8,128)(2,1)} %bitcast.23.refs_0_), channel_id=1, source_target_pairs={{0,1},{1,0},{2,3},{3,2},{4,5},{5,4},{6,7},{7,6},{8,9},{9,8},{10,11... | collective-permute-start | bytes 3538952 | tf_op jit(solution)/shard_map/ppermute | solution.py:344
  235.9 22.8 %collective-permute-start.10 = (bf16[768,768]{1,0:T(8,128)(2,1)}, bf16[768,768]{1,0:T(8,128)(2,1)}, u32[]{:S(2)}, u32[]{:S(2)}) collective-permute-start(bf16[768,768]{1,0:T(8,128)(2,1)} %collective-permute-done.9.refs_2_), channel_id=1, source_target_pairs={{0,1},{1,0},{2,3},{3,2},{4,5},{5,4},{6,7},{7,6},{8,9},{9,8},{10,11... | collective-permute-start | bytes 3538952 | tf_op jit(solution)/shard_map/ppermute | solution.py:344
  236.4 22.3 %collective-permute-start.14 = (bf16[768,768]{1,0:T(8,128)(2,1)}, bf16[768,768]{1,0:T(8,128)(2,1)}, u32[]{:S(2)}, u32[]{:S(2)}) collective-permute-start(bf16[768,768]{1,0:T(8,128)(2,1)} %bitcast.24.refs_4_), channel_id=1, source_target_pairs={{0,1},{1,0},{2,3},{3,2},{4,5},{5,4},{6,7},{7,6},{8,9},{9,8},{10,11... | collective-permute-start | bytes 3538952 | tf_op jit(solution)/shard_map/ppermute | solution.py:344
  280.5 57.7 %all-to-all-start.3 = ((bf16[8,2,40,1536]{3,2,1,0:T(8,128)(2,1)}), bf16[8,2,40,1536]{3,2,1,0:T(8,128)(2,1)}, u32[]{:S(2)}, u32[]{:S(2)}) async-start(bf16[8,2,40,1536]{3,2,1,0:T(8,128)(2,1)} %bitcast.210), calls=%async_computation.3 | async-start | bytes 3932160 | tf_op jit(solution)/shard_map/all_to_all | solution.py:649
  314.0 73.9 %collective-permute-start.25 = (bf16[768,768]{1,0:T(8,128)(2,1)}, bf16[768,768]{1,0:T(8,128)(2,1)}, u32[]{:S(2)}, u32[]{:S(2)}) collective-permute-start(bf16[768,768]{1,0:T(8,128)(2,1)} %fusion.80), channel_id=1, source_target_pairs={{0,1},{1,0},{2,3},{3,2},{4,5},{5,4},{6,7},{7,6},{8,9},{9,8},{10,11... | collective-permute-start | bytes 3538952 | tf_op jit(solution)/shard_map/ppermute | solution.py:344
  318.7 69.2 %collective-permute-start.26 = (bf16[768,768]{1,0:T(8,128)(2,1)}, bf16[768,768]{1,0:T(8,128)(2,1)}, u32[]{:S(2)}, u32[]{:S(2)}) collective-permute-start(bf16[768,768]{1,0:T(8,128)(2,1)} %fusion.83), channel_id=1, source_target_pairs={{0,1},{1,0},{2,3},{3,2},{4,5},{5,4},{6,7},{7,6},{8,9},{9,8},{10,11... | collective-permute-start | bytes 3538952 | tf_op jit(solution)/shard_map/ppermute | solution.py:344
  321.9 69.6 %collective-permute-start.28 = (bf16[768,768]{1,0:T(8,128)(2,1)}, bf16[768,768]{1,0:T(8,128)(2,1)}, u32[]{:S(2)}, u32[]{:S(2)}) collective-permute-start(bf16[768,768]{1,0:T(8,128)(2,1)} %fusion.86), channel_id=1, source_target_pairs={{0,1},{1,0},{2,3},{3,2},{4,5},{5,4},{6,7},{7,6},{8,9},{9,8},{10,11... | collective-permute-start | bytes 3538952 | tf_op jit(solution)/shard_map/ppermute | solution.py:344
  325.0 66.5 %collective-permute-start.29 = (bf16[768,768]{1,0:T(8,128)(2,1)}, bf16[768,768]{1,0:T(8,128)(2,1)}, u32[]{:S(2)}, u32[]{:S(2)}) collective-permute-start(bf16[768,768]{1,0:T(8,128)(2,1)} %fusion.89), channel_id=1, source_target_pairs={{0,1},{1,0},{2,3},{3,2},{4,5},{5,4},{6,7},{7,6},{8,9},{9,8},{10,11... | collective-permute-start | bytes 3538952 | tf_op jit(solution)/shard_map/ppermute | solution.py:344
  338.2 74.2 %all-to-all-start.5 = ((bf16[8,2,40,1536]{3,2,1,0:T(8,128)(2,1)}), bf16[8,2,40,1536]{3,2,1,0:T(8,128)(2,1)}, u32[]{:S(2)}, u32[]{:S(2)}) async-start(bf16[8,2,40,1536]{3,2,1,0:T(8,128)(2,1)} %bitcast.209), calls=%async_computation.5 | async-start | bytes 3932160 | tf_op jit(solution)/shard_map/all_to_all | solution.py:649
  344.3 335.6 %reduce-scatter.4.cloned.1.call-start = ((), (), s32[]{:S(2)}) async-start(), calls=%async_computation.9 | async-start | bytes 5068800
  387.9 93.9 %collective-permute-start.17 = (bf16[2,16,1536]{2,1,0:T(8,128)(2,1)}, bf16[2,16,1536]{2,1,0:T(8,128)(2,1)}, u32[]{:S(2)}, u32[]{:S(2)}) collective-permute-start(bf16[2,16,1536]{2,1,0:T(8,128)(2,1)} %convert_element_type.385), channel_id=1, source_target_pairs={{0,1},{1,0},{2,3},{3,2},{4,5},{5,4},{6,7},{7,6},{8,9},{9,8},{10,11... | collective-permute-start | bytes 294920 | tf_op jit(solution)/shard_map/ppermute | solution.py:344
  390.7 263.8 %collective-permute-start.27 = (bf16[768,768]{1,0:T(8,128)(2,1)}, bf16[768,768]{1,0:T(8,128)(2,1)}, u32[]{:S(2)}, u32[]{:S(2)}) collective-permute-start(bf16[768,768]{1,0:T(8,128)(2,1)} %add_convert_fusion.1), channel_id=1, source_target_pairs={{0,2},{1,3},{2,0},{3,1},{4,6},{5,7},{6,4},{7,5},{8,10},{9,11},{10,... | collective-permute-start | bytes 3538952 | tf_op jit(solution)/shard_map/ppermute | solution.py:344
  394.0 260.4 %collective-permute-start.30 = (bf16[768,768]{1,0:T(8,128)(2,1)}, bf16[768,768]{1,0:T(8,128)(2,1)}, u32[]{:S(2)}, u32[]{:S(2)}) collective-permute-start(bf16[768,768]{1,0:T(8,128)(2,1)} %add_convert_fusion), channel_id=1, source_target_pairs={{0,2},{1,3},{2,0},{3,1},{4,6},{5,7},{6,4},{7,5},{8,10},{9,11},{10,... | collective-permute-start | bytes 3538952 | tf_op jit(solution)/shard_map/ppermute | solution.py:344
  456.8 25.0 %collective-permute-start.20 = (bf16[2,16,1536]{2,1,0:T(8,128)(2,1)}, bf16[2,16,1536]{2,1,0:T(8,128)(2,1)}, u32[]{:S(2)}, u32[]{:S(2)}) collective-permute-start(bf16[2,16,1536]{2,1,0:T(8,128)(2,1)} %convert_element_type.396), channel_id=1, source_target_pairs={{0,1},{1,0},{2,3},{3,2},{4,5},{5,4},{6,7},{7,6},{8,9},{9,8},{10,11... | collective-permute-start | bytes 294920 | tf_op jit(solution)/shard_map/ppermute | solution.py:344
  576.6 24.8 %collective-permute-start.22 = (f32[2,8,1536]{2,1,0:T(8,128)S(1)}, f32[2,8,1536]{2,1,0:T(8,128)S(1)}, u32[]{:S(2)}, u32[]{:S(2)}) collective-permute-start(f32[2,8,1536]{2,1,0:T(8,128)S(1)} %slice.436), channel_id=1, source_target_pairs={{1,0},{2,1},{3,2},{5,4},{6,5},{7,6},{9,8},{10,9},{11,10},{13,12},{... | collective-permute-start | bytes 294920 | tf_op jit(solution)/shard_map/ppermute | solution.py:349
  627.4 20.0 %collective-permute-start.24 = (bf16[8,1,1,24,2048]{4,3,2,1,0:T(8,128)(2,1)S(1)}, bf16[8,1,1,24,2048]{4,3,2,1,0:T(8,128)(2,1)S(1)}, u32[]{:S(2)}, u32[]{:S(2)}) collective-permute-start(bf16[8,1,1,24,2048]{4,3,2,1,0:T(8,128)(2,1)S(1)} %dynamic-slice_convert_fusion), channel_id=1, source_target_pairs={{0,2},{1,3},{2,0},{3,1},{4,6},{5,7},{6,4},{7,5},{8,10},{9,11},{10,... | collective-permute-start | bytes 2359304 | tf_op jit(solution)/shard_map/ppermute | solution.py:344
  648.6 26.6 %all-to-all-start.6 = ((bf16[8,1,1,24,2048]{4,3,2,1,0:T(8,128)(2,1)}), bf16[8,1,1,24,2048]{4,3,2,1,0:T(8,128)(2,1)}, u32[]{:S(2)}, u32[]{:S(2)}) async-start(bf16[8,1,1,24,2048]{4,3,2,1,0:T(8,128)(2,1)} %add_convert_fusion.2), calls=%async_computation.6 | async-start | bytes 1572864 | tf_op jit(solution)/shard_map/all_to_all | solution.py:377
  (210 other events, 1540.3 us)
Sparse Core Ops, SparseCore 0:
  38.1 65.6 all-gather.1
  480.5 104.8 reduce-scatter.3

commit v3 on v2

--- a/solution.py
+++ b/solution.py
@@ -20,6 +20,7 @@
 CB = 512
 CE = 768
 VM = 48 << 20
+EXPERT_VM = 48 << 20
 COST = 1
 LOG2E = 1.0 / math.log(2.0)
 LN2 = math.log(2.0)
@@ -141,8 +142,8 @@
     )(s,x,bt,l,r,h0)
 
 
-def bwd_kernel(chunks, s_ref, x_ref, g_ref, bt_ref, l_ref, one_ref, r_ref, h0_ref, m0_ref, h_ref,
-               pull_ref, gs_ref, alog_ref, gi_ref, lam_e, fr_e, lam_o, fr_o):
+def bwd_kernel(chunks, s_ref, x_ref, g_ref, bt_ref, l_ref, one_ref, r_ref, k_ref, h0_ref, m0_ref, h_ref,
+               pre_ref, base_ref, bias_ref, alog_ref, gi_ref, lam_e, fr_e, lam_o, fr_o):
     r = r_ref[...]
     width = r.shape[1]
     j = pl.program_id(1)
@@ -152,18 +153,28 @@
     @pl.when(j==0)
     def _():
         gi_ref[...]=jnp.zeros_like(gi_ref)
+    bias_ref[...] = jnp.zeros_like(bias_ref)
     lam_o[...] = jnp.zeros_like(lam_o)
     fr_o[...] = jnp.zeros_like(fr_o)
     def sums(c, lam_s, fr_s, first=None):
         rows = rows_at(c,U)
-        d8 = (x_ref[0, rows, :].astype(F32)*s_ref[0, rows, :]).astype(BF)
+        s8 = s_ref[0, rows, :]
+        x8 = x_ref[0, rows, :].astype(F32)
+        d8 = (x8*s8).astype(BF)
         lam_all = lam_s[...]
-        pull_ref[0, rows, :] = jnp.dot(l_ref[0, rows, :], lam_all, preferred_element_type=F32)
-        gs_ref[0, rows, :] = jnp.dot(one_ref[...], fr_s[...], preferred_element_type=F32)
+        pull = jnp.dot(l_ref[0, rows, :], lam_all, preferred_element_type=F32)
+        gs = jnp.dot(one_ref[...], fr_s[...], preferred_element_type=F32)
+        slope = jnp.where(s8 < 0.03, s8*(1.0-s8*(0.5-s8*(1.0/6.0))), 1.0-jnp.exp(-s8))
+        arg = (gs*LN2 + x8*pull)*slope
+        pre_ref[0, rows, :] = arg.astype(BF)
+        base_ref[0, rows, :] = k_ref[...]*g_ref[0, rows, :] + s8*pull
+        part = arg[:8]+arg[8:]
         gi = lax.dot_general(d8, lam_all, nt, preferred_element_type=F32)
         if first is not None:
             gi = jnp.where(first, 0.0, gi)
+            part = jnp.where(first, 0.0, part)
         gi_ref[0, rows, :] += gi
+        bias_ref[0] += part
     def chunk(c, carry, mine, other, first=None):
         lam_c, alog = carry
         sums(jnp.minimum(c+1,chunks-1), *other, first)
@@ -197,7 +208,7 @@
     sums(0, *O)
     alog_ref[0] = alog
 
-def scan_bwd(s, x, g, bt, l, one, r, h0, m0, h):
+def scan_bwd(s, x, g, bt, l, one, r, k, h0, m0, h):
     S,T,C = s.shape
     cb=min(CB,C)
     row=pl.BlockSpec((1,T,cb), lambda i,j:(i,0,j))
@@ -205,14 +216,14 @@
     lo=pl.BlockSpec((1,T,U*STATE),lambda i,j:(i,0,0))
     return pl.pallas_call(functools.partial(bwd_kernel, T//U),
         grid=(S,C//cb),
-        in_specs=[row,row,row,pl.BlockSpec((1,T//U,2*STATE,U),lambda i,j:(i,0,0,0)),lo,pl.BlockSpec((U,U*STATE),lambda i,j:(0,0)),pl.BlockSpec((STATE,cb),lambda i,j:(0,j)),st,st,pl.BlockSpec((1,T*STATE,cb),lambda i,j:(i,0,j))],
-        out_specs=[row,row,st,lo],
-        out_shape=[jax.ShapeDtypeStruct((S,T,C),F32),jax.ShapeDtypeStruct((S,T,C),F32),jax.ShapeDtypeStruct((S,STATE,C),F32),jax.ShapeDtypeStruct((S,T,U*STATE),F32)],
+        in_specs=[row,row,row,pl.BlockSpec((1,T//U,2*STATE,U),lambda i,j:(i,0,0,0)),lo,pl.BlockSpec((U,U*STATE),lambda i,j:(0,0)),pl.BlockSpec((STATE,cb),lambda i,j:(0,j)),pl.BlockSpec((1,cb),lambda i,j:(0,j)),st,st,pl.BlockSpec((1,T*STATE,cb),lambda i,j:(i,0,j))],
+        out_specs=[row,row,pl.BlockSpec((1,8,cb),lambda i,j:(i,0,j)),st,lo],
+        out_shape=[jax.ShapeDtypeStruct((S,T,C),BF),jax.ShapeDtypeStruct((S,T,C),F32),jax.ShapeDtypeStruct((S,8,C),F32),jax.ShapeDtypeStruct((S,STATE,C),F32),jax.ShapeDtypeStruct((S,T,U*STATE),F32)],
         scratch_shapes=[pltpu.VMEM((U*STATE,cb),BF)]*4,
         compiler_params=pltpu.CompilerParams(vmem_limit_bytes=VM),
         cost_estimate=pl.CostEstimate(flops=COST*S*T*C,bytes_accessed=COST*S*T*C,transcendentals=0),
         name="scan_bwd",
-    )(s,x,g,bt,l,one,r,h0,m0,h)
+    )(s,x,g,bt,l,one,r,k,h0,m0,h)
 
 
 def gelu_and_slope(x):
@@ -224,14 +235,19 @@
     return x * half, slope
 
 
-def expert_kernel(pieces, tile, x_ref, *refs):
-    w_refs = refs[: 2 * pieces]
+def expert_kernel(pieces, tile, second_at, x_ref, f_ref, w_ref, *refs):
     back_ref, value_ref, grad_ref, first_s, second_s, out_s, gin_s, sems = refs[-8:]
     j = pl.program_id(0)
     rows, width = out_s.shape
+    hidden = first_s.shape[2]
     copies = [
-        pltpu.make_async_copy(w_refs[q], (first_s if q < pieces else second_s).at[q % pieces], sems.at[q])
-        for q in range(2 * pieces)
+        pltpu.make_async_copy(f_ref.at[q, pl.ds(0, width), :], first_s.at[q], sems.at[q])
+        for q in range(pieces)
+    ] + [
+        pltpu.make_async_copy(
+            w_ref.at[q, pl.ds(second_at, hidden), :], second_s.at[q], sems.at[pieces + q]
+        )
+        for q in range(pieces)
     ]
 
     @pl.when(j == 0)
@@ -279,20 +295,19 @@
         back_ref[:, width:] = gin_s[...].astype(BF)
 
 
-def expert_call(x, firsts, seconds, part, groups, shared):
+def expert_call(x, firsts, seconds, second_at, part, groups, shared):
     rows, width = x.shape[0], x.shape[1] // 2
-    pieces = len(firsts)
-    quarter = firsts[0].shape[1]
+    pieces, _, quarter = firsts.shape
     tile = math.gcd(rows, 320)
     wide = pl.BlockSpec((rows, quarter), lambda j: (part, j))
     anywhere = pl.BlockSpec(memory_space=pl.ANY)
     whole = pl.BlockSpec((rows, 2 * width), lambda j: (0, 0))
     big = jax.ShapeDtypeStruct((groups * rows, pieces * quarter), BF)
-    count = 1 + 2 * pieces
+    count = 3
     return pl.pallas_call(
-        functools.partial(expert_kernel, pieces, tile),
+        functools.partial(expert_kernel, pieces, tile, second_at),
         grid=(pieces,),
-        in_specs=[whole] + [anywhere] * (2 * pieces + len(shared)),
+        in_specs=[whole] + [anywhere] * (2 + len(shared)),
         out_specs=[whole, wide, wide],
         out_shape=[jax.ShapeDtypeStruct((rows, 2 * width), BF), big, big],
         scratch_shapes=[
@@ -303,14 +318,12 @@
             pltpu.SemaphoreType.DMA((2 * pieces,)),
         ],
         input_output_aliases={count: 1, count + 1: 2} if shared else {},
-        compiler_params=pltpu.CompilerParams(vmem_limit_bytes=VM),
+        compiler_params=pltpu.CompilerParams(vmem_limit_bytes=EXPERT_VM),
         cost_estimate=pl.CostEstimate(
-            flops=8 * rows * width * quarter * pieces,
-            bytes_accessed=4 * pieces * width * quarter + 16 * rows * width,
-            transcendentals=rows * quarter * pieces,
+            flops=COST * rows * width, bytes_accessed=COST * rows * width, transcendentals=0
         ),
         name="expert",
-    )(x, *firsts, *seconds, *shared)
+    )(x, firsts, seconds, *shared)
 
 
 def own_rows(span):
@@ -385,32 +398,13 @@
     return mine + swap(theirs, "seq", k).astype(F32)
 
 
-def scatter_sum(x):
+def sum_over_seq(x):
     bits = bits_of("seq")
     rows = x.shape[0] // (lax.axis_size("batch") << bits)
     out = x.reshape((lax.axis_size("batch"),) + (2,) * bits + (rows,) + x.shape[1:])
     for k in range(bits):
         out = halved(out, k, bits - k)
-    return over_batch(out).reshape((rows,) + x.shape[1:])
-
-
-def gather_seq(x, event):
-    parts = [x]
-    for k in reversed(range(bits_of("seq"))):
-        more = [swap(p, "seq", k) for p in parts]
-        parts = parts + (after(more, event) if k else more)
-    count = len(parts)
-    order = []
-    for k in reversed(range(bits_of("seq"))):
-        order = (order or [0]) + [o ^ (1 << k) for o in (order or [0])]
-    return [parts[order.index(j)] for j in range(count)]
-
-
-def scatter_seq(parts, k, event):
-    bit = 1 << k
-    moved = {j ^ bit: swap(p.astype(BF), "seq", k) for j, p in parts.items() if j & bit}
-    moved = after(moved, event)
-    return {j: p + moved[j].astype(F32) for j, p in parts.items() if not j & bit}
+    return out.reshape((lax.axis_size("batch"), rows) + x.shape[1:])
 
 
 def totals_of(total):
@@ -476,6 +470,16 @@
 
 def rms(x):
     return lax.rsqrt(jnp.mean(x * x, axis=-1, keepdims=True) + EPSILON)
+
+
+def side_by_side(x, rows):
+    x = x.reshape(-1, 2, rows, x.shape[1])
+    return jnp.swapaxes(x, 1, 2).reshape(-1, 2 * x.shape[3])
+
+
+def one_below(x, rows):
+    x = x.reshape(-1, rows, 2, x.shape[1] // 2)
+    return jnp.swapaxes(x, 1, 2).reshape(-1, x.shape[3])
 
 
 def pad_cols(x, width):
@@ -529,11 +533,18 @@
     feat = jnp.concatenate([norm_gain[:, None], moe_gain[:, None], router], axis=1)
     cut = 1024
     first_set = from_batch(in_proj[:, :cut])
-    later = jnp.concatenate([in_proj[:, DI:], out_proj.reshape(rows, 2 * width)], axis=1)
+    later = jnp.concatenate([in_proj[:, DI:], side_by_side(out_proj, rows)], axis=1)
     later = after(later, first_set)
     later = lax.all_gather(later, ("batch", "seq"), axis=0, tiled=True)
     w_gate_in = later[:, :DI]
-    w_back = later[:, DI:].reshape(DI, width)
+    w_back = one_below(later[:, DI:], rows)
+    if expert_in.shape[2] == width:
+        both = jnp.concatenate([expert_in[0], expert_out[0]], axis=0)
+        both = lax.all_gather(after(both, later), "seq", axis=0, tiled=False)
+        expert_weights = both, both, width
+    else:
+        own = after((expert_in[0], expert_out[0]), later)
+        expert_weights = *(lax.all_gather(x, "seq", axis=0, tiled=False) for x in own), 0
     first_set = over_seq(first_set)
     second_set = over_seq(
         from_batch(
@@ -641,11 +652,12 @@
 
     def expert(m, shared):
         p = parts[m]
-        p.rows_in = p.arrived.reshape(batch * size * capacity, 2 * width)
-        p.back, *shared = expert_call(
-            p.rows_in, first_parts, second_parts, m, groups, shared
-        )
+        arrived = after(p.arrived, parts[m - 1].back) if m else p.arrived
+        p.rows_in = arrived.reshape(batch * size * capacity, 2 * width)
+        p.back, *shared = expert_call(p.rows_in, *expert_weights, m, groups, shared)
         back = p.back.reshape(batch, size, capacity, 2 * width)
+        if m:
+            back = after(back, parts[m - 1].returned)
         back = lax.all_to_all(back, "batch", split_axis=0, concat_axis=0, tiled=True)
         p.returned = jnp.swapaxes(back, 0, 1).reshape(size, experts * capacity, 2 * width)
         return shared
@@ -672,21 +684,37 @@
         p.g_skip = jnp.sum(p.grad_mix * p.actf, axis=(0, 1))
 
     def backward_mixer(p):
-        pull, grad_rate, g_log, grad_in_map = scan_bwd(
-            p.step, p.act, p.grad_mix, p.both, p.in_rows, ones, rate, p.init, p.after, p.states
+        grad_pre, base, bias, g_log, grad_in_map = scan_bwd(
+            p.step,
+            p.act,
+            p.grad_mix,
+            p.both,
+            p.in_rows,
+            ones,
+            rate,
+            skip[None],
+            p.init,
+            p.after,
+            p.states,
         )
-        p.pull = pull
         p.g_log = jnp.sum(g_log, axis=0).T * LN2
-        grad_arg = (grad_rate * LN2 + p.actf * pull) * jax.nn.sigmoid(p.step_arg)
-        p.g_step_bias = jnp.sum(grad_arg, axis=(0, 1))
-        grad_pre = grad_arg.astype(BF)
+        p.g_step_bias = jnp.sum(bias, axis=(0, 1))
         p.g_step = tn(grad_pre, p.delta)
         grad_proj = jnp.concatenate(
             [nn(grad_pre, w_step), fold(grad_in_map), fold(p.grad_out_map)], axis=-1
         ).astype(BF)
         p.g_proj = tn(p.act, grad_proj)
-        grad_act = skip * p.grad_mix + p.step * pull + nt(grad_proj, w_proj)
+        grad_act = base + nt(grad_proj, w_proj)
         grad_conv = grad_act * silu_slope(p.conv_out)
+        p.grad_conv = grad_conv
+        rim = shift(grad_conv[:, :HALO, :], "seq", -1)
+        longer = lax.optimization_barrier(jnp.concatenate([grad_conv, rim], axis=1))
+        p.grad_conv_in = sum(
+            longer[:, CONV - 1 - k : CONV - 1 - k + span, :] * taps[k] for k in range(CONV)
+        ).astype(BF)
+
+    def backward_taps(p, event):
+        grad_conv = after(p.grad_conv, event)
         p.g_conv_bias = jnp.sum(grad_conv, axis=(0, 1))
         p.g_taps = jnp.stack(
             [
@@ -695,11 +723,6 @@
             ],
             axis=-1,
         )
-        rim = shift(grad_conv[:, :HALO, :], "seq", -1)
-        longer = jnp.concatenate([grad_conv, rim], axis=1)
-        p.grad_conv_in = sum(
-            longer[:, CONV - 1 - k : CONV - 1 - k + span, :] * taps[k] for k in range(CONV)
-        ).astype(BF)
 
     def backward_input(p):
         grad_normed = nt(p.grad_conv_in, w_conv_in) + nt(p.grad_gate_in, w_gate_in)
@@ -707,10 +730,8 @@
 
     parts = []
     parts.append(forward(0, None, None))
-    first_parts = gather_seq(after(expert_in[0], parts[0].init), parts[0].send)
     for m in range(1, groups):
         parts.append(forward(m, parts[-1].send, parts[-1].arrived))
-    second_parts = gather_seq(after(expert_out[0], parts[-1].init), parts[-1].mixed)
     shared = ()
     for m in range(groups):
         shared = expert(m, shared)
@@ -727,18 +748,16 @@
             jnp.add, [tn(getattr(p, left), getattr(p, right)) for p in parts]
         )
 
-    quarter = expert_in.shape[2]
     rows_in = joined("rows_in")
     rows_in, values, grad_hidden = after((rows_in, values, grad_hidden), parts[-1].back)
-    grad_first = []
-    grad_second = []
-    for q in range(len(first_parts)):
-        at = slice(q * quarter, (q + 1) * quarter)
-        grad_first.append(tn(rows_in[:, :width], grad_hidden[:, at]))
-        grad_second.append(tn(values[:, at], rows_in[:, width:]))
-
-    parts[0].returned = after(parts[0].returned, parts[-1].back)
+    grad_second = tn(values, rows_in[:, width:]).astype(BF)
+    grad_first = tn(grad_hidden, rows_in[:, :width]).astype(BF)
+    products = grad_first, grad_second
+    parts[0].returned = after(parts[0].returned, products)
     backward_router(parts[0])
+    grad_first, grad_second = after(products, parts[0].grad_mix)
+    grad_second = lax.psum_scatter(grad_second, "seq", scatter_dimension=0, tiled=True)
+    grad_first = lax.psum_scatter(grad_first, "seq", scatter_dimension=0, tiled=True)
     for p, earlier in zip(parts[1:], parts):
         p.returned = after(p.returned, earlier.grad_mix)
         backward_router(p)
@@ -746,7 +765,7 @@
     background = jnp.concatenate(
         [
             added_products("normed", "grad_gate_in").astype(BF),
-            added_products("gated", "grad_branch").astype(BF).reshape(-1, 2 * width),
+            side_by_side(added_products("gated", "grad_branch").astype(BF), rows),
             pad_cols(g_feat, 128).astype(BF),
         ],
         axis=1,
@@ -754,14 +773,13 @@
     background = lax.psum_scatter(background, ("batch", "seq"), scatter_dimension=0, tiled=True)
     background = background.astype(F32)
     g_gate_half = background[:, :DI]
-    g_back = background[:, DI : 2 * DI].reshape(-1, width)
+    g_back = one_below(background[:, DI : 2 * DI], rows)
     g_feat = background[:, 2 * DI :]
-    grad_first = dict(enumerate(grad_first))
-    grad_second = dict(enumerate(grad_second))
-    grad_first = scatter_seq(grad_first, 0, parts[0].grad_mix)
-    grad_second = scatter_seq(grad_second, 0, parts[0].grad_mix)
     for p in parts:
         backward_mixer(p)
+    g_conv_half = added_products("normed", "grad_conv_in")
+    for p in parts:
+        backward_taps(p, g_conv_half)
     g_chan = jnp.concatenate(
         [
             added("g_proj"),
@@ -775,19 +793,18 @@
         axis=1,
     )
     g_chan = pad_cols(g_chan, 256).reshape(-1, 512)
-    g_conv_half = added_products("normed", "grad_conv_in")
-    g_rest = scatter_sum(jnp.concatenate([g_conv_half, g_chan], axis=1))
+    g_rest = jnp.concatenate([sum_over_seq(g_conv_half), sum_over_seq(g_chan)], axis=2)
     for p in parts:
-        p.grad_conv_in = after(p.grad_conv_in, g_conv_half)
-    for k in range(1, bits_of("seq")):
-        grad_first = scatter_seq(grad_first, k, g_conv_half)
-        grad_second = scatter_seq(grad_second, k, g_conv_half)
+        p.grad_conv_in = after(p.grad_conv_in, (g_conv_half, background))
+        backward_input(p)
+    grad_first, grad_second = after((grad_first, grad_second), g_conv_half)
+    grad_first = grad_first.astype(F32).T
+    grad_second = grad_second.astype(F32)
+    g_rest = after(g_rest, (parts[0].input_grad, grad_first, grad_second))
+    g_rest = over_batch(g_rest)
+    g_rest = after(g_rest, parts[-1].input_grad)
     g_conv_half = g_rest[:, :DI]
     g_chan = g_rest[:, DI:].reshape(-1, 256)
-    grad_first = grad_first[0]
-    grad_second = grad_second[0]
-    for p in parts:
-        backward_input(p)
     g_in = jnp.concatenate([g_conv_half, g_gate_half], axis=1)
     g_gain_one = jnp.sum(g_in * in_proj.astype(F32), axis=1) / norm_gain.astype(F32)
     at = maps + DT_RANK

time: 701 us -> 675 us (0.963)
  other arithmetic: 95.1 us -> 73.3 us
  matrix products: 151 us -> 139 us
  local copies, waits for them, and re-layouts: 76.6 us -> 85 us
    ppermute x28 -> x18, waiting for transfers between devices: 59.4 us -> 27.1 us  [swap(): return lax.ppermute(x, axis, [(i, i ^ 1 << k) for i in range(count)])]
    all_to_all x2, waiting for transfers between devices: 3.22 us -> 30.8 us  [forward(): lax.all_to_all(send, 'batch', split_axis=0, concat_axis=0, tiled=True)]
    reduce_sum x4, other arithmetic: 24.7 us -> 5.06 us  [the longest x2 3.23 us: backward_taps(): jnp.sum(grad_conv * p.conv_ext[:, lo + k:lo + k + span, :], axis=(0, 1))]
    dot_general x52 -> x46, matrix products: 148 us -> 136 us  [mm(): lax.dot_general(left, right, (dims, ((), ())), preferred_element_type=F32)]
    unnamed x396 -> x407, local copies, waits for them, and re-layouts: 28.8 us -> 39 us
    concatenate x2 -> x6, other arithmetic: 3.25 us -> 10.9 us  [the longest x2 3.48 us: backward_mixer(): longer = lax.optimization_barrier(jnp.concatenate([grad_conv, rim], axis=1))]
    ppermute x28 -> x18, starting transfers between devices: 17.7 us -> 14.3 us  [swap(): return lax.ppermute(x, axis, [(i, i ^ 1 << k) for i in range(count)])]
  transfers between devices with their start and end apart: 40 -> 33, of which waited for: 14 -> 14; matrix products, arithmetic and copies ran while one was open for 39% -> 35% of each run, Pallas kernels for 30% -> 32%
where the time goes in v3:
time: 675 us; the launch traced here: 667 us
  Pallas kernels  213 us (32%)
  matrix products  139 us (21%)
  local copies, waits for them, and re-layouts  85 us (13%)
  waiting for transfers between devices  83.9 us (12%)
  other arithmetic  73.3 us (11%)
  starting transfers between devices  55.3 us (8%)
  between operations  16.8 us (2%)
    dot_general x46, matrix products, mm(): lax.dot_general(left, right, (dims, ((), ())), preferred_element_type=F32)  136 us
    pallas_call x2, Pallas kernels, scan_bwd(): pl.pallas_call(functools.partial(bwd_kernel, T // U), grid=(S, C // cb),...  68.6 us
    pallas_call x2, Pallas kernels, expert_call(): pl.pallas_call(functools.partial(expert_kernel, pieces, tile, second_at),...  43 us
    pallas_call x2, Pallas kernels, scan_end_b(): pl.pallas_call(functools.partial(end_b_kernel, T // U), grid=(S, C // cb)...  40.8 us
    unnamed x407, local copies, waits for them, and re-layouts  39 us
    pallas_call x2, Pallas kernels, scan_fwd(): pl.pallas_call(functools.partial(fwd_kernel, T // U), grid=(S, C // cb),...  36.2 us
    all_to_all x2, waiting for transfers between devices, forward(): lax.all_to_all(send, 'batch', split_axis=0, concat_axis=0, tiled=True)  30.8 us
    ppermute x18, waiting for transfers between devices, swap(): return lax.ppermute(x, axis, [(i, i ^ 1 << k) for i in range(count)])  27.1 us
  transfers between devices with their start and end apart: 33, of which 14 were waited for; matrix products, arithmetic and copies ran while one was open for 35% of the time, Pallas kernels for 32%

profile of v3, /device:TPU:0, one launch (start us, length us, event | category | flops | bytes accessed | tf_op | source)
XLA Modules:
  0.0 666.7 jit_solution(11379532855237943765)
XLA Ops:
  9.0 7.3 %all-to-all-start.1 = ((bf16[8,24,1024]{2,1,0:T(8,128)(2,1)}), bf16[8,24,1024]{2,1,0:T(8,128)(2,1)}, u32[]{:S(2)}, u32[]{:S(2)}) async-start(bf16[8,24,1024]{2,1,0:T(8,128)(2,1)} %broadcast_in_dim.108), calls=%async_computation.1 | async-start | bytes 786432 | tf_op jit(solution)/shard_map/all_to_all | solution.py:378
  38.3 9.5 %all-to-all-done = bf16[8,24,1152]{2,1,0:T(8,128)(2,1)} async-done(((bf16[8,24,1152]{2,1,0:T(8,128)(2,1)}), bf16[8,24,1152]{2,1,0:T(8,128)(2,1)}, u32[]{:S(2)}, u32[]{:S(2)}) %all-to-all-start) | async-done | bytes 442400 | tf_op jit(solution)/shard_map/all_to_all | solution.py:378
  53.8 6.4 collective-permute-done
  83.4 12.3 %scan_end_f.2 = f32[2,16,1536]{2,1,0:T(8,128)S(1)} custom-call(f32[2,256,1536]{2,1,0:T(8,128)S(1)} %copy-done, bf16[2,256,1536]{2,1,0:T(8,128)(2,1)S(1)} %get-tuple-element.228.x_ref, f32[2,16,32,16]{3,2,1,0:T(8,128)S(1)} %bitcast.214, f32[16,1536]{1,0:T(8,128)S(1)} %get-tuple-element.249.r_ref), custom_call_target="tpu_custom_call" | custom-call | flops 786432 | bytes 786432 | tf_op jit(solution)/shard_map/scan_end_f/pallas_call | solution.py:51
  104.5 18.2 %scan_fwd.2 = (f32[2,256,1536]{2,1,0:T(8,128)S(1)}, bf16[2,4096,1536]{2,1,0:T(8,128)(2,1)}) custom-call(f32[2,256,1536]{2,1,0:T(8,128)} %get-tuple-element.277.s_ref, bf16[2,256,1536]{2,1,0:T(8,128)(2,1)S(1)} %get-tuple-element.228.x_ref, f32[2,16,32,16]{3,2,1,0:T(8,128)S(1)} %bitcast.215, bf16[2,256,256]{2,1,0:T(8,128)(2,1)S(1)} %fusion.48.l_ref, ...), custom_call_target="tpu_custom_call" | custom-call | flops 786432 | bytes 786432 | tf_op jit(solution)/shard_map/scan_fwd/pallas_call | solution.py:133
  125.8 6.0 reshape.542
  147.3 6.6 all-to-all-start.2
  171.7 12.3 %scan_end_f.3 = f32[2,16,1536]{2,1,0:T(8,128)S(1)} custom-call(f32[2,256,1536]{2,1,0:T(8,128)S(1)} %copy-done.2, bf16[2,256,1536]{2,1,0:T(8,128)(2,1)S(1)} %get-tuple-element.224.x_ref, f32[2,16,32,16]{3,2,1,0:T(8,128)S(1)} %bitcast.218, f32[16,1536]{1,0:T(8,128)S(1)} %get-tuple-element.249.r_ref), custom_call_target="tpu_custom_call" | custom-call | flops 786432 | bytes 786432 | tf_op jit(solution)/shard_map/scan_end_f/pallas_call | solution.py:51
  190.8 7.8 %all-to-all-done.2 = bf16[8,2,40,1536]{3,2,1,0:T(8,128)(2,1)} async-done(((bf16[8,2,40,1536]{3,2,1,0:T(8,128)(2,1)}), bf16[8,2,40,1536]{3,2,1,0:T(8,128)(2,1)}, u32[]{:S(2)}, u32[]{:S(2)}) %all-to-all-start.2) | async-done | bytes 1966112 | tf_op jit(solution)/shard_map/all_to_all | solution.py:650
  200.7 18.0 %scan_fwd.3 = (f32[2,256,1536]{2,1,0:T(8,128)S(1)}, bf16[2,4096,1536]{2,1,0:T(8,128)(2,1)}) custom-call(f32[2,256,1536]{2,1,0:T(8,128)} %get-tuple-element.287.s_ref, bf16[2,256,1536]{2,1,0:T(8,128)(2,1)S(1)} %get-tuple-element.224.x_ref, f32[2,16,32,16]{3,2,1,0:T(8,128)S(1)} %bitcast.219, bf16[2,256,256]{2,1,0:T(8,128)(2,1)S(1)} %copy-done.24, ...), custom_call_target="tpu_custom_call" | custom-call | flops 786432 | bytes 786432 | tf_op jit(solution)/shard_map/scan_fwd/pallas_call | solution.py:133
  218.7 6.3 multiply_convert_fusion.2
  237.0 20.8 %expert.2 = (bf16[640,1536]{1,0:T(8,128)(2,1)S(1)}, bf16[1280,3072]{1,0:T(8,128)(2,1)}, bf16[1280,3072]{1,0:T(8,128)(2,1)}) custom-call(bf16[640,1536]{1,0:T(8,128)(2,1)} %bitcast.27.x_ref, bf16[4,1536,768]{2,1,0:T(8,128)(2,1)} %bitcast.224, bf16[4,1536,768]{2,1,0:T(8,128)(2,1)} %bitcast.225), custom_call_target="tpu_custom_call" | custom-call | flops 491520 | bytes 491520 | tf_op jit(solution)/shard_map/expert/pallas_call | solution.py:307
  259.1 22.9 %all-to-all-done.4 = bf16[8,2,40,1536]{3,2,1,0:T(8,128)(2,1)} async-done(((bf16[8,2,40,1536]{3,2,1,0:T(8,128)(2,1)}), bf16[8,2,40,1536]{3,2,1,0:T(8,128)(2,1)}, u32[]{:S(2)}, u32[]{:S(2)}) %all-to-all-start.4) | async-done | bytes 1966112 | tf_op jit(solution)/shard_map/all_to_all | solution.py:650
  288.8 22.2 %expert.3 = (bf16[640,1536]{1,0:T(8,128)(2,1)S(1)}, bf16[1280,3072]{1,0:T(8,128)(2,1)}, bf16[1280,3072]{1,0:T(8,128)(2,1)}) custom-call(bf16[640,1536]{1,0:T(8,128)(2,1)} %bitcast.40.x_ref, bf16[4,1536,768]{2,1,0:T(8,128)(2,1)} %bitcast.226, bf16[4,1536,768]{2,1,0:T(8,128)(2,1)} %bitcast.227, ...), custom_call_target="tpu_custom_call", output_to_operand_aliasing={{1}: (3, {}), {2}: (4, {})} | custom-call | flops 491520 | bytes 491520 | tf_op jit(solution)/shard_map/expert/pallas_call | solution.py:307
  312.3 11.3 %convolution_convert_fusion.1 = bf16[3072,768]{1,0:T(8,128)(2,1)} fusion(bf16[1280,3072]{1,0:T(8,128)(2,1)} %get-tuple-element.74, bf16[1280,1536]{1,0:T(8,128)(2,1)S(1)} %pad_maximum_fusion), kind=kOutput, calls=%fused_computation.7 | convolution fusion | flops 6042157056 | bytes 14548992 | tf_op jit(solution)/shard_map/dot_general | solution.py:442
  323.6 11.1 %convolution_convert_fusion = bf16[3072,768]{1,0:T(8,128)(2,1)} fusion(bf16[1280,3072]{1,0:T(8,128)(2,1)} %get-tuple-element.76, bf16[1280,1536]{1,0:T(8,128)(2,1)} %copy-done.77), kind=kOutput, calls=%fused_computation.6 | convolution fusion | flops 6042157056 | bytes 14548992 | tf_op jit(solution)/shard_map/dot_general | solution.py:442
  348.6 6.3 fusion.9
  368.4 20.3 %scan_end_b.2 = (f32[2,16,1536]{2,1,0:T(8,128)S(1)}, f32[2,256,256]{2,1,0:T(8,128)S(1)}) custom-call(f32[2,256,1536]{2,1,0:T(8,128)S(1)} %copy-done.1, f32[2,256,1536]{2,1,0:T(8,128)} %get-tuple-element.221.g_ref, f32[2,16,32,16]{3,2,1,0:T(8,128)S(1)} %bitcast.216, f32[16,1536]{1,0:T(8,128)S(1)} %get-tuple-element.249.r_ref, ...), custom_call_target="tpu_custom_call" | custom-call | flops 786432 | bytes 786432 | tf_op jit(solution)/shard_map/scan_end_b/pallas_call | solution.py:88
  421.7 6.4 fusion.11
  428.1 20.5 %scan_end_b.3 = (f32[2,16,1536]{2,1,0:T(8,128)S(1)}, f32[2,256,256]{2,1,0:T(8,128)S(1)}) custom-call(f32[2,256,1536]{2,1,0:T(8,128)S(1)} %copy-done.3, f32[2,256,1536]{2,1,0:T(8,128)} %get-tuple-element.219.g_ref, f32[2,16,32,16]{3,2,1,0:T(8,128)S(1)} %bitcast.220, f32[16,1536]{1,0:T(8,128)S(1)} %get-tuple-element.249.r_ref, ...), custom_call_target="tpu_custom_call" | custom-call | flops 786432 | bytes 786432 | tf_op jit(solution)/shard_map/scan_end_b/pallas_call | solution.py:88
  482.2 34.4 %scan_bwd.2 = (bf16[2,256,1536]{2,1,0:T(8,128)(2,1)S(1)}, f32[2,256,1536]{2,1,0:T(8,128)}, f32[2,8,1536]{2,1,0:T(8,128)S(1)}, f32[2,16,1536]{2,1,0:T(8,128)S(1)}, f32[2,256,256]{2,1,0:T(8,128)S(1)}) custom-call(f32[2,256,1536]{2,1,0:T(8,128)} %get-tuple-element.277.s_ref, bf16[2,256,1536]{2,1,0:T(8,128)(2,1)S(1)} %get-tuple-element.228.x_ref, ...), custom_call_target="tpu_custom_call" | custom-call | flops 786432 | bytes 786432 | tf_op jit(solution)/shard_map/scan_bwd/pallas_call | solution.py:217
  524.8 34.2 %scan_bwd.3 = (bf16[2,256,1536]{2,1,0:T(8,128)(2,1)S(1)}, f32[2,256,1536]{2,1,0:T(8,128)}, f32[2,8,1536]{2,1,0:T(8,128)S(1)}, f32[2,16,1536]{2,1,0:T(8,128)S(1)}, f32[2,256,256]{2,1,0:T(8,128)S(1)}) custom-call(f32[2,256,1536]{2,1,0:T(8,128)} %get-tuple-element.287.s_ref, bf16[2,256,1536]{2,1,0:T(8,128)(2,1)S(1)} %get-tuple-element.224.x_ref, ...), custom_call_target="tpu_custom_call" | custom-call | flops 786432 | bytes 786432 | tf_op jit(solution)/shard_map/scan_bwd/pallas_call | solution.py:217
  604.6 12.4 %collective-permute-done.18 = bf16[8,1,1,24,1536]{4,3,2,1,0:T(8,128)(2,1)S(1)} collective-permute-done((bf16[8,1,1,24,1536]{4,3,2,1,0:T(8,128)(2,1)S(1)}, bf16[8,1,1,24,1536]{4,3,2,1,0:T(8,128)(2,1)S(1)}, u32[]{:S(2)}, u32[]{:S(2)}) %collective-permute-start.18) | collective-permute-done | bytes 589856 | tf_op jit(solution)/shard_map/ppermute | solution.py:357
  645.8 9.2 %all-to-all-done.6 = bf16[8,24,2048]{2,1,0:T(8,128)(2,1)S(1)} async-done(((bf16[8,24,2048]{2,1,0:T(8,128)(2,1)}), bf16[8,24,2048]{2,1,0:T(8,128)(2,1)S(1)}, u32[]{:S(2)}, u32[]{:S(2)}) %all-to-all-start.6) | async-done | bytes 786464 | tf_op jit(solution)/shard_map/all_to_all | solution.py:390
  (683 shorter events, 307.2 us)
Async XLA Ops:
  9.0 19.1 %all-to-all-start.1 = ((bf16[8,24,1024]{2,1,0:T(8,128)(2,1)}), bf16[8,24,1024]{2,1,0:T(8,128)(2,1)}, u32[]{:S(2)}, u32[]{:S(2)}) async-start(bf16[8,24,1024]{2,1,0:T(8,128)(2,1)} %broadcast_in_dim.108), calls=%async_computation.1 | async-start | bytes 786432 | tf_op jit(solution)/shard_map/all_to_all | solution.py:378
  16.2 84.6 %all-gather.4.cloned.1.call-start = ((), (), s32[]{:S(2)}) async-start(), calls=%async_computation.10 | async-start | bytes 4866048 | tf_op jit(solution)/shard_map/all_gather | solution.py:538
  28.8 18.9 %all-to-all-start = ((bf16[8,24,1152]{2,1,0:T(8,128)(2,1)}), bf16[8,24,1152]{2,1,0:T(8,128)(2,1)}, u32[]{:S(2)}, u32[]{:S(2)}) async-start(bf16[8,24,1152]{2,1,0:T(8,128)(2,1)} %broadcast_in_dim.105), calls=%async_computation | async-start | bytes 884736 | tf_op jit(solution)/shard_map/all_to_all | solution.py:378
  33.0 204.0 %all-gather.6.cloned.1.call-start = ((), (), s32[]{:S(2)}) async-start(), calls=%async_computation.13 | async-start | bytes 11796480 | tf_op jit(solution)/shard_map/all_gather | solution.py:543
  33.1 28.8 %collective-permute-start.2 = (bf16[4,8,768]{2,1,0:T(8,128)(2,1)S(1)}, bf16[4,8,768]{2,1,0:T(8,128)(2,1)S(1)}, u32[]{:S(2)}, u32[]{:S(2)}) collective-permute-start(bf16[4,8,768]{2,1,0:T(8,128)(2,1)S(1)} %slice.280), channel_id=1, source_target_pairs={{0,1},{1,2},{2,3},{4,5},{5,6},{6,7},{8,9},{9,10},{10,11},{12,13},{... | collective-permute-start | bytes 147464 | tf_op jit(solution)/shard_map/ppermute | solution.py:362
  36.1 16.4 %collective-permute-start.3 = (bf16[8,1,1,24,1024]{4,3,2,1,0:T(8,128)(2,1)}, bf16[8,1,1,24,1024]{4,3,2,1,0:T(8,128)(2,1)S(1)}, u32[]{:S(2)}, u32[]{:S(2)}) collective-permute-start(bf16[8,1,1,24,1024]{4,3,2,1,0:T(8,128)(2,1)} %bitcast.7), channel_id=1, source_target_pairs={{0,2},{1,3},{2,0},{3,1},{4,6},{5,7},{6,4},{7,5},{8,10},{9,11},{10,... | collective-permute-start | bytes 1179656 | tf_op jit(solution)/shard_map/ppermute | solution.py:357
  47.8 12.4 %collective-permute-start = (bf16[8,1,1,24,1152]{4,3,2,1,0:T(8,128)(2,1)}, bf16[8,1,1,24,1152]{4,3,2,1,0:T(8,128)(2,1)}, u32[]{:S(2)}, u32[]{:S(2)}) collective-permute-start(bf16[8,1,1,24,1152]{4,3,2,1,0:T(8,128)(2,1)} %bitcast.5), channel_id=1, source_target_pairs={{0,2},{1,3},{2,0},{3,1},{4,6},{5,7},{6,4},{7,5},{8,10},{9,11},{10,... | collective-permute-start | bytes 1327112 | tf_op jit(solution)/shard_map/ppermute | solution.py:357
  53.7 8.5 %collective-permute-start.4 = (bf16[8,2,1,24,1024]{4,3,2,1,0:T(8,128)(2,1)S(1)}, bf16[8,2,1,24,1024]{4,3,2,1,0:T(8,128)(2,1)S(1)}, u32[]{:S(2)}, u32[]{:S(2)}) collective-permute-start(bf16[8,2,1,24,1024]{4,3,2,1,0:T(8,128)(2,1)S(1)} %maximum_select_fusion.3), channel_id=1, source_target_pairs={{0,1},{1,0},{2,3},{3,2},{4,5},{5,4},{6,7},{7,6},{8,9},{9,8},{10,11... | collective-permute-start | bytes 2359304 | tf_op jit(solution)/shard_map/ppermute | solution.py:357
  80.7 15.6 %collective-permute-start.6 = (f32[2,1536]{1,0:T(2,128)S(1)}, f32[2,1536]{1,0:T(2,128)}, u32[]{:S(2)}, u32[]{:S(2)}) collective-permute-start(f32[2,1536]{1,0:T(2,128)S(1)} %get-tuple-element.276), channel_id=1, source_target_pairs={{0,1},{1,0},{2,3},{3,2},{4,5},{5,4},{6,7},{7,6},{8,9},{9,8},{10,11... | collective-permute-start | bytes 36872 | tf_op jit(solution)/shard_map/ppermute | solution.py:357
  147.3 51.4 %all-to-all-start.2 = ((bf16[8,2,40,1536]{3,2,1,0:T(8,128)(2,1)}), bf16[8,2,40,1536]{3,2,1,0:T(8,128)(2,1)}, u32[]{:S(2)}, u32[]{:S(2)}) async-start(bf16[8,2,40,1536]{3,2,1,0:T(8,128)(2,1)} %bitcast.242), calls=%async_computation.2 | async-start | bytes 3932160 | tf_op jit(solution)/shard_map/all_to_all | solution.py:650
  164.4 20.2 %collective-permute-start.9 = (f32[2,1536]{1,0:T(2,128)S(1)}, f32[2,1536]{1,0:T(2,128)S(1)}, u32[]{:S(2)}, u32[]{:S(2)}) collective-permute-start(f32[2,1536]{1,0:T(2,128)S(1)} %get-tuple-element.286), channel_id=1, source_target_pairs={{0,1},{1,0},{2,3},{3,2},{4,5},{5,4},{6,7},{7,6},{8,9},{9,8},{10,11... | collective-permute-start | bytes 36872 | tf_op jit(solution)/shard_map/ppermute | solution.py:357
  232.4 49.5 %all-to-all-start.4 = ((bf16[8,2,40,1536]{3,2,1,0:T(8,128)(2,1)}), bf16[8,2,40,1536]{3,2,1,0:T(8,128)(2,1)}, u32[]{:S(2)}, u32[]{:S(2)}) async-start(bf16[8,2,40,1536]{3,2,1,0:T(8,128)(2,1)} %bitcast.243), calls=%async_computation.4 | async-start | bytes 3932160 | tf_op jit(solution)/shard_map/all_to_all | solution.py:650
  282.0 52.7 %all-to-all-start.3 = ((bf16[8,2,40,1536]{3,2,1,0:T(8,128)(2,1)}), bf16[8,2,40,1536]{3,2,1,0:T(8,128)(2,1)}, u32[]{:S(2)}, u32[]{:S(2)}) async-start(bf16[8,2,40,1536]{3,2,1,0:T(8,128)(2,1)} %bitcast.223), calls=%async_computation.3 | async-start | bytes 3932160 | tf_op jit(solution)/shard_map/all_to_all | solution.py:661
  286.3 331.8 %reduce-scatter.6.cloned.1.call-start = ((), (), s32[]{:S(2)}) async-start(), calls=%async_computation.11 | async-start | bytes 5898240 | tf_op jit(solution)/shard_map/reduce_scatter | solution.py:760
  355.0 263.2 %reduce-scatter.8.cloned.1.call-start = ((), (), s32[]{:S(2)}) async-start(), calls=%async_computation.12 | async-start | bytes 5898240 | tf_op jit(solution)/shard_map/reduce_scatter | solution.py:759
  355.6 50.4 %all-to-all-start.5 = ((bf16[8,2,40,1536]{3,2,1,0:T(8,128)(2,1)}), bf16[8,2,40,1536]{3,2,1,0:T(8,128)(2,1)}, u32[]{:S(2)}, u32[]{:S(2)}) async-start(bf16[8,2,40,1536]{3,2,1,0:T(8,128)(2,1)} %bitcast.222), calls=%async_computation.5 | async-start | bytes 3932160 | tf_op jit(solution)/shard_map/all_to_all | solution.py:661
  361.5 263.4 %reduce-scatter.10.cloned.1.call-start = ((), (), s32[]{:S(2)}) async-start(), calls=%async_computation.14 | async-start | bytes 5068800
  390.1 79.3 %collective-permute-start.11 = (bf16[2,16,1536]{2,1,0:T(8,128)(2,1)}, bf16[2,16,1536]{2,1,0:T(8,128)(2,1)}, u32[]{:S(2)}, u32[]{:S(2)}) collective-permute-start(bf16[2,16,1536]{2,1,0:T(8,128)(2,1)} %convert_element_type.381), channel_id=1, source_target_pairs={{0,1},{1,0},{2,3},{3,2},{4,5},{5,4},{6,7},{7,6},{8,9},{9,8},{10,11... | collective-permute-start | bytes 294920 | tf_op jit(solution)/shard_map/ppermute | solution.py:357
  450.7 18.8 %collective-permute-start.14 = (bf16[2,16,1536]{2,1,0:T(8,128)(2,1)}, bf16[2,16,1536]{2,1,0:T(8,128)(2,1)}, u32[]{:S(2)}, u32[]{:S(2)}) collective-permute-start(bf16[2,16,1536]{2,1,0:T(8,128)(2,1)} %convert_element_type.391), channel_id=1, source_target_pairs={{0,1},{1,0},{2,3},{3,2},{4,5},{5,4},{6,7},{7,6},{8,9},{9,8},{10,11... | collective-permute-start | bytes 294920 | tf_op jit(solution)/shard_map/ppermute | solution.py:357
  523.5 48.2 %collective-permute-start.13 = (f32[2,8,1536]{2,1,0:T(8,128)}, f32[2,8,1536]{2,1,0:T(8,128)}, u32[]{:S(2)}, u32[]{:S(2)}) collective-permute-start(f32[2,8,1536]{2,1,0:T(8,128)} %slice.399), channel_id=1, source_target_pairs={{1,0},{2,1},{3,2},{5,4},{6,5},{7,6},{9,8},{10,9},{11,10},{13,12},{... | collective-permute-start | bytes 294920 | tf_op jit(solution)/shard_map/ppermute | solution.py:362
  565.4 8.7 %collective-permute-start.16 = (f32[2,8,1536]{2,1,0:T(8,128)}, f32[2,8,1536]{2,1,0:T(8,128)}, u32[]{:S(2)}, u32[]{:S(2)}) collective-permute-start(f32[2,8,1536]{2,1,0:T(8,128)} %slice.406), channel_id=1, source_target_pairs={{1,0},{2,1},{3,2},{5,4},{6,5},{7,6},{9,8},{10,9},{11,10},{13,12},{... | collective-permute-start | bytes 294920 | tf_op jit(solution)/shard_map/ppermute | solution.py:362
  584.3 14.4 %collective-permute-start.17 = (bf16[8,2,1,24,1536]{4,3,2,1,0:T(8,128)(2,1)}, bf16[8,2,1,24,1536]{4,3,2,1,0:T(8,128)(2,1)}, u32[]{:S(2)}, u32[]{:S(2)}) collective-permute-start(bf16[8,2,1,24,1536]{4,3,2,1,0:T(8,128)(2,1)} %dynamic-slice_convert_fusion), channel_id=1, source_target_pairs={{0,1},{1,0},{2,3},{3,2},{4,5},{5,4},{6,7},{7,6},{8,9},{9,8},{10,11... | collective-permute-start | bytes 3538952 | tf_op jit(solution)/shard_map/ppermute | solution.py:357
  600.5 16.5 %collective-permute-start.18 = (bf16[8,1,1,24,1536]{4,3,2,1,0:T(8,128)(2,1)S(1)}, bf16[8,1,1,24,1536]{4,3,2,1,0:T(8,128)(2,1)S(1)}, u32[]{:S(2)}, u32[]{:S(2)}) collective-permute-start(bf16[8,1,1,24,1536]{4,3,2,1,0:T(8,128)(2,1)S(1)} %dynamic-slice_convert_fusion.1), channel_id=1, source_target_pairs={{0,2},{1,3},{2,0},{3,1},{4,6},{5,7},{6,4},{7,5},{8,10},{9,11},{10,... | collective-permute-start | bytes 1769480 | tf_op jit(solution)/shard_map/ppermute | solution.py:357
  630.7 24.3 %all-to-all-start.6 = ((bf16[8,24,2048]{2,1,0:T(8,128)(2,1)}), bf16[8,24,2048]{2,1,0:T(8,128)(2,1)S(1)}, u32[]{:S(2)}, u32[]{:S(2)}) async-start(bf16[8,24,2048]{2,1,0:T(8,128)(2,1)} %pad_maximum_fusion.6), calls=%async_computation.8 | async-start | bytes 1572864 | tf_op jit(solution)/shard_map/all_to_all | solution.py:390
  (208 other events, 2324.1 us)
Sparse Core Ops, SparseCore 0:
  28.1 64.8 all-gather.3
  100.9 64.5 all-gather.5
  355.1 49.0 reduce-scatter.5
  406.8 47.8 reduce-scatter.7
  476.7 105.1 reduce-scatter.9

commit v4 on v3

--- a/solution.py
+++ b/solution.py
@@ -473,13 +473,15 @@
 
 
 def side_by_side(x, rows):
-    x = x.reshape(-1, 2, rows, x.shape[1])
-    return jnp.swapaxes(x, 1, 2).reshape(-1, 2 * x.shape[3])
+    width = x.shape[1]
+    x = x.reshape(-1, 2, rows, width)
+    return jnp.concatenate([x[:, h].reshape(-1, width) for h in range(2)], axis=1)
 
 
 def one_below(x, rows):
-    x = x.reshape(-1, rows, 2, x.shape[1] // 2)
-    return jnp.swapaxes(x, 1, 2).reshape(-1, x.shape[3])
+    width = x.shape[1] // 2
+    halves = [x[:, h * width : (h + 1) * width].reshape(-1, rows, width) for h in range(2)]
+    return jnp.concatenate(halves, axis=1).reshape(-1, width)
 
 
 def pad_cols(x, width):
@@ -531,8 +533,7 @@
         axis=1,
     )
     feat = jnp.concatenate([norm_gain[:, None], moe_gain[:, None], router], axis=1)
-    cut = 1024
-    first_set = from_batch(in_proj[:, :cut])
+    first_set = from_batch(in_proj[:, :DI])
     later = jnp.concatenate([in_proj[:, DI:], side_by_side(out_proj, rows)], axis=1)
     later = after(later, first_set)
     later = lax.all_gather(later, ("batch", "seq"), axis=0, tiled=True)
@@ -548,15 +549,12 @@
     first_set = over_seq(first_set)
     second_set = over_seq(
         from_batch(
-            jnp.concatenate(
-                [in_proj[:, cut:DI], pad_cols(chan, 256).reshape(rows, 512), pad_cols(feat, 128)],
-                axis=1,
-            )
+            jnp.concatenate([pad_cols(chan, 256).reshape(rows, 512), pad_cols(feat, 128)], axis=1)
         )
     )
-    w_conv_in = jnp.concatenate([first_set, second_set[:, : DI - cut]], axis=1)
-    chan = second_set[:, DI - cut : DI - cut + 512].reshape(-1, 256)
-    feat = second_set[:, DI - cut + 512 :]
+    w_conv_in = first_set
+    chan = second_set[:, :512].reshape(-1, 256)
+    feat = second_set[:, 512:]
     gain_one = feat[:, 0].astype(F32)
     gain_two = feat[:, 1].astype(F32)
     router_weight = feat[:, 2 : 2 + experts]

time: 675 us -> 670 us (level)
  waiting for transfers between devices: 83.9 us -> 92.7 us
  local copies, waits for them, and re-layouts: 85 us -> 76.6 us
    ppermute x18, waiting for transfers between devices: 27.1 us -> 38.2 us  [swap(): return lax.ppermute(x, axis, [(i, i ^ 1 << k) for i in range(count)])]
    reshape x5 -> x2, local copies, waits for them, and re-layouts: 10.7 us -> 1.36 us  [the longest x1 1.35 us: shards(): chan = second_set[:, :512].reshape(-1, 256)]
    unnamed x407 -> x403, local copies, waits for them, and re-layouts: 39 us -> 43.1 us
  transfers between devices with their start and end apart: 33 -> 33, of which waited for: 14 -> 14; matrix products, arithmetic and copies ran while one was open for 35% -> 33% of each run, Pallas kernels for 32% -> 32%
where the time goes in v4:
time: 670 us; the launch traced here: 659 us
  Pallas kernels  214 us (32%)
  matrix products  138 us (21%)
  waiting for transfers between devices  92.7 us (14%)
  local copies, waits for them, and re-layouts  76.6 us (11%)
  other arithmetic  69.3 us (10%)
  starting transfers between devices  52.5 us (8%)
  between operations  16.8 us (3%)
    dot_general x46, matrix products, mm(): lax.dot_general(left, right, (dims, ((), ())), preferred_element_type=F32)  134 us
    pallas_call x2, Pallas kernels, scan_bwd(): pl.pallas_call(functools.partial(bwd_kernel, T // U), grid=(S, C // cb),...  68.8 us
    unnamed x403, local copies, waits for them, and re-layouts  43.1 us
    pallas_call x2, Pallas kernels, expert_call(): pl.pallas_call(functools.partial(expert_kernel, pieces, tile, second_at),...  43 us
    pallas_call x2, Pallas kernels, scan_end_b(): pl.pallas_call(functools.partial(end_b_kernel, T // U), grid=(S, C // cb)...  40.6 us
    ppermute x18, waiting for transfers between devices, swap(): return lax.ppermute(x, axis, [(i, i ^ 1 << k) for i in range(count)])  38.2 us
    pallas_call x2, Pallas kernels, scan_fwd(): pl.pallas_call(functools.partial(fwd_kernel, T // U), grid=(S, C // cb),...  36.5 us
    all_to_all x2, waiting for transfers between devices, forward(): lax.all_to_all(send, 'batch', split_axis=0, concat_axis=0, tiled=True)  28.1 us
  transfers between devices with their start and end apart: 33, of which 14 were waited for; matrix products, arithmetic and copies ran while one was open for 33% of the time, Pallas kernels for 32%

profile of v4, /device:TPU:0, one launch (start us, length us, event | category | flops | bytes accessed | tf_op | source)
XLA Modules:
  0.0 659.1 jit_solution(1135574953355200683)
XLA Ops:
  9.1 7.3 %all-to-all-start.1 = ((bf16[8,24,1536]{2,1,0:T(8,128)(2,1)}), bf16[8,24,1536]{2,1,0:T(8,128)(2,1)}, u32[]{:S(2)}, u32[]{:S(2)}) async-start(bf16[8,24,1536]{2,1,0:T(8,128)(2,1)} %broadcast_in_dim.108), calls=%async_computation.1 | async-start | bytes 1179648 | tf_op jit(solution)/shard_map/all_to_all | solution.py:378
  25.5 6.9 %all-to-all-done.1 = bf16[8,24,1536]{2,1,0:T(8,128)(2,1)} async-done(((bf16[8,24,1536]{2,1,0:T(8,128)(2,1)}), bf16[8,24,1536]{2,1,0:T(8,128)(2,1)}, u32[]{:S(2)}, u32[]{:S(2)}) %all-to-all-start.1) | async-done | bytes 589856 | tf_op jit(solution)/shard_map/all_to_all | solution.py:378
  57.4 10.7 %collective-permute-done.3 = bf16[8,1,1,24,1536]{4,3,2,1,0:T(8,128)(2,1)} collective-permute-done((bf16[8,1,1,24,1536]{4,3,2,1,0:T(8,128)(2,1)}, bf16[8,1,1,24,1536]{4,3,2,1,0:T(8,128)(2,1)}, u32[]{:S(2)}, u32[]{:S(2)}) %collective-permute-start.3) | collective-permute-done | bytes 589856 | tf_op jit(solution)/shard_map/ppermute | solution.py:357
  86.7 12.3 %scan_end_f.2 = f32[2,16,1536]{2,1,0:T(8,128)S(1)} custom-call(f32[2,256,1536]{2,1,0:T(8,128)S(1)} %copy-done, bf16[2,256,1536]{2,1,0:T(8,128)(2,1)S(1)} %get-tuple-element.228.x_ref, f32[2,16,32,16]{3,2,1,0:T(8,128)S(1)} %bitcast.218, f32[16,1536]{1,0:T(8,128)S(1)} %get-tuple-element.255.r_ref), custom_call_target="tpu_custom_call" | custom-call | flops 786432 | bytes 786432 | tf_op jit(solution)/shard_map/scan_end_f/pallas_call | solution.py:51
  105.9 18.5 %scan_fwd.2 = (f32[2,256,1536]{2,1,0:T(8,128)S(1)}, bf16[2,4096,1536]{2,1,0:T(8,128)(2,1)}) custom-call(f32[2,256,1536]{2,1,0:T(8,128)} %get-tuple-element.283.s_ref, bf16[2,256,1536]{2,1,0:T(8,128)(2,1)S(1)} %get-tuple-element.228.x_ref, f32[2,16,32,16]{3,2,1,0:T(8,128)S(1)} %bitcast.219, bf16[2,256,256]{2,1,0:T(8,128)(2,1)S(1)} %fusion.48.l_ref, ...), custom_call_target="tpu_custom_call" | custom-call | flops 786432 | bytes 786432 | tf_op jit(solution)/shard_map/scan_fwd/pallas_call | solution.py:133
  143.1 5.4 all-to-all-start.2
  166.8 12.3 %scan_end_f.3 = f32[2,16,1536]{2,1,0:T(8,128)S(1)} custom-call(f32[2,256,1536]{2,1,0:T(8,128)S(1)} %copy-done.2, bf16[2,256,1536]{2,1,0:T(8,128)(2,1)S(1)} %get-tuple-element.224.x_ref, f32[2,16,32,16]{3,2,1,0:T(8,128)S(1)} %bitcast.222, f32[16,1536]{1,0:T(8,128)S(1)} %get-tuple-element.255.r_ref), custom_call_target="tpu_custom_call" | custom-call | flops 786432 | bytes 786432 | tf_op jit(solution)/shard_map/scan_end_f/pallas_call | solution.py:51
  195.7 18.0 %scan_fwd.3 = (f32[2,256,1536]{2,1,0:T(8,128)S(1)}, bf16[2,4096,1536]{2,1,0:T(8,128)(2,1)}) custom-call(f32[2,256,1536]{2,1,0:T(8,128)} %get-tuple-element.293.s_ref, bf16[2,256,1536]{2,1,0:T(8,128)(2,1)S(1)} %get-tuple-element.224.x_ref, f32[2,16,32,16]{3,2,1,0:T(8,128)S(1)} %bitcast.223, bf16[2,256,256]{2,1,0:T(8,128)(2,1)S(1)} %copy-done.24, ...), custom_call_target="tpu_custom_call" | custom-call | flops 786432 | bytes 786432 | tf_op jit(solution)/shard_map/scan_fwd/pallas_call | solution.py:133
  213.7 6.3 multiply_convert_fusion.2
  231.7 20.8 %expert.2 = (bf16[640,1536]{1,0:T(8,128)(2,1)S(1)}, bf16[1280,3072]{1,0:T(8,128)(2,1)}, bf16[1280,3072]{1,0:T(8,128)(2,1)}) custom-call(bf16[640,1536]{1,0:T(8,128)(2,1)} %bitcast.29.x_ref, bf16[4,1536,768]{2,1,0:T(8,128)(2,1)} %bitcast.228, bf16[4,1536,768]{2,1,0:T(8,128)(2,1)} %bitcast.229), custom_call_target="tpu_custom_call" | custom-call | flops 491520 | bytes 491520 | tf_op jit(solution)/shard_map/expert/pallas_call | solution.py:307
  253.8 22.9 %all-to-all-done.4 = bf16[8,2,40,1536]{3,2,1,0:T(8,128)(2,1)} async-done(((bf16[8,2,40,1536]{3,2,1,0:T(8,128)(2,1)}), bf16[8,2,40,1536]{3,2,1,0:T(8,128)(2,1)}, u32[]{:S(2)}, u32[]{:S(2)}) %all-to-all-start.4) | async-done | bytes 1966112 | tf_op jit(solution)/shard_map/all_to_all | solution.py:648
  283.5 22.2 %expert.3 = (bf16[640,1536]{1,0:T(8,128)(2,1)S(1)}, bf16[1280,3072]{1,0:T(8,128)(2,1)}, bf16[1280,3072]{1,0:T(8,128)(2,1)}) custom-call(bf16[640,1536]{1,0:T(8,128)(2,1)} %bitcast.42.x_ref, bf16[4,1536,768]{2,1,0:T(8,128)(2,1)} %bitcast.230, bf16[4,1536,768]{2,1,0:T(8,128)(2,1)} %bitcast.231, ...), custom_call_target="tpu_custom_call", output_to_operand_aliasing={{1}: (3, {}), {2}: (4, {})} | custom-call | flops 491520 | bytes 491520 | tf_op jit(solution)/shard_map/expert/pallas_call | solution.py:307
  307.0 11.3 %convolution_convert_fusion.1 = bf16[3072,768]{1,0:T(8,128)(2,1)} fusion(bf16[1280,3072]{1,0:T(8,128)(2,1)} %get-tuple-element.74, bf16[1280,1536]{1,0:T(8,128)(2,1)S(1)} %pad_maximum_fusion), kind=kOutput, calls=%fused_computation.7 | convolution fusion | flops 6042157056 | bytes 14548992 | tf_op jit(solution)/shard_map/dot_general | solution.py:442
  318.3 11.1 %convolution_convert_fusion = bf16[3072,768]{1,0:T(8,128)(2,1)} fusion(bf16[1280,3072]{1,0:T(8,128)(2,1)} %get-tuple-element.76, bf16[1280,1536]{1,0:T(8,128)(2,1)} %copy-done.79), kind=kOutput, calls=%fused_computation.6 | convolution fusion | flops 6042157056 | bytes 14548992 | tf_op jit(solution)/shard_map/dot_general | solution.py:442
  343.4 6.3 fusion.9
  349.8 5.9 all-to-all-start.5
  363.0 20.3 %scan_end_b.2 = (f32[2,16,1536]{2,1,0:T(8,128)S(1)}, f32[2,256,256]{2,1,0:T(8,128)S(1)}) custom-call(f32[2,256,1536]{2,1,0:T(8,128)S(1)} %copy-done.1, f32[2,256,1536]{2,1,0:T(8,128)} %get-tuple-element.221.g_ref, f32[2,16,32,16]{3,2,1,0:T(8,128)S(1)} %bitcast.220, f32[16,1536]{1,0:T(8,128)S(1)} %get-tuple-element.255.r_ref, ...), custom_call_target="tpu_custom_call" | custom-call | flops 786432 | bytes 786432 | tf_op jit(solution)/shard_map/scan_end_b/pallas_call | solution.py:88
  388.6 5.3 fusion.67
  415.9 6.4 fusion.11
  422.3 20.3 %scan_end_b.3 = (f32[2,16,1536]{2,1,0:T(8,128)S(1)}, f32[2,256,256]{2,1,0:T(8,128)S(1)}) custom-call(f32[2,256,1536]{2,1,0:T(8,128)S(1)} %copy-done.3, f32[2,256,1536]{2,1,0:T(8,128)} %get-tuple-element.219.g_ref, f32[2,16,32,16]{3,2,1,0:T(8,128)S(1)} %bitcast.224, f32[16,1536]{1,0:T(8,128)S(1)} %get-tuple-element.255.r_ref, ...), custom_call_target="tpu_custom_call" | custom-call | flops 786432 | bytes 786432 | tf_op jit(solution)/shard_map/scan_end_b/pallas_call | solution.py:88
  474.5 34.6 %scan_bwd.2 = (bf16[2,256,1536]{2,1,0:T(8,128)(2,1)S(1)}, f32[2,256,1536]{2,1,0:T(8,128)}, f32[2,8,1536]{2,1,0:T(8,128)S(1)}, f32[2,16,1536]{2,1,0:T(8,128)S(1)}, f32[2,256,256]{2,1,0:T(8,128)S(1)}) custom-call(f32[2,256,1536]{2,1,0:T(8,128)} %get-tuple-element.283.s_ref, bf16[2,256,1536]{2,1,0:T(8,128)(2,1)S(1)} %get-tuple-element.228.x_ref, ...), custom_call_target="tpu_custom_call" | custom-call | flops 786432 | bytes 786432 | tf_op jit(solution)/shard_map/scan_bwd/pallas_call | solution.py:217
  517.1 34.2 %scan_bwd.3 = (bf16[2,256,1536]{2,1,0:T(8,128)(2,1)S(1)}, f32[2,256,1536]{2,1,0:T(8,128)}, f32[2,8,1536]{2,1,0:T(8,128)S(1)}, f32[2,16,1536]{2,1,0:T(8,128)S(1)}, f32[2,256,256]{2,1,0:T(8,128)S(1)}) custom-call(f32[2,256,1536]{2,1,0:T(8,128)} %get-tuple-element.293.s_ref, bf16[2,256,1536]{2,1,0:T(8,128)(2,1)S(1)} %get-tuple-element.224.x_ref, ...), custom_call_target="tpu_custom_call" | custom-call | flops 786432 | bytes 786432 | tf_op jit(solution)/shard_map/scan_bwd/pallas_call | solution.py:217
  597.1 12.4 %collective-permute-done.18 = bf16[8,1,1,24,1536]{4,3,2,1,0:T(8,128)(2,1)S(1)} collective-permute-done((bf16[8,1,1,24,1536]{4,3,2,1,0:T(8,128)(2,1)S(1)}, bf16[8,1,1,24,1536]{4,3,2,1,0:T(8,128)(2,1)S(1)}, u32[]{:S(2)}, u32[]{:S(2)}) %collective-permute-start.18) | collective-permute-done | bytes 589856 | tf_op jit(solution)/shard_map/ppermute | solution.py:357
  634.8 12.5 %all-to-all-done.6 = bf16[8,24,2048]{2,1,0:T(8,128)(2,1)S(1)} async-done(((bf16[8,24,2048]{2,1,0:T(8,128)(2,1)}), bf16[8,24,2048]{2,1,0:T(8,128)(2,1)S(1)}, u32[]{:S(2)}, u32[]{:S(2)}) %all-to-all-start.6) | async-done | bytes 786464 | tf_op jit(solution)/shard_map/all_to_all | solution.py:390
  (676 shorter events, 298.0 us)
Async XLA Ops:
  9.1 23.2 %all-to-all-start.1 = ((bf16[8,24,1536]{2,1,0:T(8,128)(2,1)}), bf16[8,24,1536]{2,1,0:T(8,128)(2,1)}, u32[]{:S(2)}, u32[]{:S(2)}) async-start(bf16[8,24,1536]{2,1,0:T(8,128)(2,1)} %broadcast_in_dim.108), calls=%async_computation.1 | async-start | bytes 1179648 | tf_op jit(solution)/shard_map/all_to_all | solution.py:378
  17.8 29.3 %collective-permute-start.2 = (bf16[4,8,768]{2,1,0:T(8,128)(2,1)}, bf16[4,8,768]{2,1,0:T(8,128)(2,1)S(1)}, u32[]{:S(2)}, u32[]{:S(2)}) collective-permute-start(bf16[4,8,768]{2,1,0:T(8,128)(2,1)} %slice.297), channel_id=1, source_target_pairs={{0,1},{1,2},{2,3},{4,5},{5,6},{6,7},{8,9},{9,10},{10,11},{12,13},{... | collective-permute-start | bytes 147464 | tf_op jit(solution)/shard_map/ppermute | solution.py:362
  33.1 12.5 %all-to-all-start = ((bf16[8,24,640]{2,1,0:T(8,128)(2,1)}), bf16[8,24,640]{2,1,0:T(8,128)(2,1)S(1)}, u32[]{:S(2)}, u32[]{:S(2)}) async-start(bf16[8,24,640]{2,1,0:T(8,128)(2,1)} %broadcast_in_dim.105), calls=%async_computation | async-start | bytes 491520 | tf_op jit(solution)/shard_map/all_to_all | solution.py:378
  36.7 90.0 %all-gather.4.cloned.1.call-start = ((), (), s32[]{:S(2)}) async-start(), calls=%async_computation.10 | async-start | bytes 4866048 | tf_op jit(solution)/shard_map/all_gather | solution.py:539
  37.5 194.2 %all-gather.6.cloned.1.call-start = ((), (), s32[]{:S(2)}) async-start(), calls=%async_computation.13 | async-start | bytes 11796480 | tf_op jit(solution)/shard_map/all_gather | solution.py:544
  52.0 16.1 %collective-permute-start.3 = (bf16[8,1,1,24,1536]{4,3,2,1,0:T(8,128)(2,1)}, bf16[8,1,1,24,1536]{4,3,2,1,0:T(8,128)(2,1)}, u32[]{:S(2)}, u32[]{:S(2)}) collective-permute-start(bf16[8,1,1,24,1536]{4,3,2,1,0:T(8,128)(2,1)} %bitcast.7), channel_id=1, source_target_pairs={{0,2},{1,3},{2,0},{3,1},{4,6},{5,7},{6,4},{7,5},{8,10},{9,11},{10,... | collective-permute-start | bytes 1769480 | tf_op jit(solution)/shard_map/ppermute | solution.py:357
  83.6 15.5 %collective-permute-start.6 = (f32[2,1536]{1,0:T(2,128)S(1)}, f32[2,1536]{1,0:T(2,128)}, u32[]{:S(2)}, u32[]{:S(2)}) collective-permute-start(f32[2,1536]{1,0:T(2,128)S(1)} %get-tuple-element.282), channel_id=1, source_target_pairs={{0,1},{1,0},{2,3},{3,2},{4,5},{5,4},{6,7},{7,6},{8,9},{9,8},{10,11... | collective-permute-start | bytes 36872 | tf_op jit(solution)/shard_map/ppermute | solution.py:357
  143.1 50.6 %all-to-all-start.2 = ((bf16[8,2,40,1536]{3,2,1,0:T(8,128)(2,1)}), bf16[8,2,40,1536]{3,2,1,0:T(8,128)(2,1)}, u32[]{:S(2)}, u32[]{:S(2)}) async-start(bf16[8,2,40,1536]{3,2,1,0:T(8,128)(2,1)} %bitcast.243), calls=%async_computation.2 | async-start | bytes 3932160 | tf_op jit(solution)/shard_map/all_to_all | solution.py:648
  159.5 20.3 %collective-permute-start.9 = (f32[2,1536]{1,0:T(2,128)S(1)}, f32[2,1536]{1,0:T(2,128)S(1)}, u32[]{:S(2)}, u32[]{:S(2)}) collective-permute-start(f32[2,1536]{1,0:T(2,128)S(1)} %get-tuple-element.292), channel_id=1, source_target_pairs={{0,1},{1,0},{2,3},{3,2},{4,5},{5,4},{6,7},{7,6},{8,9},{9,8},{10,11... | collective-permute-start | bytes 36872 | tf_op jit(solution)/shard_map/ppermute | solution.py:357
  180.8 7.6 %collective-permute-start.10 = (bf16[2,16,1536]{2,1,0:T(8,128)(2,1)S(1)}, bf16[2,16,1536]{2,1,0:T(8,128)(2,1)S(1)}, u32[]{:S(2)}, u32[]{:S(2)}) collective-permute-start(bf16[2,16,1536]{2,1,0:T(8,128)(2,1)S(1)} %fusion.99), channel_id=1, source_target_pairs={{0,2},{1,3},{2,0},{3,1},{4,6},{5,7},{6,4},{7,5},{8,10},{9,11},{10,... | collective-permute-start | bytes 294920 | tf_op jit(solution)/shard_map/ppermute | solution.py:357
  227.2 49.6 %all-to-all-start.4 = ((bf16[8,2,40,1536]{3,2,1,0:T(8,128)(2,1)}), bf16[8,2,40,1536]{3,2,1,0:T(8,128)(2,1)}, u32[]{:S(2)}, u32[]{:S(2)}) async-start(bf16[8,2,40,1536]{3,2,1,0:T(8,128)(2,1)} %bitcast.244), calls=%async_computation.4 | async-start | bytes 3932160 | tf_op jit(solution)/shard_map/all_to_all | solution.py:648
  276.7 52.8 %all-to-all-start.3 = ((bf16[8,2,40,1536]{3,2,1,0:T(8,128)(2,1)}), bf16[8,2,40,1536]{3,2,1,0:T(8,128)(2,1)}, u32[]{:S(2)}, u32[]{:S(2)}) async-start(bf16[8,2,40,1536]{3,2,1,0:T(8,128)(2,1)} %bitcast.227), calls=%async_computation.3 | async-start | bytes 3932160 | tf_op jit(solution)/shard_map/all_to_all | solution.py:659
  281.1 329.6 %reduce-scatter.6.cloned.1.call-start = ((), (), s32[]{:S(2)}) async-start(), calls=%async_computation.11 | async-start | bytes 5898240 | tf_op jit(solution)/shard_map/reduce_scatter | solution.py:758
  349.8 50.4 %all-to-all-start.5 = ((bf16[8,2,40,1536]{3,2,1,0:T(8,128)(2,1)}), bf16[8,2,40,1536]{3,2,1,0:T(8,128)(2,1)}, u32[]{:S(2)}, u32[]{:S(2)}) async-start(bf16[8,2,40,1536]{3,2,1,0:T(8,128)(2,1)} %bitcast.226), calls=%async_computation.5 | async-start | bytes 3932160 | tf_op jit(solution)/shard_map/all_to_all | solution.py:659
  355.6 255.0 %reduce-scatter.8.cloned.1.call-start = ((), (), s32[]{:S(2)}) async-start(), calls=%async_computation.12 | async-start | bytes 5898240 | tf_op jit(solution)/shard_map/reduce_scatter | solution.py:757
  356.2 261.1 %reduce-scatter.10.cloned.1.call-start = ((), (), s32[]{:S(2)}) async-start(), calls=%async_computation.14 | async-start | bytes 5068800
  384.8 76.9 %collective-permute-start.11 = (bf16[2,16,1536]{2,1,0:T(8,128)(2,1)}, bf16[2,16,1536]{2,1,0:T(8,128)(2,1)}, u32[]{:S(2)}, u32[]{:S(2)}) collective-permute-start(bf16[2,16,1536]{2,1,0:T(8,128)(2,1)} %convert_element_type.381), channel_id=1, source_target_pairs={{0,1},{1,0},{2,3},{3,2},{4,5},{5,4},{6,7},{7,6},{8,9},{9,8},{10,11... | collective-permute-start | bytes 294920 | tf_op jit(solution)/shard_map/ppermute | solution.py:357
  444.7 17.0 %collective-permute-start.14 = (bf16[2,16,1536]{2,1,0:T(8,128)(2,1)}, bf16[2,16,1536]{2,1,0:T(8,128)(2,1)}, u32[]{:S(2)}, u32[]{:S(2)}) collective-permute-start(bf16[2,16,1536]{2,1,0:T(8,128)(2,1)} %convert_element_type.391), channel_id=1, source_target_pairs={{0,1},{1,0},{2,3},{3,2},{4,5},{5,4},{6,7},{7,6},{8,9},{9,8},{10,11... | collective-permute-start | bytes 294920 | tf_op jit(solution)/shard_map/ppermute | solution.py:357
  515.7 48.0 %collective-permute-start.13 = (f32[2,8,1536]{2,1,0:T(8,128)}, f32[2,8,1536]{2,1,0:T(8,128)}, u32[]{:S(2)}, u32[]{:S(2)}) collective-permute-start(f32[2,8,1536]{2,1,0:T(8,128)} %slice.423), channel_id=1, source_target_pairs={{1,0},{2,1},{3,2},{5,4},{6,5},{7,6},{9,8},{10,9},{11,10},{13,12},{... | collective-permute-start | bytes 294920 | tf_op jit(solution)/shard_map/ppermute | solution.py:362
  557.6 8.5 %collective-permute-start.16 = (f32[2,8,1536]{2,1,0:T(8,128)}, f32[2,8,1536]{2,1,0:T(8,128)}, u32[]{:S(2)}, u32[]{:S(2)}) collective-permute-start(f32[2,8,1536]{2,1,0:T(8,128)} %slice.430), channel_id=1, source_target_pairs={{1,0},{2,1},{3,2},{5,4},{6,5},{7,6},{9,8},{10,9},{11,10},{13,12},{... | collective-permute-start | bytes 294920 | tf_op jit(solution)/shard_map/ppermute | solution.py:362
  576.5 14.6 %collective-permute-start.17 = (bf16[8,2,1,24,1536]{4,3,2,1,0:T(8,128)(2,1)}, bf16[8,2,1,24,1536]{4,3,2,1,0:T(8,128)(2,1)}, u32[]{:S(2)}, u32[]{:S(2)}) collective-permute-start(bf16[8,2,1,24,1536]{4,3,2,1,0:T(8,128)(2,1)} %dynamic-slice_convert_fusion), channel_id=1, source_target_pairs={{0,1},{1,0},{2,3},{3,2},{4,5},{5,4},{6,7},{7,6},{8,9},{9,8},{10,11... | collective-permute-start | bytes 3538952 | tf_op jit(solution)/shard_map/ppermute | solution.py:357
  588.6 8.4 %collective-permute-start.20 = (bf16[8,1,1,24,512]{4,3,2,1,0:T(8,128)(2,1)S(1)}, bf16[8,1,1,24,512]{4,3,2,1,0:T(8,128)(2,1)S(1)}, u32[]{:S(2)}, u32[]{:S(2)}) collective-permute-start(bf16[8,1,1,24,512]{4,3,2,1,0:T(8,128)(2,1)S(1)} %dynamic-slice_convert_fusion.3), channel_id=1, source_target_pairs={{0,2},{1,3},{2,0},{3,1},{4,6},{5,7},{6,4},{7,5},{8,10},{9,11},{10,... | collective-permute-start | bytes 589832 | tf_op jit(solution)/shard_map/ppermute | solution.py:357
  593.0 16.5 %collective-permute-start.18 = (bf16[8,1,1,24,1536]{4,3,2,1,0:T(8,128)(2,1)S(1)}, bf16[8,1,1,24,1536]{4,3,2,1,0:T(8,128)(2,1)S(1)}, u32[]{:S(2)}, u32[]{:S(2)}) collective-permute-start(bf16[8,1,1,24,1536]{4,3,2,1,0:T(8,128)(2,1)S(1)} %dynamic-slice_convert_fusion.1), channel_id=1, source_target_pairs={{0,2},{1,3},{2,0},{3,1},{4,6},{5,7},{6,4},{7,5},{8,10},{9,11},{10,... | collective-permute-start | bytes 1769480 | tf_op jit(solution)/shard_map/ppermute | solution.py:357
  623.2 24.2 %all-to-all-start.6 = ((bf16[8,24,2048]{2,1,0:T(8,128)(2,1)}), bf16[8,24,2048]{2,1,0:T(8,128)(2,1)S(1)}, u32[]{:S(2)}, u32[]{:S(2)}) async-start(bf16[8,24,2048]{2,1,0:T(8,128)(2,1)} %pad_maximum_fusion.7), calls=%async_computation.8 | async-start | bytes 1572864 | tf_op jit(solution)/shard_map/all_to_all | solution.py:390
  (206 other events, 2465.4 us)
Sparse Core Ops, SparseCore 0:
  41.1 65.4 all-gather.3
  126.9 66.4 all-gather.5
  349.9 48.6 reduce-scatter.5
  401.1 47.8 reduce-scatter.7
  468.9 105.1 reduce-scatter.9

commit v5 on v4

--- a/solution.py
+++ b/solution.py
@@ -533,7 +533,17 @@
         axis=1,
     )
     feat = jnp.concatenate([norm_gain[:, None], moe_gain[:, None], router], axis=1)
+    used = chan.shape[1]
+    second_set = jnp.concatenate(
+        [
+            pad_cols(jnp.concatenate([chan[:rows], feat], axis=1), 192),
+            pad_cols(chan[rows:], 192),
+        ],
+        axis=1,
+    )
+    second_set = over_seq(second_set[None])
     first_set = from_batch(in_proj[:, :DI])
+    second_set = from_batch(after(second_set, first_set)).reshape(-1, second_set.shape[1])
     later = jnp.concatenate([in_proj[:, DI:], side_by_side(out_proj, rows)], axis=1)
     later = after(later, first_set)
     later = lax.all_gather(later, ("batch", "seq"), axis=0, tiled=True)
@@ -547,14 +557,9 @@
         own = after((expert_in[0], expert_out[0]), later)
         expert_weights = *(lax.all_gather(x, "seq", axis=0, tiled=False) for x in own), 0
     first_set = over_seq(first_set)
-    second_set = over_seq(
-        from_batch(
-            jnp.concatenate([pad_cols(chan, 256).reshape(rows, 512), pad_cols(feat, 128)], axis=1)
-        )
-    )
     w_conv_in = first_set
-    chan = second_set[:, :512].reshape(-1, 256)
-    feat = second_set[:, 512:]
+    chan = one_below(second_set, rows)
+    feat = chan.reshape(-1, 2, rows, 192)[:, 0].reshape(-1, 192)[:, used:]
     gain_one = feat[:, 0].astype(F32)
     gain_two = feat[:, 1].astype(F32)
     router_weight = feat[:, 2 : 2 + experts]

time: 670 us -> 659 us (0.984)
    unnamed x403 -> x413, local copies, waits for them, and re-layouts: 43.1 us -> 43.4 us
  transfers between devices with their start and end apart: 33 -> 33, of which waited for: 14 -> 15; matrix products, arithmetic and copies ran while one was open for 33% -> 32% of each run, Pallas kernels for 32% -> 33%
where the time goes in v5:
time: 659 us; the launch traced here: 652 us
  Pallas kernels  213 us (32%)
  matrix products  135 us (20%)
  waiting for transfers between devices  90.1 us (14%)
  local copies, waits for them, and re-layouts  72.8 us (11%)
  other arithmetic  70.4 us (11%)
  starting transfers between devices  53.1 us (8%)
  between operations  16.8 us (3%)
    dot_general x46, matrix products, mm(): lax.dot_general(left, right, (dims, ((), ())), preferred_element_type=F32)  132 us
    pallas_call x2, Pallas kernels, scan_bwd(): pl.pallas_call(functools.partial(bwd_kernel, T // U), grid=(S, C // cb),...  68.8 us
    unnamed x413, local copies, waits for them, and re-layouts  43.4 us
    pallas_call x2, Pallas kernels, expert_call(): pl.pallas_call(functools.partial(expert_kernel, pieces, tile, second_at),...  43.1 us
    pallas_call x2, Pallas kernels, scan_end_b(): pl.pallas_call(functools.partial(end_b_kernel, T // U), grid=(S, C // cb)...  40.7 us
    ppermute x18, waiting for transfers between devices, swap(): return lax.ppermute(x, axis, [(i, i ^ 1 << k) for i in range(count)])  37.4 us
    pallas_call x2, Pallas kernels, scan_fwd(): pl.pallas_call(functools.partial(fwd_kernel, T // U), grid=(S, C // cb),...  36.1 us
    all_to_all x2, waiting for transfers between devices, forward(): lax.all_to_all(send, 'batch', split_axis=0, concat_axis=0, tiled=True)  29.5 us
  transfers between devices with their start and end apart: 33, of which 15 were waited for; matrix products, arithmetic and copies ran while one was open for 32% of the time, Pallas kernels for 33%

profile of v5, /device:TPU:0, one launch (start us, length us, event | category | flops | bytes accessed | tf_op | source)
XLA Modules:
  0.0 651.7 jit_solution(8681783485954812890)
XLA Ops:
  9.2 7.3 %all-to-all-start = ((bf16[8,24,1536]{2,1,0:T(8,128)(2,1)}), bf16[8,24,1536]{2,1,0:T(8,128)(2,1)S(1)}, u32[]{:S(2)}, u32[]{:S(2)}) async-start(bf16[8,24,1536]{2,1,0:T(8,128)(2,1)} %broadcast_in_dim.105), calls=%async_computation | async-start | bytes 1179648 | tf_op jit(solution)/shard_map/all_to_all | solution.py:378
  25.4 6.9 %all-to-all-done = bf16[8,24,1536]{2,1,0:T(8,128)(2,1)S(1)} async-done(((bf16[8,24,1536]{2,1,0:T(8,128)(2,1)}), bf16[8,24,1536]{2,1,0:T(8,128)(2,1)S(1)}, u32[]{:S(2)}, u32[]{:S(2)}) %all-to-all-start) | async-done | bytes 589856 | tf_op jit(solution)/shard_map/all_to_all | solution.py:378
  45.2 13.4 %collective-permute-done.3 = bf16[8,1,1,24,1536]{4,3,2,1,0:T(8,128)(2,1)S(1)} collective-permute-done((bf16[8,1,1,24,1536]{4,3,2,1,0:T(8,128)(2,1)S(1)}, bf16[8,1,1,24,1536]{4,3,2,1,0:T(8,128)(2,1)S(1)}, u32[]{:S(2)}, u32[]{:S(2)}) %collective-permute-start.3) | collective-permute-done | bytes 589856 | tf_op jit(solution)/shard_map/ppermute | solution.py:357
  80.8 12.3 %scan_end_f.2 = f32[2,16,1536]{2,1,0:T(8,128)S(1)} custom-call(f32[2,256,1536]{2,1,0:T(8,128)S(1)} %copy-done, bf16[2,256,1536]{2,1,0:T(8,128)(2,1)S(1)} %get-tuple-element.230.x_ref, f32[2,16,32,16]{3,2,1,0:T(8,128)S(1)} %bitcast.225, f32[16,1536]{1,0:T(8,128)S(1)} %get-tuple-element.259.r_ref), custom_call_target="tpu_custom_call" | custom-call | flops 786432 | bytes 786432 | tf_op jit(solution)/shard_map/scan_end_f/pallas_call | solution.py:51
  99.9 18.1 %scan_fwd.2 = (f32[2,256,1536]{2,1,0:T(8,128)S(1)}, bf16[2,4096,1536]{2,1,0:T(8,128)(2,1)}) custom-call(f32[2,256,1536]{2,1,0:T(8,128)} %get-tuple-element.289.s_ref, bf16[2,256,1536]{2,1,0:T(8,128)(2,1)S(1)} %get-tuple-element.230.x_ref, f32[2,16,32,16]{3,2,1,0:T(8,128)S(1)} %bitcast.226, bf16[2,256,256]{2,1,0:T(8,128)(2,1)S(1)} %fusion.48.l_ref, ...), custom_call_target="tpu_custom_call" | custom-call | flops 786432 | bytes 786432 | tf_op jit(solution)/shard_map/scan_fwd/pallas_call | solution.py:133
  157.1 12.3 %scan_end_f.3 = f32[2,16,1536]{2,1,0:T(8,128)S(1)} custom-call(f32[2,256,1536]{2,1,0:T(8,128)S(1)} %copy-done.2, bf16[2,256,1536]{2,1,0:T(8,128)(2,1)S(1)} %get-tuple-element.226.x_ref, f32[2,16,32,16]{3,2,1,0:T(8,128)S(1)} %bitcast.229, f32[16,1536]{1,0:T(8,128)S(1)} %get-tuple-element.259.r_ref), custom_call_target="tpu_custom_call" | custom-call | flops 786432 | bytes 786432 | tf_op jit(solution)/shard_map/scan_end_f/pallas_call | solution.py:51
  178.7 6.7 %all-to-all-done.2 = bf16[8,2,40,1536]{3,2,1,0:T(8,128)(2,1)} async-done(((bf16[8,2,40,1536]{3,2,1,0:T(8,128)(2,1)}), bf16[8,2,40,1536]{3,2,1,0:T(8,128)(2,1)}, u32[]{:S(2)}, u32[]{:S(2)}) %all-to-all-start.2) | async-done | bytes 1966112 | tf_op jit(solution)/shard_map/all_to_all | solution.py:653
  187.4 18.0 %scan_fwd.3 = (f32[2,256,1536]{2,1,0:T(8,128)S(1)}, bf16[2,4096,1536]{2,1,0:T(8,128)(2,1)}) custom-call(f32[2,256,1536]{2,1,0:T(8,128)} %get-tuple-element.299.s_ref, bf16[2,256,1536]{2,1,0:T(8,128)(2,1)S(1)} %get-tuple-element.226.x_ref, f32[2,16,32,16]{3,2,1,0:T(8,128)S(1)} %bitcast.230, bf16[2,256,256]{2,1,0:T(8,128)(2,1)S(1)} %copy-done.24, ...), custom_call_target="tpu_custom_call" | custom-call | flops 786432 | bytes 786432 | tf_op jit(solution)/shard_map/scan_fwd/pallas_call | solution.py:133
  205.5 6.2 multiply_convert_fusion.2
  222.6 20.8 %expert.2 = (bf16[640,1536]{1,0:T(8,128)(2,1)S(1)}, bf16[1280,3072]{1,0:T(8,128)(2,1)}, bf16[1280,3072]{1,0:T(8,128)(2,1)}) custom-call(bf16[640,1536]{1,0:T(8,128)(2,1)} %bitcast.35.x_ref, bf16[4,1536,768]{2,1,0:T(8,128)(2,1)} %bitcast.235, bf16[4,1536,768]{2,1,0:T(8,128)(2,1)} %bitcast.236), custom_call_target="tpu_custom_call" | custom-call | flops 491520 | bytes 491520 | tf_op jit(solution)/shard_map/expert/pallas_call | solution.py:307
  244.7 22.9 %all-to-all-done.4 = bf16[8,2,40,1536]{3,2,1,0:T(8,128)(2,1)} async-done(((bf16[8,2,40,1536]{3,2,1,0:T(8,128)(2,1)}), bf16[8,2,40,1536]{3,2,1,0:T(8,128)(2,1)}, u32[]{:S(2)}, u32[]{:S(2)}) %all-to-all-start.4) | async-done | bytes 1966112 | tf_op jit(solution)/shard_map/all_to_all | solution.py:653
  274.3 22.2 %expert.3 = (bf16[640,1536]{1,0:T(8,128)(2,1)S(1)}, bf16[1280,3072]{1,0:T(8,128)(2,1)}, bf16[1280,3072]{1,0:T(8,128)(2,1)}) custom-call(bf16[640,1536]{1,0:T(8,128)(2,1)} %bitcast.48.x_ref, bf16[4,1536,768]{2,1,0:T(8,128)(2,1)} %bitcast.237, bf16[4,1536,768]{2,1,0:T(8,128)(2,1)} %bitcast.238, ...), custom_call_target="tpu_custom_call", output_to_operand_aliasing={{1}: (3, {}), {2}: (4, {})} | custom-call | flops 491520 | bytes 491520 | tf_op jit(solution)/shard_map/expert/pallas_call | solution.py:307
  297.8 11.4 %convolution_convert_fusion.1 = bf16[3072,768]{1,0:T(8,128)(2,1)} fusion(bf16[1280,3072]{1,0:T(8,128)(2,1)} %get-tuple-element.76, bf16[1280,1536]{1,0:T(8,128)(2,1)S(1)} %pad_maximum_fusion), kind=kOutput, calls=%fused_computation.7 | convolution fusion | flops 6042157056 | bytes 14548992 | tf_op jit(solution)/shard_map/dot_general | solution.py:442
  309.2 11.1 %convolution_convert_fusion = bf16[3072,768]{1,0:T(8,128)(2,1)} fusion(bf16[1280,3072]{1,0:T(8,128)(2,1)} %get-tuple-element.78, bf16[1280,1536]{1,0:T(8,128)(2,1)} %copy-done.81), kind=kOutput, calls=%fused_computation.6 | convolution fusion | flops 6042157056 | bytes 14548992 | tf_op jit(solution)/shard_map/dot_general | solution.py:442
  334.3 6.4 fusion.9
  340.6 5.9 all-to-all-start.5
  354.1 20.4 %scan_end_b.2 = (f32[2,16,1536]{2,1,0:T(8,128)S(1)}, f32[2,256,256]{2,1,0:T(8,128)S(1)}) custom-call(f32[2,256,1536]{2,1,0:T(8,128)S(1)} %copy-done.1, f32[2,256,1536]{2,1,0:T(8,128)} %get-tuple-element.223.g_ref, f32[2,16,32,16]{3,2,1,0:T(8,128)S(1)} %bitcast.227, f32[16,1536]{1,0:T(8,128)S(1)} %get-tuple-element.259.r_ref, ...), custom_call_target="tpu_custom_call" | custom-call | flops 786432 | bytes 786432 | tf_op jit(solution)/shard_map/scan_end_b/pallas_call | solution.py:88
  379.8 5.3 fusion.67
  407.1 6.4 fusion.11
  413.6 20.3 %scan_end_b.3 = (f32[2,16,1536]{2,1,0:T(8,128)S(1)}, f32[2,256,256]{2,1,0:T(8,128)S(1)}) custom-call(f32[2,256,1536]{2,1,0:T(8,128)S(1)} %copy-done.3, f32[2,256,1536]{2,1,0:T(8,128)} %get-tuple-element.221.g_ref, f32[2,16,32,16]{3,2,1,0:T(8,128)S(1)} %bitcast.231, f32[16,1536]{1,0:T(8,128)S(1)} %get-tuple-element.259.r_ref, ...), custom_call_target="tpu_custom_call" | custom-call | flops 786432 | bytes 786432 | tf_op jit(solution)/shard_map/scan_end_b/pallas_call | solution.py:88
  465.6 34.6 %scan_bwd.2 = (bf16[2,256,1536]{2,1,0:T(8,128)(2,1)S(1)}, f32[2,256,1536]{2,1,0:T(8,128)}, f32[2,8,1536]{2,1,0:T(8,128)S(1)}, f32[2,16,1536]{2,1,0:T(8,128)S(1)}, f32[2,256,256]{2,1,0:T(8,128)S(1)}) custom-call(f32[2,256,1536]{2,1,0:T(8,128)} %get-tuple-element.289.s_ref, bf16[2,256,1536]{2,1,0:T(8,128)(2,1)S(1)} %get-tuple-element.230.x_ref, ...), custom_call_target="tpu_custom_call" | custom-call | flops 786432 | bytes 786432 | tf_op jit(solution)/shard_map/scan_bwd/pallas_call | solution.py:217
  508.3 34.2 %scan_bwd.3 = (bf16[2,256,1536]{2,1,0:T(8,128)(2,1)S(1)}, f32[2,256,1536]{2,1,0:T(8,128)}, f32[2,8,1536]{2,1,0:T(8,128)S(1)}, f32[2,16,1536]{2,1,0:T(8,128)S(1)}, f32[2,256,256]{2,1,0:T(8,128)S(1)}) custom-call(f32[2,256,1536]{2,1,0:T(8,128)} %get-tuple-element.299.s_ref, bf16[2,256,1536]{2,1,0:T(8,128)(2,1)S(1)} %get-tuple-element.226.x_ref, ...), custom_call_target="tpu_custom_call" | custom-call | flops 786432 | bytes 786432 | tf_op jit(solution)/shard_map/scan_bwd/pallas_call | solution.py:217
  588.3 12.5 %collective-permute-done.18 = bf16[8,1,1,24,1536]{4,3,2,1,0:T(8,128)(2,1)S(1)} collective-permute-done((bf16[8,1,1,24,1536]{4,3,2,1,0:T(8,128)(2,1)S(1)}, bf16[8,1,1,24,1536]{4,3,2,1,0:T(8,128)(2,1)S(1)}, u32[]{:S(2)}, u32[]{:S(2)}) %collective-permute-start.18) | collective-permute-done | bytes 589856 | tf_op jit(solution)/shard_map/ppermute | solution.py:357
  628.4 11.5 %all-to-all-done.6 = bf16[8,24,2048]{2,1,0:T(8,128)(2,1)S(1)} async-done(((bf16[8,24,2048]{2,1,0:T(8,128)(2,1)}), bf16[8,24,2048]{2,1,0:T(8,128)(2,1)S(1)}, u32[]{:S(2)}, u32[]{:S(2)}) %all-to-all-start.6) | async-done | bytes 786464 | tf_op jit(solution)/shard_map/all_to_all | solution.py:390
  (687 shorter events, 287.7 us)
Async XLA Ops:
  9.2 23.1 %all-to-all-start = ((bf16[8,24,1536]{2,1,0:T(8,128)(2,1)}), bf16[8,24,1536]{2,1,0:T(8,128)(2,1)S(1)}, u32[]{:S(2)}, u32[]{:S(2)}) async-start(bf16[8,24,1536]{2,1,0:T(8,128)(2,1)} %broadcast_in_dim.105), calls=%async_computation | async-start | bytes 1179648 | tf_op jit(solution)/shard_map/all_to_all | solution.py:378
  16.4 103.2 %all-gather.4.cloned.1.call-start = ((), (), s32[]{:S(2)}) async-start(), calls=%async_computation.10 | async-start | bytes 4866048 | tf_op jit(solution)/shard_map/all_gather | solution.py:549
  21.6 15.8 %collective-permute-start = (bf16[1,1,1,24,384]{4,3,2,1,0:T(8,128)(2,1)S(1)}, bf16[1,1,1,24,384]{4,3,2,1,0:T(8,128)(2,1)S(1)}, u32[]{:S(2)}, u32[]{:S(2)}) collective-permute-start(bf16[1,1,1,24,384]{4,3,2,1,0:T(8,128)(2,1)S(1)} %fusion.123), channel_id=1, source_target_pairs={{0,2},{1,3},{2,0},{3,1},{4,6},{5,7},{6,4},{7,5},{8,10},{9,11},{10,... | collective-permute-start | bytes 55304 | tf_op jit(solution)/shard_map/ppermute | solution.py:357
  23.1 21.7 %collective-permute-start.2 = (bf16[4,8,768]{2,1,0:T(8,128)(2,1)S(1)}, bf16[4,8,768]{2,1,0:T(8,128)(2,1)S(1)}, u32[]{:S(2)}, u32[]{:S(2)}) collective-permute-start(bf16[4,8,768]{2,1,0:T(8,128)(2,1)S(1)} %slice.313), channel_id=1, source_target_pairs={{0,1},{1,2},{2,3},{4,5},{5,6},{6,7},{8,9},{9,10},{10,11},{12,13},{... | collective-permute-start | bytes 147464 | tf_op jit(solution)/shard_map/ppermute | solution.py:362
  39.6 22.0 %all-to-all-start.1 = ((bf16[8,96,384]{2,1,0:T(8,128)(2,1)}), bf16[8,96,384]{2,1,0:T(8,128)(2,1)S(1)}, u32[]{:S(2)}, u32[]{:S(2)}) async-start(bf16[8,96,384]{2,1,0:T(8,128)(2,1)} %broadcast_in_dim.106), calls=%async_computation.1 | async-start | bytes 1179648 | tf_op jit(solution)/shard_map/all_to_all | solution.py:378
  43.2 179.4 %all-gather.6.cloned.1.call-start = ((), (), s32[]{:S(2)}) async-start(), calls=%async_computation.13 | async-start | bytes 11796480 | tf_op jit(solution)/shard_map/all_gather | solution.py:554
  43.3 15.4 %collective-permute-start.3 = (bf16[8,1,1,24,1536]{4,3,2,1,0:T(8,128)(2,1)S(1)}, bf16[8,1,1,24,1536]{4,3,2,1,0:T(8,128)(2,1)S(1)}, u32[]{:S(2)}, u32[]{:S(2)}) collective-permute-start(bf16[8,1,1,24,1536]{4,3,2,1,0:T(8,128)(2,1)S(1)} %bitcast.270), channel_id=1, source_target_pairs={{0,2},{1,3},{2,0},{3,1},{4,6},{5,7},{6,4},{7,5},{8,10},{9,11},{10,... | collective-permute-start | bytes 1769480 | tf_op jit(solution)/shard_map/ppermute | solution.py:357
  78.2 15.5 %collective-permute-start.6 = (f32[2,1536]{1,0:T(2,128)S(1)}, f32[2,1536]{1,0:T(2,128)S(1)}, u32[]{:S(2)}, u32[]{:S(2)}) collective-permute-start(f32[2,1536]{1,0:T(2,128)S(1)} %get-tuple-element.288), channel_id=1, source_target_pairs={{0,1},{1,0},{2,3},{3,2},{4,5},{5,4},{6,7},{7,6},{8,9},{9,8},{10,11... | collective-permute-start | bytes 36872 | tf_op jit(solution)/shard_map/ppermute | solution.py:357
  135.1 50.3 %all-to-all-start.2 = ((bf16[8,2,40,1536]{3,2,1,0:T(8,128)(2,1)}), bf16[8,2,40,1536]{3,2,1,0:T(8,128)(2,1)}, u32[]{:S(2)}, u32[]{:S(2)}) async-start(bf16[8,2,40,1536]{3,2,1,0:T(8,128)(2,1)} %bitcast.256), calls=%async_computation.2 | async-start | bytes 3932160 | tf_op jit(solution)/shard_map/all_to_all | solution.py:653
  151.3 18.7 %collective-permute-start.9 = (f32[2,1536]{1,0:T(2,128)S(1)}, f32[2,1536]{1,0:T(2,128)S(1)}, u32[]{:S(2)}, u32[]{:S(2)}) collective-permute-start(f32[2,1536]{1,0:T(2,128)S(1)} %get-tuple-element.298), channel_id=1, source_target_pairs={{0,1},{1,0},{2,3},{3,2},{4,5},{5,4},{6,7},{7,6},{8,9},{9,8},{10,11... | collective-permute-start | bytes 36872 | tf_op jit(solution)/shard_map/ppermute | solution.py:357
  218.0 49.5 %all-to-all-start.4 = ((bf16[8,2,40,1536]{3,2,1,0:T(8,128)(2,1)}), bf16[8,2,40,1536]{3,2,1,0:T(8,128)(2,1)}, u32[]{:S(2)}, u32[]{:S(2)}) async-start(bf16[8,2,40,1536]{3,2,1,0:T(8,128)(2,1)} %bitcast.257), calls=%async_computation.4 | async-start | bytes 3932160 | tf_op jit(solution)/shard_map/all_to_all | solution.py:653
  267.5 52.8 %all-to-all-start.3 = ((bf16[8,2,40,1536]{3,2,1,0:T(8,128)(2,1)}), bf16[8,2,40,1536]{3,2,1,0:T(8,128)(2,1)}, u32[]{:S(2)}, u32[]{:S(2)}) async-start(bf16[8,2,40,1536]{3,2,1,0:T(8,128)(2,1)} %bitcast.234), calls=%async_computation.3 | async-start | bytes 3932160 | tf_op jit(solution)/shard_map/all_to_all | solution.py:664
  271.9 330.0 %reduce-scatter.6.cloned.1.call-start = ((), (), s32[]{:S(2)}) async-start(), calls=%async_computation.11 | async-start | bytes 5898240 | tf_op jit(solution)/shard_map/reduce_scatter | solution.py:763
  340.6 50.4 %all-to-all-start.5 = ((bf16[8,2,40,1536]{3,2,1,0:T(8,128)(2,1)}), bf16[8,2,40,1536]{3,2,1,0:T(8,128)(2,1)}, u32[]{:S(2)}, u32[]{:S(2)}) async-start(bf16[8,2,40,1536]{3,2,1,0:T(8,128)(2,1)} %bitcast.233), calls=%async_computation.5 | async-start | bytes 3932160 | tf_op jit(solution)/shard_map/all_to_all | solution.py:664
  346.5 255.4 %reduce-scatter.8.cloned.1.call-start = ((), (), s32[]{:S(2)}) async-start(), calls=%async_computation.12 | async-start | bytes 5898240 | tf_op jit(solution)/shard_map/reduce_scatter | solution.py:762
  347.1 261.4 %reduce-scatter.10.cloned.1.call-start = ((), (), s32[]{:S(2)}) async-start(), calls=%async_computation.14 | async-start | bytes 5068800
  376.0 77.0 %collective-permute-start.11 = (bf16[2,16,1536]{2,1,0:T(8,128)(2,1)}, bf16[2,16,1536]{2,1,0:T(8,128)(2,1)}, u32[]{:S(2)}, u32[]{:S(2)}) collective-permute-start(bf16[2,16,1536]{2,1,0:T(8,128)(2,1)} %convert_element_type.381), channel_id=1, source_target_pairs={{0,1},{1,0},{2,3},{3,2},{4,5},{5,4},{6,7},{7,6},{8,9},{9,8},{10,11... | collective-permute-start | bytes 294920 | tf_op jit(solution)/shard_map/ppermute | solution.py:357
  436.0 16.9 %collective-permute-start.14 = (bf16[2,16,1536]{2,1,0:T(8,128)(2,1)}, bf16[2,16,1536]{2,1,0:T(8,128)(2,1)}, u32[]{:S(2)}, u32[]{:S(2)}) collective-permute-start(bf16[2,16,1536]{2,1,0:T(8,128)(2,1)} %convert_element_type.391), channel_id=1, source_target_pairs={{0,1},{1,0},{2,3},{3,2},{4,5},{5,4},{6,7},{7,6},{8,9},{9,8},{10,11... | collective-permute-start | bytes 294920 | tf_op jit(solution)/shard_map/ppermute | solution.py:357
  507.0 47.9 %collective-permute-start.13 = (f32[2,8,1536]{2,1,0:T(8,128)}, f32[2,8,1536]{2,1,0:T(8,128)}, u32[]{:S(2)}, u32[]{:S(2)}) collective-permute-start(f32[2,8,1536]{2,1,0:T(8,128)} %slice.443), channel_id=1, source_target_pairs={{1,0},{2,1},{3,2},{5,4},{6,5},{7,6},{9,8},{10,9},{11,10},{13,12},{... | collective-permute-start | bytes 294920 | tf_op jit(solution)/shard_map/ppermute | solution.py:362
  548.9 8.3 %collective-permute-start.16 = (f32[2,8,1536]{2,1,0:T(8,128)}, f32[2,8,1536]{2,1,0:T(8,128)}, u32[]{:S(2)}, u32[]{:S(2)}) collective-permute-start(f32[2,8,1536]{2,1,0:T(8,128)} %slice.450), channel_id=1, source_target_pairs={{1,0},{2,1},{3,2},{5,4},{6,5},{7,6},{9,8},{10,9},{11,10},{13,12},{... | collective-permute-start | bytes 294920 | tf_op jit(solution)/shard_map/ppermute | solution.py:362
  567.7 14.8 %collective-permute-start.17 = (bf16[8,2,1,24,1536]{4,3,2,1,0:T(8,128)(2,1)}, bf16[8,2,1,24,1536]{4,3,2,1,0:T(8,128)(2,1)}, u32[]{:S(2)}, u32[]{:S(2)}) collective-permute-start(bf16[8,2,1,24,1536]{4,3,2,1,0:T(8,128)(2,1)} %dynamic-slice_convert_fusion), channel_id=1, source_target_pairs={{0,1},{1,0},{2,3},{3,2},{4,5},{5,4},{6,7},{7,6},{8,9},{9,8},{10,11... | collective-permute-start | bytes 3538952 | tf_op jit(solution)/shard_map/ppermute | solution.py:357
  579.8 8.4 %collective-permute-start.20 = (bf16[8,1,1,24,512]{4,3,2,1,0:T(8,128)(2,1)S(1)}, bf16[8,1,1,24,512]{4,3,2,1,0:T(8,128)(2,1)S(1)}, u32[]{:S(2)}, u32[]{:S(2)}) collective-permute-start(bf16[8,1,1,24,512]{4,3,2,1,0:T(8,128)(2,1)S(1)} %dynamic-slice_convert_fusion.3), channel_id=1, source_target_pairs={{0,2},{1,3},{2,0},{3,1},{4,6},{5,7},{6,4},{7,5},{8,10},{9,11},{10,... | collective-permute-start | bytes 589832 | tf_op jit(solution)/shard_map/ppermute | solution.py:357
  584.2 16.6 %collective-permute-start.18 = (bf16[8,1,1,24,1536]{4,3,2,1,0:T(8,128)(2,1)S(1)}, bf16[8,1,1,24,1536]{4,3,2,1,0:T(8,128)(2,1)S(1)}, u32[]{:S(2)}, u32[]{:S(2)}) collective-permute-start(bf16[8,1,1,24,1536]{4,3,2,1,0:T(8,128)(2,1)S(1)} %dynamic-slice_convert_fusion.1), channel_id=1, source_target_pairs={{0,2},{1,3},{2,0},{3,1},{4,6},{5,7},{6,4},{7,5},{8,10},{9,11},{10,... | collective-permute-start | bytes 1769480 | tf_op jit(solution)/shard_map/ppermute | solution.py:357
  615.8 24.1 %all-to-all-start.6 = ((bf16[8,24,2048]{2,1,0:T(8,128)(2,1)}), bf16[8,24,2048]{2,1,0:T(8,128)(2,1)S(1)}, u32[]{:S(2)}, u32[]{:S(2)}) async-start(bf16[8,24,2048]{2,1,0:T(8,128)(2,1)} %pad_maximum_fusion.7), calls=%async_computation.8 | async-start | bytes 1572864 | tf_op jit(solution)/shard_map/all_to_all | solution.py:390
  (211 other events, 2062.1 us)
Sparse Core Ops, SparseCore 0:
  32.5 66.0 all-gather.3
  119.8 65.7 all-gather.5
  340.8 49.2 reduce-scatter.5
  392.6 47.7 reduce-scatter.7
  460.1 105.2 reduce-scatter.9

commit v6 on v5

--- a/solution.py
+++ b/solution.py
@@ -255,6 +255,8 @@
         for q in range(pieces):
             copies[q].start()
             copies[q + pieces].start()
+        out_s[...] = jnp.zeros_like(out_s)
+        gin_s[...] = jnp.zeros_like(gin_s)
 
     for q in range(pieces):
         @pl.when(j == q)
@@ -279,15 +281,8 @@
         out = mm(value, second, ((1,), (0,)))
         gin = mm(grad, first, ((1,), (1,)))
 
-        @pl.when(j == 0)
-        def _():
-            out_s[at, :] = out
-            gin_s[at, :] = gin
-
-        @pl.when(j > 0)
-        def _():
-            out_s[at, :] += out
-            gin_s[at, :] += gin
+        out_s[at, :] += out
+        gin_s[at, :] += gin
 
     @pl.when(j == pieces - 1)
     def _():

time: 659 us -> 657 us (level)
  transfers between devices with their start and end apart: 33 -> 33, of which waited for: 15 -> 15; matrix products, arithmetic and copies ran while one was open for 32% -> 32% of each run, Pallas kernels for 33% -> 32%
where the time goes in v6:
time: 657 us; the launch traced here: 650 us
  Pallas kernels  210 us (32%)
  matrix products  135 us (21%)
  waiting for transfers between devices  91.9 us (14%)
  local copies, waits for them, and re-layouts  72.8 us (11%)
  other arithmetic  70.4 us (11%)
  starting transfers between devices  53.1 us (8%)
  between operations  16.8 us (3%)
    dot_general x46, matrix products, mm(): lax.dot_general(left, right, (dims, ((), ())), preferred_element_type=F32)  132 us
    pallas_call x2, Pallas kernels, scan_bwd(): pl.pallas_call(functools.partial(bwd_kernel, T // U), grid=(S, C // cb),...  68.8 us
    unnamed x413, local copies, waits for them, and re-layouts  43.4 us
    pallas_call x2, Pallas kernels, scan_end_b(): pl.pallas_call(functools.partial(end_b_kernel, T // U), grid=(S, C // cb)...  40.7 us
    pallas_call x2, Pallas kernels, expert_call(): pl.pallas_call(functools.partial(expert_kernel, pieces, tile, second_at),...  39.5 us
    ppermute x18, waiting for transfers between devices, swap(): return lax.ppermute(x, axis, [(i, i ^ 1 << k) for i in range(count)])  37.4 us
    pallas_call x2, Pallas kernels, scan_fwd(): pl.pallas_call(functools.partial(fwd_kernel, T // U), grid=(S, C // cb),...  36.1 us
    all_to_all x2, waiting for transfers between devices, forward(): lax.all_to_all(send, 'batch', split_axis=0, concat_axis=0, tiled=True)  31.3 us
  transfers between devices with their start and end apart: 33, of which 15 were waited for; matrix products, arithmetic and copies ran while one was open for 32% of the time, Pallas kernels for 32%

profile of v6, /device:TPU:0, one launch (start us, length us, event | category | flops | bytes accessed | tf_op | source)
XLA Modules:
  0.0 649.9 jit_solution(13892444034554530698)
XLA Ops:
  9.2 7.3 %all-to-all-start = ((bf16[8,24,1536]{2,1,0:T(8,128)(2,1)}), bf16[8,24,1536]{2,1,0:T(8,128)(2,1)S(1)}, u32[]{:S(2)}, u32[]{:S(2)}) async-start(bf16[8,24,1536]{2,1,0:T(8,128)(2,1)} %broadcast_in_dim.105), calls=%async_computation | async-start | bytes 1179648 | tf_op jit(solution)/shard_map/all_to_all | solution.py:373
  25.4 6.9 %all-to-all-done = bf16[8,24,1536]{2,1,0:T(8,128)(2,1)S(1)} async-done(((bf16[8,24,1536]{2,1,0:T(8,128)(2,1)}), bf16[8,24,1536]{2,1,0:T(8,128)(2,1)S(1)}, u32[]{:S(2)}, u32[]{:S(2)}) %all-to-all-start) | async-done | bytes 589856 | tf_op jit(solution)/shard_map/all_to_all | solution.py:373
  45.2 13.4 %collective-permute-done.3 = bf16[8,1,1,24,1536]{4,3,2,1,0:T(8,128)(2,1)S(1)} collective-permute-done((bf16[8,1,1,24,1536]{4,3,2,1,0:T(8,128)(2,1)S(1)}, bf16[8,1,1,24,1536]{4,3,2,1,0:T(8,128)(2,1)S(1)}, u32[]{:S(2)}, u32[]{:S(2)}) %collective-permute-start.3) | collective-permute-done | bytes 589856 | tf_op jit(solution)/shard_map/ppermute | solution.py:352
  80.8 12.3 %scan_end_f.2 = f32[2,16,1536]{2,1,0:T(8,128)S(1)} custom-call(f32[2,256,1536]{2,1,0:T(8,128)S(1)} %copy-done, bf16[2,256,1536]{2,1,0:T(8,128)(2,1)S(1)} %get-tuple-element.230.x_ref, f32[2,16,32,16]{3,2,1,0:T(8,128)S(1)} %bitcast.225, f32[16,1536]{1,0:T(8,128)S(1)} %get-tuple-element.259.r_ref), custom_call_target="tpu_custom_call" | custom-call | flops 786432 | bytes 786432 | tf_op jit(solution)/shard_map/scan_end_f/pallas_call | solution.py:51
  99.9 18.1 %scan_fwd.2 = (f32[2,256,1536]{2,1,0:T(8,128)S(1)}, bf16[2,4096,1536]{2,1,0:T(8,128)(2,1)}) custom-call(f32[2,256,1536]{2,1,0:T(8,128)} %get-tuple-element.289.s_ref, bf16[2,256,1536]{2,1,0:T(8,128)(2,1)S(1)} %get-tuple-element.230.x_ref, f32[2,16,32,16]{3,2,1,0:T(8,128)S(1)} %bitcast.226, bf16[2,256,256]{2,1,0:T(8,128)(2,1)S(1)} %fusion.48.l_ref, ...), custom_call_target="tpu_custom_call" | custom-call | flops 786432 | bytes 786432 | tf_op jit(solution)/shard_map/scan_fwd/pallas_call | solution.py:133
  157.1 12.3 %scan_end_f.3 = f32[2,16,1536]{2,1,0:T(8,128)S(1)} custom-call(f32[2,256,1536]{2,1,0:T(8,128)S(1)} %copy-done.2, bf16[2,256,1536]{2,1,0:T(8,128)(2,1)S(1)} %get-tuple-element.226.x_ref, f32[2,16,32,16]{3,2,1,0:T(8,128)S(1)} %bitcast.229, f32[16,1536]{1,0:T(8,128)S(1)} %get-tuple-element.259.r_ref), custom_call_target="tpu_custom_call" | custom-call | flops 786432 | bytes 786432 | tf_op jit(solution)/shard_map/scan_end_f/pallas_call | solution.py:51
  178.7 6.7 %all-to-all-done.2 = bf16[8,2,40,1536]{3,2,1,0:T(8,128)(2,1)} async-done(((bf16[8,2,40,1536]{3,2,1,0:T(8,128)(2,1)}), bf16[8,2,40,1536]{3,2,1,0:T(8,128)(2,1)}, u32[]{:S(2)}, u32[]{:S(2)}) %all-to-all-start.2) | async-done | bytes 1966112 | tf_op jit(solution)/shard_map/all_to_all | solution.py:648
  187.4 18.0 %scan_fwd.3 = (f32[2,256,1536]{2,1,0:T(8,128)S(1)}, bf16[2,4096,1536]{2,1,0:T(8,128)(2,1)}) custom-call(f32[2,256,1536]{2,1,0:T(8,128)} %get-tuple-element.299.s_ref, bf16[2,256,1536]{2,1,0:T(8,128)(2,1)S(1)} %get-tuple-element.226.x_ref, f32[2,16,32,16]{3,2,1,0:T(8,128)S(1)} %bitcast.230, bf16[2,256,256]{2,1,0:T(8,128)(2,1)S(1)} %copy-done.24, ...), custom_call_target="tpu_custom_call" | custom-call | flops 786432 | bytes 786432 | tf_op jit(solution)/shard_map/scan_fwd/pallas_call | solution.py:133
  205.5 6.2 multiply_convert_fusion.2
  222.6 19.1 %expert.2 = (bf16[640,1536]{1,0:T(8,128)(2,1)S(1)}, bf16[1280,3072]{1,0:T(8,128)(2,1)}, bf16[1280,3072]{1,0:T(8,128)(2,1)}) custom-call(bf16[640,1536]{1,0:T(8,128)(2,1)} %bitcast.35.x_ref, bf16[4,1536,768]{2,1,0:T(8,128)(2,1)} %bitcast.235, bf16[4,1536,768]{2,1,0:T(8,128)(2,1)} %bitcast.236), custom_call_target="tpu_custom_call" | custom-call | flops 491520 | bytes 491520 | tf_op jit(solution)/shard_map/expert/pallas_call | solution.py:302
  242.9 24.6 %all-to-all-done.4 = bf16[8,2,40,1536]{3,2,1,0:T(8,128)(2,1)} async-done(((bf16[8,2,40,1536]{3,2,1,0:T(8,128)(2,1)}), bf16[8,2,40,1536]{3,2,1,0:T(8,128)(2,1)}, u32[]{:S(2)}, u32[]{:S(2)}) %all-to-all-start.4) | async-done | bytes 1966112 | tf_op jit(solution)/shard_map/all_to_all | solution.py:648
  274.3 20.4 %expert.3 = (bf16[640,1536]{1,0:T(8,128)(2,1)S(1)}, bf16[1280,3072]{1,0:T(8,128)(2,1)}, bf16[1280,3072]{1,0:T(8,128)(2,1)}) custom-call(bf16[640,1536]{1,0:T(8,128)(2,1)} %bitcast.48.x_ref, bf16[4,1536,768]{2,1,0:T(8,128)(2,1)} %bitcast.237, bf16[4,1536,768]{2,1,0:T(8,128)(2,1)} %bitcast.238, ...), custom_call_target="tpu_custom_call", output_to_operand_aliasing={{1}: (3, {}), {2}: (4, {})} | custom-call | flops 491520 | bytes 491520 | tf_op jit(solution)/shard_map/expert/pallas_call | solution.py:302
  296.0 11.4 %convolution_convert_fusion.1 = bf16[3072,768]{1,0:T(8,128)(2,1)} fusion(bf16[1280,3072]{1,0:T(8,128)(2,1)} %get-tuple-element.76, bf16[1280,1536]{1,0:T(8,128)(2,1)S(1)} %pad_maximum_fusion), kind=kOutput, calls=%fused_computation.7 | convolution fusion | flops 6042157056 | bytes 14548992 | tf_op jit(solution)/shard_map/dot_general | solution.py:437
  307.4 11.1 %convolution_convert_fusion = bf16[3072,768]{1,0:T(8,128)(2,1)} fusion(bf16[1280,3072]{1,0:T(8,128)(2,1)} %get-tuple-element.78, bf16[1280,1536]{1,0:T(8,128)(2,1)} %copy-done.81), kind=kOutput, calls=%fused_computation.6 | convolution fusion | flops 6042157056 | bytes 14548992 | tf_op jit(solution)/shard_map/dot_general | solution.py:437
  332.5 6.4 fusion.9
  338.8 5.9 all-to-all-start.5
  352.3 20.4 %scan_end_b.2 = (f32[2,16,1536]{2,1,0:T(8,128)S(1)}, f32[2,256,256]{2,1,0:T(8,128)S(1)}) custom-call(f32[2,256,1536]{2,1,0:T(8,128)S(1)} %copy-done.1, f32[2,256,1536]{2,1,0:T(8,128)} %get-tuple-element.223.g_ref, f32[2,16,32,16]{3,2,1,0:T(8,128)S(1)} %bitcast.227, f32[16,1536]{1,0:T(8,128)S(1)} %get-tuple-element.259.r_ref, ...), custom_call_target="tpu_custom_call" | custom-call | flops 786432 | bytes 786432 | tf_op jit(solution)/shard_map/scan_end_b/pallas_call | solution.py:88
  378.0 5.3 fusion.67
  405.4 6.4 fusion.11
  411.8 20.3 %scan_end_b.3 = (f32[2,16,1536]{2,1,0:T(8,128)S(1)}, f32[2,256,256]{2,1,0:T(8,128)S(1)}) custom-call(f32[2,256,1536]{2,1,0:T(8,128)S(1)} %copy-done.3, f32[2,256,1536]{2,1,0:T(8,128)} %get-tuple-element.221.g_ref, f32[2,16,32,16]{3,2,1,0:T(8,128)S(1)} %bitcast.231, f32[16,1536]{1,0:T(8,128)S(1)} %get-tuple-element.259.r_ref, ...), custom_call_target="tpu_custom_call" | custom-call | flops 786432 | bytes 786432 | tf_op jit(solution)/shard_map/scan_end_b/pallas_call | solution.py:88
  463.9 34.6 %scan_bwd.2 = (bf16[2,256,1536]{2,1,0:T(8,128)(2,1)S(1)}, f32[2,256,1536]{2,1,0:T(8,128)}, f32[2,8,1536]{2,1,0:T(8,128)S(1)}, f32[2,16,1536]{2,1,0:T(8,128)S(1)}, f32[2,256,256]{2,1,0:T(8,128)S(1)}) custom-call(f32[2,256,1536]{2,1,0:T(8,128)} %get-tuple-element.289.s_ref, bf16[2,256,1536]{2,1,0:T(8,128)(2,1)S(1)} %get-tuple-element.230.x_ref, ...), custom_call_target="tpu_custom_call" | custom-call | flops 786432 | bytes 786432 | tf_op jit(solution)/shard_map/scan_bwd/pallas_call | solution.py:217
  506.5 34.2 %scan_bwd.3 = (bf16[2,256,1536]{2,1,0:T(8,128)(2,1)S(1)}, f32[2,256,1536]{2,1,0:T(8,128)}, f32[2,8,1536]{2,1,0:T(8,128)S(1)}, f32[2,16,1536]{2,1,0:T(8,128)S(1)}, f32[2,256,256]{2,1,0:T(8,128)S(1)}) custom-call(f32[2,256,1536]{2,1,0:T(8,128)} %get-tuple-element.299.s_ref, bf16[2,256,1536]{2,1,0:T(8,128)(2,1)S(1)} %get-tuple-element.226.x_ref, ...), custom_call_target="tpu_custom_call" | custom-call | flops 786432 | bytes 786432 | tf_op jit(solution)/shard_map/scan_bwd/pallas_call | solution.py:217
  586.5 12.5 %collective-permute-done.18 = bf16[8,1,1,24,1536]{4,3,2,1,0:T(8,128)(2,1)S(1)} collective-permute-done((bf16[8,1,1,24,1536]{4,3,2,1,0:T(8,128)(2,1)S(1)}, bf16[8,1,1,24,1536]{4,3,2,1,0:T(8,128)(2,1)S(1)}, u32[]{:S(2)}, u32[]{:S(2)}) %collective-permute-start.18) | collective-permute-done | bytes 589856 | tf_op jit(solution)/shard_map/ppermute | solution.py:352
  626.6 11.5 %all-to-all-done.6 = bf16[8,24,2048]{2,1,0:T(8,128)(2,1)S(1)} async-done(((bf16[8,24,2048]{2,1,0:T(8,128)(2,1)}), bf16[8,24,2048]{2,1,0:T(8,128)(2,1)S(1)}, u32[]{:S(2)}, u32[]{:S(2)}) %all-to-all-start.6) | async-done | bytes 786464 | tf_op jit(solution)/shard_map/all_to_all | solution.py:385
  (687 shorter events, 287.7 us)
Async XLA Ops:
  9.2 23.1 %all-to-all-start = ((bf16[8,24,1536]{2,1,0:T(8,128)(2,1)}), bf16[8,24,1536]{2,1,0:T(8,128)(2,1)S(1)}, u32[]{:S(2)}, u32[]{:S(2)}) async-start(bf16[8,24,1536]{2,1,0:T(8,128)(2,1)} %broadcast_in_dim.105), calls=%async_computation | async-start | bytes 1179648 | tf_op jit(solution)/shard_map/all_to_all | solution.py:373
  16.4 103.2 %all-gather.4.cloned.1.call-start = ((), (), s32[]{:S(2)}) async-start(), calls=%async_computation.10 | async-start | bytes 4866048 | tf_op jit(solution)/shard_map/all_gather | solution.py:544
  21.6 15.8 %collective-permute-start = (bf16[1,1,1,24,384]{4,3,2,1,0:T(8,128)(2,1)S(1)}, bf16[1,1,1,24,384]{4,3,2,1,0:T(8,128)(2,1)S(1)}, u32[]{:S(2)}, u32[]{:S(2)}) collective-permute-start(bf16[1,1,1,24,384]{4,3,2,1,0:T(8,128)(2,1)S(1)} %fusion.123), channel_id=1, source_target_pairs={{0,2},{1,3},{2,0},{3,1},{4,6},{5,7},{6,4},{7,5},{8,10},{9,11},{10,... | collective-permute-start | bytes 55304 | tf_op jit(solution)/shard_map/ppermute | solution.py:352
  23.1 21.7 %collective-permute-start.2 = (bf16[4,8,768]{2,1,0:T(8,128)(2,1)S(1)}, bf16[4,8,768]{2,1,0:T(8,128)(2,1)S(1)}, u32[]{:S(2)}, u32[]{:S(2)}) collective-permute-start(bf16[4,8,768]{2,1,0:T(8,128)(2,1)S(1)} %slice.313), channel_id=1, source_target_pairs={{0,1},{1,2},{2,3},{4,5},{5,6},{6,7},{8,9},{9,10},{10,11},{12,13},{... | collective-permute-start | bytes 147464 | tf_op jit(solution)/shard_map/ppermute | solution.py:357
  39.6 22.0 %all-to-all-start.1 = ((bf16[8,96,384]{2,1,0:T(8,128)(2,1)}), bf16[8,96,384]{2,1,0:T(8,128)(2,1)S(1)}, u32[]{:S(2)}, u32[]{:S(2)}) async-start(bf16[8,96,384]{2,1,0:T(8,128)(2,1)} %broadcast_in_dim.106), calls=%async_computation.1 | async-start | bytes 1179648 | tf_op jit(solution)/shard_map/all_to_all | solution.py:373
  43.2 179.4 %all-gather.6.cloned.1.call-start = ((), (), s32[]{:S(2)}) async-start(), calls=%async_computation.13 | async-start | bytes 11796480 | tf_op jit(solution)/shard_map/all_gather | solution.py:549
  43.3 15.4 %collective-permute-start.3 = (bf16[8,1,1,24,1536]{4,3,2,1,0:T(8,128)(2,1)S(1)}, bf16[8,1,1,24,1536]{4,3,2,1,0:T(8,128)(2,1)S(1)}, u32[]{:S(2)}, u32[]{:S(2)}) collective-permute-start(bf16[8,1,1,24,1536]{4,3,2,1,0:T(8,128)(2,1)S(1)} %bitcast.270), channel_id=1, source_target_pairs={{0,2},{1,3},{2,0},{3,1},{4,6},{5,7},{6,4},{7,5},{8,10},{9,11},{10,... | collective-permute-start | bytes 1769480 | tf_op jit(solution)/shard_map/ppermute | solution.py:352
  78.2 15.5 %collective-permute-start.6 = (f32[2,1536]{1,0:T(2,128)S(1)}, f32[2,1536]{1,0:T(2,128)S(1)}, u32[]{:S(2)}, u32[]{:S(2)}) collective-permute-start(f32[2,1536]{1,0:T(2,128)S(1)} %get-tuple-element.288), channel_id=1, source_target_pairs={{0,1},{1,0},{2,3},{3,2},{4,5},{5,4},{6,7},{7,6},{8,9},{9,8},{10,11... | collective-permute-start | bytes 36872 | tf_op jit(solution)/shard_map/ppermute | solution.py:352
  135.1 50.3 %all-to-all-start.2 = ((bf16[8,2,40,1536]{3,2,1,0:T(8,128)(2,1)}), bf16[8,2,40,1536]{3,2,1,0:T(8,128)(2,1)}, u32[]{:S(2)}, u32[]{:S(2)}) async-start(bf16[8,2,40,1536]{3,2,1,0:T(8,128)(2,1)} %bitcast.256), calls=%async_computation.2 | async-start | bytes 3932160 | tf_op jit(solution)/shard_map/all_to_all | solution.py:648
  151.3 18.7 %collective-permute-start.9 = (f32[2,1536]{1,0:T(2,128)S(1)}, f32[2,1536]{1,0:T(2,128)S(1)}, u32[]{:S(2)}, u32[]{:S(2)}) collective-permute-start(f32[2,1536]{1,0:T(2,128)S(1)} %get-tuple-element.298), channel_id=1, source_target_pairs={{0,1},{1,0},{2,3},{3,2},{4,5},{5,4},{6,7},{7,6},{8,9},{9,8},{10,11... | collective-permute-start | bytes 36872 | tf_op jit(solution)/shard_map/ppermute | solution.py:352
  218.0 49.5 %all-to-all-start.4 = ((bf16[8,2,40,1536]{3,2,1,0:T(8,128)(2,1)}), bf16[8,2,40,1536]{3,2,1,0:T(8,128)(2,1)}, u32[]{:S(2)}, u32[]{:S(2)}) async-start(bf16[8,2,40,1536]{3,2,1,0:T(8,128)(2,1)} %bitcast.257), calls=%async_computation.4 | async-start | bytes 3932160 | tf_op jit(solution)/shard_map/all_to_all | solution.py:648
  267.5 51.0 %all-to-all-start.3 = ((bf16[8,2,40,1536]{3,2,1,0:T(8,128)(2,1)}), bf16[8,2,40,1536]{3,2,1,0:T(8,128)(2,1)}, u32[]{:S(2)}, u32[]{:S(2)}) async-start(bf16[8,2,40,1536]{3,2,1,0:T(8,128)(2,1)} %bitcast.234), calls=%async_computation.3 | async-start | bytes 3932160 | tf_op jit(solution)/shard_map/all_to_all | solution.py:659
  271.9 328.2 %reduce-scatter.6.cloned.1.call-start = ((), (), s32[]{:S(2)}) async-start(), calls=%async_computation.11 | async-start | bytes 5898240 | tf_op jit(solution)/shard_map/reduce_scatter | solution.py:758
  338.8 50.4 %all-to-all-start.5 = ((bf16[8,2,40,1536]{3,2,1,0:T(8,128)(2,1)}), bf16[8,2,40,1536]{3,2,1,0:T(8,128)(2,1)}, u32[]{:S(2)}, u32[]{:S(2)}) async-start(bf16[8,2,40,1536]{3,2,1,0:T(8,128)(2,1)} %bitcast.233), calls=%async_computation.5 | async-start | bytes 3932160 | tf_op jit(solution)/shard_map/all_to_all | solution.py:659
  344.7 255.4 %reduce-scatter.8.cloned.1.call-start = ((), (), s32[]{:S(2)}) async-start(), calls=%async_computation.12 | async-start | bytes 5898240 | tf_op jit(solution)/shard_map/reduce_scatter | solution.py:757
  345.3 261.4 %reduce-scatter.10.cloned.1.call-start = ((), (), s32[]{:S(2)}) async-start(), calls=%async_computation.14 | async-start | bytes 5068800
  374.2 77.0 %collective-permute-start.11 = (bf16[2,16,1536]{2,1,0:T(8,128)(2,1)}, bf16[2,16,1536]{2,1,0:T(8,128)(2,1)}, u32[]{:S(2)}, u32[]{:S(2)}) collective-permute-start(bf16[2,16,1536]{2,1,0:T(8,128)(2,1)} %convert_element_type.381), channel_id=1, source_target_pairs={{0,1},{1,0},{2,3},{3,2},{4,5},{5,4},{6,7},{7,6},{8,9},{9,8},{10,11... | collective-permute-start | bytes 294920 | tf_op jit(solution)/shard_map/ppermute | solution.py:352
  434.2 16.9 %collective-permute-start.14 = (bf16[2,16,1536]{2,1,0:T(8,128)(2,1)}, bf16[2,16,1536]{2,1,0:T(8,128)(2,1)}, u32[]{:S(2)}, u32[]{:S(2)}) collective-permute-start(bf16[2,16,1536]{2,1,0:T(8,128)(2,1)} %convert_element_type.391), channel_id=1, source_target_pairs={{0,1},{1,0},{2,3},{3,2},{4,5},{5,4},{6,7},{7,6},{8,9},{9,8},{10,11... | collective-permute-start | bytes 294920 | tf_op jit(solution)/shard_map/ppermute | solution.py:352
  505.2 47.9 %collective-permute-start.13 = (f32[2,8,1536]{2,1,0:T(8,128)}, f32[2,8,1536]{2,1,0:T(8,128)}, u32[]{:S(2)}, u32[]{:S(2)}) collective-permute-start(f32[2,8,1536]{2,1,0:T(8,128)} %slice.443), channel_id=1, source_target_pairs={{1,0},{2,1},{3,2},{5,4},{6,5},{7,6},{9,8},{10,9},{11,10},{13,12},{... | collective-permute-start | bytes 294920 | tf_op jit(solution)/shard_map/ppermute | solution.py:357
  547.2 8.3 %collective-permute-start.16 = (f32[2,8,1536]{2,1,0:T(8,128)}, f32[2,8,1536]{2,1,0:T(8,128)}, u32[]{:S(2)}, u32[]{:S(2)}) collective-permute-start(f32[2,8,1536]{2,1,0:T(8,128)} %slice.450), channel_id=1, source_target_pairs={{1,0},{2,1},{3,2},{5,4},{6,5},{7,6},{9,8},{10,9},{11,10},{13,12},{... | collective-permute-start | bytes 294920 | tf_op jit(solution)/shard_map/ppermute | solution.py:357
  565.9 14.7 %collective-permute-start.17 = (bf16[8,2,1,24,1536]{4,3,2,1,0:T(8,128)(2,1)}, bf16[8,2,1,24,1536]{4,3,2,1,0:T(8,128)(2,1)}, u32[]{:S(2)}, u32[]{:S(2)}) collective-permute-start(bf16[8,2,1,24,1536]{4,3,2,1,0:T(8,128)(2,1)} %dynamic-slice_convert_fusion), channel_id=1, source_target_pairs={{0,1},{1,0},{2,3},{3,2},{4,5},{5,4},{6,7},{7,6},{8,9},{9,8},{10,11... | collective-permute-start | bytes 3538952 | tf_op jit(solution)/shard_map/ppermute | solution.py:352
  578.1 8.4 %collective-permute-start.20 = (bf16[8,1,1,24,512]{4,3,2,1,0:T(8,128)(2,1)S(1)}, bf16[8,1,1,24,512]{4,3,2,1,0:T(8,128)(2,1)S(1)}, u32[]{:S(2)}, u32[]{:S(2)}) collective-permute-start(bf16[8,1,1,24,512]{4,3,2,1,0:T(8,128)(2,1)S(1)} %dynamic-slice_convert_fusion.3), channel_id=1, source_target_pairs={{0,2},{1,3},{2,0},{3,1},{4,6},{5,7},{6,4},{7,5},{8,10},{9,11},{10,... | collective-permute-start | bytes 589832 | tf_op jit(solution)/shard_map/ppermute | solution.py:352
  582.4 16.6 %collective-permute-start.18 = (bf16[8,1,1,24,1536]{4,3,2,1,0:T(8,128)(2,1)S(1)}, bf16[8,1,1,24,1536]{4,3,2,1,0:T(8,128)(2,1)S(1)}, u32[]{:S(2)}, u32[]{:S(2)}) collective-permute-start(bf16[8,1,1,24,1536]{4,3,2,1,0:T(8,128)(2,1)S(1)} %dynamic-slice_convert_fusion.1), channel_id=1, source_target_pairs={{0,2},{1,3},{2,0},{3,1},{4,6},{5,7},{6,4},{7,5},{8,10},{9,11},{10,... | collective-permute-start | bytes 1769480 | tf_op jit(solution)/shard_map/ppermute | solution.py:352
  614.0 24.1 %all-to-all-start.6 = ((bf16[8,24,2048]{2,1,0:T(8,128)(2,1)}), bf16[8,24,2048]{2,1,0:T(8,128)(2,1)S(1)}, u32[]{:S(2)}, u32[]{:S(2)}) async-start(bf16[8,24,2048]{2,1,0:T(8,128)(2,1)} %pad_maximum_fusion.7), calls=%async_computation.8 | async-start | bytes 1572864 | tf_op jit(solution)/shard_map/all_to_all | solution.py:385
  (211 other events, 2056.5 us)
Sparse Core Ops, SparseCore 0:
  32.5 66.0 all-gather.3
  119.8 65.7 all-gather.5
  339.0 49.2 reduce-scatter.5
  390.8 47.8 reduce-scatter.7
  458.4 105.1 reduce-scatter.9

commit v7 on v6

--- a/solution.py
+++ b/solution.py
@@ -18,7 +18,7 @@
 BF = jnp.bfloat16
 U = 16
 CB = 512
-CE = 768
+CE = 1536
 VM = 48 << 20
 EXPERT_VM = 48 << 20
 COST = 1

time: 657 us -> 656 us (level)
  no operation moved by 1% of the time
where the time goes in v7:
time: 656 us; the launch traced here: 649 us
  Pallas kernels  207 us (32%)
  matrix products  135 us (21%)
  waiting for transfers between devices  93.3 us (14%)
  local copies, waits for them, and re-layouts  72.9 us (11%)
  other arithmetic  70.4 us (11%)
  starting transfers between devices  53.1 us (8%)
  between operations  16.9 us (3%)
    dot_general x46, matrix products, mm(): lax.dot_general(left, right, (dims, ((), ())), preferred_element_type=F32)  132 us
    pallas_call x2, Pallas kernels, scan_bwd(): pl.pallas_call(functools.partial(bwd_kernel, T // U), grid=(S, C // cb),...  68.8 us
    unnamed x413, local copies, waits for them, and re-layouts  43.4 us
    pallas_call x2, Pallas kernels, scan_end_b(): pl.pallas_call(functools.partial(end_b_kernel, T // U), grid=(S, C // cb)...  39.8 us
    pallas_call x2, Pallas kernels, expert_call(): pl.pallas_call(functools.partial(expert_kernel, pieces, tile, second_at),...  39.5 us
    ppermute x18, waiting for transfers between devices, swap(): return lax.ppermute(x, axis, [(i, i ^ 1 << k) for i in range(count)])  37.4 us
    pallas_call x2, Pallas kernels, scan_fwd(): pl.pallas_call(functools.partial(fwd_kernel, T // U), grid=(S, C // cb),...  36.1 us
    all_to_all x2, waiting for transfers between devices, forward(): lax.all_to_all(send, 'batch', split_axis=0, concat_axis=0, tiled=True)  32.2 us
  transfers between devices with their start and end apart: 33, of which 15 were waited for; matrix products, arithmetic and copies ran while one was open for 32% of the time, Pallas kernels for 32%

profile of v7, /device:TPU:0, one launch (start us, length us, event | category | flops | bytes accessed | tf_op | source)
XLA Modules:
  0.0 648.8 jit_solution(10556636346323183418)
XLA Ops:
  9.2 7.3 %all-to-all-start = ((bf16[8,24,1536]{2,1,0:T(8,128)(2,1)}), bf16[8,24,1536]{2,1,0:T(8,128)(2,1)S(1)}, u32[]{:S(2)}, u32[]{:S(2)}) async-start(bf16[8,24,1536]{2,1,0:T(8,128)(2,1)} %broadcast_in_dim.105), calls=%async_computation | async-start | bytes 1179648 | tf_op jit(solution)/shard_map/all_to_all | solution.py:373
  25.4 6.9 %all-to-all-done = bf16[8,24,1536]{2,1,0:T(8,128)(2,1)S(1)} async-done(((bf16[8,24,1536]{2,1,0:T(8,128)(2,1)}), bf16[8,24,1536]{2,1,0:T(8,128)(2,1)S(1)}, u32[]{:S(2)}, u32[]{:S(2)}) %all-to-all-start) | async-done | bytes 589856 | tf_op jit(solution)/shard_map/all_to_all | solution.py:373
  45.2 13.4 %collective-permute-done.3 = bf16[8,1,1,24,1536]{4,3,2,1,0:T(8,128)(2,1)S(1)} collective-permute-done((bf16[8,1,1,24,1536]{4,3,2,1,0:T(8,128)(2,1)S(1)}, bf16[8,1,1,24,1536]{4,3,2,1,0:T(8,128)(2,1)S(1)}, u32[]{:S(2)}, u32[]{:S(2)}) %collective-permute-start.3) | collective-permute-done | bytes 589856 | tf_op jit(solution)/shard_map/ppermute | solution.py:352
  80.8 11.5 %scan_end_f.2 = f32[2,16,1536]{2,1,0:T(8,128)S(1)} custom-call(f32[2,256,1536]{2,1,0:T(8,128)S(1)} %copy-done, bf16[2,256,1536]{2,1,0:T(8,128)(2,1)S(1)} %get-tuple-element.230.x_ref, f32[2,16,32,16]{3,2,1,0:T(8,128)S(1)} %bitcast.225, f32[16,1536]{1,0:T(8,128)S(1)} %get-tuple-element.259.r_ref), custom_call_target="tpu_custom_call" | custom-call | flops 786432 | bytes 786432 | tf_op jit(solution)/shard_map/scan_end_f/pallas_call | solution.py:51
  99.1 18.1 %scan_fwd.2 = (f32[2,256,1536]{2,1,0:T(8,128)S(1)}, bf16[2,4096,1536]{2,1,0:T(8,128)(2,1)}) custom-call(f32[2,256,1536]{2,1,0:T(8,128)} %get-tuple-element.289.s_ref, bf16[2,256,1536]{2,1,0:T(8,128)(2,1)S(1)} %get-tuple-element.230.x_ref, f32[2,16,32,16]{3,2,1,0:T(8,128)S(1)} %bitcast.226, bf16[2,256,256]{2,1,0:T(8,128)(2,1)S(1)} %fusion.48.l_ref, ...), custom_call_target="tpu_custom_call" | custom-call | flops 786432 | bytes 786432 | tf_op jit(solution)/shard_map/scan_fwd/pallas_call | solution.py:133
  156.3 11.5 %scan_end_f.3 = f32[2,16,1536]{2,1,0:T(8,128)S(1)} custom-call(f32[2,256,1536]{2,1,0:T(8,128)S(1)} %copy-done.2, bf16[2,256,1536]{2,1,0:T(8,128)(2,1)S(1)} %get-tuple-element.226.x_ref, f32[2,16,32,16]{3,2,1,0:T(8,128)S(1)} %bitcast.229, f32[16,1536]{1,0:T(8,128)S(1)} %get-tuple-element.259.r_ref), custom_call_target="tpu_custom_call" | custom-call | flops 786432 | bytes 786432 | tf_op jit(solution)/shard_map/scan_end_f/pallas_call | solution.py:51
  177.2 7.5 %all-to-all-done.2 = bf16[8,2,40,1536]{3,2,1,0:T(8,128)(2,1)} async-done(((bf16[8,2,40,1536]{3,2,1,0:T(8,128)(2,1)}), bf16[8,2,40,1536]{3,2,1,0:T(8,128)(2,1)}, u32[]{:S(2)}, u32[]{:S(2)}) %all-to-all-start.2) | async-done | bytes 1966112 | tf_op jit(solution)/shard_map/all_to_all | solution.py:648
  186.7 18.0 %scan_fwd.3 = (f32[2,256,1536]{2,1,0:T(8,128)S(1)}, bf16[2,4096,1536]{2,1,0:T(8,128)(2,1)}) custom-call(f32[2,256,1536]{2,1,0:T(8,128)} %get-tuple-element.299.s_ref, bf16[2,256,1536]{2,1,0:T(8,128)(2,1)S(1)} %get-tuple-element.226.x_ref, f32[2,16,32,16]{3,2,1,0:T(8,128)S(1)} %bitcast.230, bf16[2,256,256]{2,1,0:T(8,128)(2,1)S(1)} %copy-done.24, ...), custom_call_target="tpu_custom_call" | custom-call | flops 786432 | bytes 786432 | tf_op jit(solution)/shard_map/scan_fwd/pallas_call | solution.py:133
  204.7 6.2 multiply_convert_fusion.2
  221.8 19.1 %expert.2 = (bf16[640,1536]{1,0:T(8,128)(2,1)S(1)}, bf16[1280,3072]{1,0:T(8,128)(2,1)}, bf16[1280,3072]{1,0:T(8,128)(2,1)}) custom-call(bf16[640,1536]{1,0:T(8,128)(2,1)} %bitcast.35.x_ref, bf16[4,1536,768]{2,1,0:T(8,128)(2,1)} %bitcast.235, bf16[4,1536,768]{2,1,0:T(8,128)(2,1)} %bitcast.236), custom_call_target="tpu_custom_call" | custom-call | flops 491520 | bytes 491520 | tf_op jit(solution)/shard_map/expert/pallas_call | solution.py:302
  242.2 24.6 %all-to-all-done.4 = bf16[8,2,40,1536]{3,2,1,0:T(8,128)(2,1)} async-done(((bf16[8,2,40,1536]{3,2,1,0:T(8,128)(2,1)}), bf16[8,2,40,1536]{3,2,1,0:T(8,128)(2,1)}, u32[]{:S(2)}, u32[]{:S(2)}) %all-to-all-start.4) | async-done | bytes 1966112 | tf_op jit(solution)/shard_map/all_to_all | solution.py:648
  273.6 20.4 %expert.3 = (bf16[640,1536]{1,0:T(8,128)(2,1)S(1)}, bf16[1280,3072]{1,0:T(8,128)(2,1)}, bf16[1280,3072]{1,0:T(8,128)(2,1)}) custom-call(bf16[640,1536]{1,0:T(8,128)(2,1)} %bitcast.48.x_ref, bf16[4,1536,768]{2,1,0:T(8,128)(2,1)} %bitcast.237, bf16[4,1536,768]{2,1,0:T(8,128)(2,1)} %bitcast.238, ...), custom_call_target="tpu_custom_call", output_to_operand_aliasing={{1}: (3, {}), {2}: (4, {})} | custom-call | flops 491520 | bytes 491520 | tf_op jit(solution)/shard_map/expert/pallas_call | solution.py:302
  295.3 11.4 %convolution_convert_fusion.1 = bf16[3072,768]{1,0:T(8,128)(2,1)} fusion(bf16[1280,3072]{1,0:T(8,128)(2,1)} %get-tuple-element.76, bf16[1280,1536]{1,0:T(8,128)(2,1)S(1)} %pad_maximum_fusion), kind=kOutput, calls=%fused_computation.7 | convolution fusion | flops 6042157056 | bytes 14548992 | tf_op jit(solution)/shard_map/dot_general | solution.py:437
  306.7 11.1 %convolution_convert_fusion = bf16[3072,768]{1,0:T(8,128)(2,1)} fusion(bf16[1280,3072]{1,0:T(8,128)(2,1)} %get-tuple-element.78, bf16[1280,1536]{1,0:T(8,128)(2,1)} %copy-done.81), kind=kOutput, calls=%fused_computation.6 | convolution fusion | flops 6042157056 | bytes 14548992 | tf_op jit(solution)/shard_map/dot_general | solution.py:437
  331.8 6.4 fusion.9
  338.1 5.9 all-to-all-start.5
  351.6 19.9 %scan_end_b.2 = (f32[2,16,1536]{2,1,0:T(8,128)S(1)}, f32[2,256,256]{2,1,0:T(8,128)S(1)}) custom-call(f32[2,256,1536]{2,1,0:T(8,128)S(1)} %copy-done.1, f32[2,256,1536]{2,1,0:T(8,128)} %get-tuple-element.223.g_ref, f32[2,16,32,16]{3,2,1,0:T(8,128)S(1)} %bitcast.227, f32[16,1536]{1,0:T(8,128)S(1)} %get-tuple-element.259.r_ref, ...), custom_call_target="tpu_custom_call" | custom-call | flops 786432 | bytes 786432 | tf_op jit(solution)/shard_map/scan_end_b/pallas_call | solution.py:88
  376.8 5.3 fusion.67
  404.7 6.4 fusion.11
  411.1 19.9 %scan_end_b.3 = (f32[2,16,1536]{2,1,0:T(8,128)S(1)}, f32[2,256,256]{2,1,0:T(8,128)S(1)}) custom-call(f32[2,256,1536]{2,1,0:T(8,128)S(1)} %copy-done.3, f32[2,256,1536]{2,1,0:T(8,128)} %get-tuple-element.221.g_ref, f32[2,16,32,16]{3,2,1,0:T(8,128)S(1)} %bitcast.231, f32[16,1536]{1,0:T(8,128)S(1)} %get-tuple-element.259.r_ref, ...), custom_call_target="tpu_custom_call" | custom-call | flops 786432 | bytes 786432 | tf_op jit(solution)/shard_map/scan_end_b/pallas_call | solution.py:88
  462.8 34.6 %scan_bwd.2 = (bf16[2,256,1536]{2,1,0:T(8,128)(2,1)S(1)}, f32[2,256,1536]{2,1,0:T(8,128)}, f32[2,8,1536]{2,1,0:T(8,128)S(1)}, f32[2,16,1536]{2,1,0:T(8,128)S(1)}, f32[2,256,256]{2,1,0:T(8,128)S(1)}) custom-call(f32[2,256,1536]{2,1,0:T(8,128)} %get-tuple-element.289.s_ref, bf16[2,256,1536]{2,1,0:T(8,128)(2,1)S(1)} %get-tuple-element.230.x_ref, ...), custom_call_target="tpu_custom_call" | custom-call | flops 786432 | bytes 786432 | tf_op jit(solution)/shard_map/scan_bwd/pallas_call | solution.py:217
  505.3 34.2 %scan_bwd.3 = (bf16[2,256,1536]{2,1,0:T(8,128)(2,1)S(1)}, f32[2,256,1536]{2,1,0:T(8,128)}, f32[2,8,1536]{2,1,0:T(8,128)S(1)}, f32[2,16,1536]{2,1,0:T(8,128)S(1)}, f32[2,256,256]{2,1,0:T(8,128)S(1)}) custom-call(f32[2,256,1536]{2,1,0:T(8,128)} %get-tuple-element.299.s_ref, bf16[2,256,1536]{2,1,0:T(8,128)(2,1)S(1)} %get-tuple-element.226.x_ref, ...), custom_call_target="tpu_custom_call" | custom-call | flops 786432 | bytes 786432 | tf_op jit(solution)/shard_map/scan_bwd/pallas_call | solution.py:217
  585.4 12.5 %collective-permute-done.18 = bf16[8,1,1,24,1536]{4,3,2,1,0:T(8,128)(2,1)S(1)} collective-permute-done((bf16[8,1,1,24,1536]{4,3,2,1,0:T(8,128)(2,1)S(1)}, bf16[8,1,1,24,1536]{4,3,2,1,0:T(8,128)(2,1)S(1)}, u32[]{:S(2)}, u32[]{:S(2)}) %collective-permute-start.18) | collective-permute-done | bytes 589856 | tf_op jit(solution)/shard_map/ppermute | solution.py:352
  625.5 11.5 %all-to-all-done.6 = bf16[8,24,2048]{2,1,0:T(8,128)(2,1)S(1)} async-done(((bf16[8,24,2048]{2,1,0:T(8,128)(2,1)}), bf16[8,24,2048]{2,1,0:T(8,128)(2,1)S(1)}, u32[]{:S(2)}, u32[]{:S(2)}) %all-to-all-start.6) | async-done | bytes 786464 | tf_op jit(solution)/shard_map/all_to_all | solution.py:385
  (687 shorter events, 288.2 us)
Async XLA Ops:
  9.2 23.1 %all-to-all-start = ((bf16[8,24,1536]{2,1,0:T(8,128)(2,1)}), bf16[8,24,1536]{2,1,0:T(8,128)(2,1)S(1)}, u32[]{:S(2)}, u32[]{:S(2)}) async-start(bf16[8,24,1536]{2,1,0:T(8,128)(2,1)} %broadcast_in_dim.105), calls=%async_computation | async-start | bytes 1179648 | tf_op jit(solution)/shard_map/all_to_all | solution.py:373
  16.4 102.4 %all-gather.4.cloned.1.call-start = ((), (), s32[]{:S(2)}) async-start(), calls=%async_computation.10 | async-start | bytes 4866048 | tf_op jit(solution)/shard_map/all_gather | solution.py:544
  21.6 15.8 %collective-permute-start = (bf16[1,1,1,24,384]{4,3,2,1,0:T(8,128)(2,1)S(1)}, bf16[1,1,1,24,384]{4,3,2,1,0:T(8,128)(2,1)S(1)}, u32[]{:S(2)}, u32[]{:S(2)}) collective-permute-start(bf16[1,1,1,24,384]{4,3,2,1,0:T(8,128)(2,1)S(1)} %fusion.123), channel_id=1, source_target_pairs={{0,2},{1,3},{2,0},{3,1},{4,6},{5,7},{6,4},{7,5},{8,10},{9,11},{10,... | collective-permute-start | bytes 55304 | tf_op jit(solution)/shard_map/ppermute | solution.py:352
  23.1 21.7 %collective-permute-start.2 = (bf16[4,8,768]{2,1,0:T(8,128)(2,1)S(1)}, bf16[4,8,768]{2,1,0:T(8,128)(2,1)S(1)}, u32[]{:S(2)}, u32[]{:S(2)}) collective-permute-start(bf16[4,8,768]{2,1,0:T(8,128)(2,1)S(1)} %slice.313), channel_id=1, source_target_pairs={{0,1},{1,2},{2,3},{4,5},{5,6},{6,7},{8,9},{9,10},{10,11},{12,13},{... | collective-permute-start | bytes 147464 | tf_op jit(solution)/shard_map/ppermute | solution.py:357
  39.6 22.0 %all-to-all-start.1 = ((bf16[8,96,384]{2,1,0:T(8,128)(2,1)}), bf16[8,96,384]{2,1,0:T(8,128)(2,1)S(1)}, u32[]{:S(2)}, u32[]{:S(2)}) async-start(bf16[8,96,384]{2,1,0:T(8,128)(2,1)} %broadcast_in_dim.106), calls=%async_computation.1 | async-start | bytes 1179648 | tf_op jit(solution)/shard_map/all_to_all | solution.py:373
  43.2 178.7 %all-gather.6.cloned.1.call-start = ((), (), s32[]{:S(2)}) async-start(), calls=%async_computation.13 | async-start | bytes 11796480 | tf_op jit(solution)/shard_map/all_gather | solution.py:549
  43.3 15.4 %collective-permute-start.3 = (bf16[8,1,1,24,1536]{4,3,2,1,0:T(8,128)(2,1)S(1)}, bf16[8,1,1,24,1536]{4,3,2,1,0:T(8,128)(2,1)S(1)}, u32[]{:S(2)}, u32[]{:S(2)}) collective-permute-start(bf16[8,1,1,24,1536]{4,3,2,1,0:T(8,128)(2,1)S(1)} %bitcast.270), channel_id=1, source_target_pairs={{0,2},{1,3},{2,0},{3,1},{4,6},{5,7},{6,4},{7,5},{8,10},{9,11},{10,... | collective-permute-start | bytes 1769480 | tf_op jit(solution)/shard_map/ppermute | solution.py:352
  78.2 14.7 %collective-permute-start.6 = (f32[2,1536]{1,0:T(2,128)S(1)}, f32[2,1536]{1,0:T(2,128)S(1)}, u32[]{:S(2)}, u32[]{:S(2)}) collective-permute-start(f32[2,1536]{1,0:T(2,128)S(1)} %get-tuple-element.288), channel_id=1, source_target_pairs={{0,1},{1,0},{2,3},{3,2},{4,5},{5,4},{6,7},{7,6},{8,9},{9,8},{10,11... | collective-permute-start | bytes 36872 | tf_op jit(solution)/shard_map/ppermute | solution.py:352
  134.3 50.4 %all-to-all-start.2 = ((bf16[8,2,40,1536]{3,2,1,0:T(8,128)(2,1)}), bf16[8,2,40,1536]{3,2,1,0:T(8,128)(2,1)}, u32[]{:S(2)}, u32[]{:S(2)}) async-start(bf16[8,2,40,1536]{3,2,1,0:T(8,128)(2,1)} %bitcast.256), calls=%async_computation.2 | async-start | bytes 3932160 | tf_op jit(solution)/shard_map/all_to_all | solution.py:648
  150.5 18.0 %collective-permute-start.9 = (f32[2,1536]{1,0:T(2,128)S(1)}, f32[2,1536]{1,0:T(2,128)S(1)}, u32[]{:S(2)}, u32[]{:S(2)}) collective-permute-start(f32[2,1536]{1,0:T(2,128)S(1)} %get-tuple-element.298), channel_id=1, source_target_pairs={{0,1},{1,0},{2,3},{3,2},{4,5},{5,4},{6,7},{7,6},{8,9},{9,8},{10,11... | collective-permute-start | bytes 36872 | tf_op jit(solution)/shard_map/ppermute | solution.py:352
  217.3 49.5 %all-to-all-start.4 = ((bf16[8,2,40,1536]{3,2,1,0:T(8,128)(2,1)}), bf16[8,2,40,1536]{3,2,1,0:T(8,128)(2,1)}, u32[]{:S(2)}, u32[]{:S(2)}) async-start(bf16[8,2,40,1536]{3,2,1,0:T(8,128)(2,1)} %bitcast.257), calls=%async_computation.4 | async-start | bytes 3932160 | tf_op jit(solution)/shard_map/all_to_all | solution.py:648
  266.8 51.0 %all-to-all-start.3 = ((bf16[8,2,40,1536]{3,2,1,0:T(8,128)(2,1)}), bf16[8,2,40,1536]{3,2,1,0:T(8,128)(2,1)}, u32[]{:S(2)}, u32[]{:S(2)}) async-start(bf16[8,2,40,1536]{3,2,1,0:T(8,128)(2,1)} %bitcast.234), calls=%async_computation.3 | async-start | bytes 3932160 | tf_op jit(solution)/shard_map/all_to_all | solution.py:659
  271.2 327.9 %reduce-scatter.6.cloned.1.call-start = ((), (), s32[]{:S(2)}) async-start(), calls=%async_computation.11 | async-start | bytes 5898240 | tf_op jit(solution)/shard_map/reduce_scatter | solution.py:758
  338.1 50.4 %all-to-all-start.5 = ((bf16[8,2,40,1536]{3,2,1,0:T(8,128)(2,1)}), bf16[8,2,40,1536]{3,2,1,0:T(8,128)(2,1)}, u32[]{:S(2)}, u32[]{:S(2)}) async-start(bf16[8,2,40,1536]{3,2,1,0:T(8,128)(2,1)} %bitcast.233), calls=%async_computation.5 | async-start | bytes 3932160 | tf_op jit(solution)/shard_map/all_to_all | solution.py:659
  344.0 255.0 %reduce-scatter.8.cloned.1.call-start = ((), (), s32[]{:S(2)}) async-start(), calls=%async_computation.12 | async-start | bytes 5898240 | tf_op jit(solution)/shard_map/reduce_scatter | solution.py:757
  344.6 261.0 %reduce-scatter.10.cloned.1.call-start = ((), (), s32[]{:S(2)}) async-start(), calls=%async_computation.14 | async-start | bytes 5068800
  373.0 77.1 %collective-permute-start.11 = (bf16[2,16,1536]{2,1,0:T(8,128)(2,1)}, bf16[2,16,1536]{2,1,0:T(8,128)(2,1)}, u32[]{:S(2)}, u32[]{:S(2)}) collective-permute-start(bf16[2,16,1536]{2,1,0:T(8,128)(2,1)} %convert_element_type.381), channel_id=1, source_target_pairs={{0,1},{1,0},{2,3},{3,2},{4,5},{5,4},{6,7},{7,6},{8,9},{9,8},{10,11... | collective-permute-start | bytes 294920 | tf_op jit(solution)/shard_map/ppermute | solution.py:352
  433.1 17.0 %collective-permute-start.14 = (bf16[2,16,1536]{2,1,0:T(8,128)(2,1)}, bf16[2,16,1536]{2,1,0:T(8,128)(2,1)}, u32[]{:S(2)}, u32[]{:S(2)}) collective-permute-start(bf16[2,16,1536]{2,1,0:T(8,128)(2,1)} %convert_element_type.391), channel_id=1, source_target_pairs={{0,1},{1,0},{2,3},{3,2},{4,5},{5,4},{6,7},{7,6},{8,9},{9,8},{10,11... | collective-permute-start | bytes 294920 | tf_op jit(solution)/shard_map/ppermute | solution.py:352
  504.0 48.0 %collective-permute-start.13 = (f32[2,8,1536]{2,1,0:T(8,128)}, f32[2,8,1536]{2,1,0:T(8,128)}, u32[]{:S(2)}, u32[]{:S(2)}) collective-permute-start(f32[2,8,1536]{2,1,0:T(8,128)} %slice.443), channel_id=1, source_target_pairs={{1,0},{2,1},{3,2},{5,4},{6,5},{7,6},{9,8},{10,9},{11,10},{13,12},{... | collective-permute-start | bytes 294920 | tf_op jit(solution)/shard_map/ppermute | solution.py:357
  546.0 8.3 %collective-permute-start.16 = (f32[2,8,1536]{2,1,0:T(8,128)}, f32[2,8,1536]{2,1,0:T(8,128)}, u32[]{:S(2)}, u32[]{:S(2)}) collective-permute-start(f32[2,8,1536]{2,1,0:T(8,128)} %slice.450), channel_id=1, source_target_pairs={{1,0},{2,1},{3,2},{5,4},{6,5},{7,6},{9,8},{10,9},{11,10},{13,12},{... | collective-permute-start | bytes 294920 | tf_op jit(solution)/shard_map/ppermute | solution.py:357
  564.8 14.8 %collective-permute-start.17 = (bf16[8,2,1,24,1536]{4,3,2,1,0:T(8,128)(2,1)}, bf16[8,2,1,24,1536]{4,3,2,1,0:T(8,128)(2,1)}, u32[]{:S(2)}, u32[]{:S(2)}) collective-permute-start(bf16[8,2,1,24,1536]{4,3,2,1,0:T(8,128)(2,1)} %dynamic-slice_convert_fusion), channel_id=1, source_target_pairs={{0,1},{1,0},{2,3},{3,2},{4,5},{5,4},{6,7},{7,6},{8,9},{9,8},{10,11... | collective-permute-start | bytes 3538952 | tf_op jit(solution)/shard_map/ppermute | solution.py:352
  576.9 8.4 %collective-permute-start.20 = (bf16[8,1,1,24,512]{4,3,2,1,0:T(8,128)(2,1)S(1)}, bf16[8,1,1,24,512]{4,3,2,1,0:T(8,128)(2,1)S(1)}, u32[]{:S(2)}, u32[]{:S(2)}) collective-permute-start(bf16[8,1,1,24,512]{4,3,2,1,0:T(8,128)(2,1)S(1)} %dynamic-slice_convert_fusion.3), channel_id=1, source_target_pairs={{0,2},{1,3},{2,0},{3,1},{4,6},{5,7},{6,4},{7,5},{8,10},{9,11},{10,... | collective-permute-start | bytes 589832 | tf_op jit(solution)/shard_map/ppermute | solution.py:352
  581.3 16.6 %collective-permute-start.18 = (bf16[8,1,1,24,1536]{4,3,2,1,0:T(8,128)(2,1)S(1)}, bf16[8,1,1,24,1536]{4,3,2,1,0:T(8,128)(2,1)S(1)}, u32[]{:S(2)}, u32[]{:S(2)}) collective-permute-start(bf16[8,1,1,24,1536]{4,3,2,1,0:T(8,128)(2,1)S(1)} %dynamic-slice_convert_fusion.1), channel_id=1, source_target_pairs={{0,2},{1,3},{2,0},{3,1},{4,6},{5,7},{6,4},{7,5},{8,10},{9,11},{10,... | collective-permute-start | bytes 1769480 | tf_op jit(solution)/shard_map/ppermute | solution.py:352
  612.9 24.1 %all-to-all-start.6 = ((bf16[8,24,2048]{2,1,0:T(8,128)(2,1)}), bf16[8,24,2048]{2,1,0:T(8,128)(2,1)S(1)}, u32[]{:S(2)}, u32[]{:S(2)}) async-start(bf16[8,24,2048]{2,1,0:T(8,128)(2,1)} %pad_maximum_fusion.7), calls=%async_computation.8 | async-start | bytes 1572864 | tf_op jit(solution)/shard_map/all_to_all | solution.py:385
  (211 other events, 2048.3 us)
Sparse Core Ops, SparseCore 0:
  32.5 66.0 all-gather.3
  119.0 65.7 all-gather.5
  338.3 49.2 reduce-scatter.5
  390.1 47.8 reduce-scatter.7
  457.3 105.0 reduce-scatter.9
